TPU v7x, 32 devices: a whole 2x2x4 slice. The times are simulated.
32 devices in a mesh: groups: 2 (over y), dp: 16 (over z, x, core).
Axes of the slice: x: 2, y: 2, z: 4, core: 2. Of those that a mesh axis runs over, the one named last changes fastest.
Arguments:
- queries: bfloat16 [96, 128, 2560], P(('groups', 'dp')), parts along dimension 0, may hold values from -50 to 50
- keys: bfloat16 [96, 128, 2560], P(('groups', 'dp')), parts along dimension 0, may hold values from -4 to 4
- values: bfloat16 [96, 128, 2560], P(('groups', 'dp')), parts along dimension 0, may hold values from -6 to 6
- counts: int32 [32], P(('groups', 'dp')), parts along dimension 0, may hold values from 1 to 3, as said below
- neighbours: int32 [96, 3], P(('groups', 'dp')), parts along dimension 0, may hold values from 0 to 5, as said below
- gate_table: float32 [50, 2560], replicated, may hold values from 1 to 8
- step: int32 [1], replicated, may hold values from 0 to 49
- out_weight: bfloat16 [2560, 5120], P(None, 'dp'), may hold values from -0.125 to 0.125
Outputs:
- mixed: bfloat16 [96, 128, 5120], P(('groups', 'dp')), parts along dimension 0
There are 2 independent parts, one for each index of `groups`. A program takes and returns all parts, laid end to end along the dimension named above; an argument that names none is the same for every part. Nothing has to cross between parts.
Inputs may be any that keep to these rules, and one draw needn't show every extreme that they name: `counts`: the live slots of a device come first. Member m holds the devices (m*4 + 4//2 + r) modulo the number of devices, r = 0 to 3, its tile list running through them in that order. Some device holds 3 live tiles. `neighbours`: row t (a tile of device d) names 3 places of device d's extended list: places 0 to 0 are tiles s to s+1 - 1 of device d-1 (around the axis) with s = max(counts[d-1]-1, 0), place 1+j is the device's slot j, places 1 + 3 onward are the first tiles of device d+1 (around the axis), and 5 names no tile. In a live tile's row the first entry is the tile itself and the others name distinct live tiles of the same member or no tile; rows of slots past the device's count name no tile at all.
All inputs are finite; a program needn't handle non-finite values.
Results may differ from a plain program's by a relative error of at most 0.0052.
Values may be sent and summed in bfloat16 or wider, within the bound.
No kernel may reach another device: no remote copies, remote signals or barrier semaphores. Data moves between devices by JAX's collectives and lax.ppermute only.
A program may use at most 192 MiB of HBM per device.

v0:
```python
import functools
import math

import jax
import jax.numpy as jnp
from jax import lax
from jax.experimental import pallas as pl
from jax.experimental.pallas import tpu as pltpu
from jax.sharding import PartitionSpec as P

HEADS = 20
HALO = 1
MEMBER_DEVS = 4
CORES = 2
COLUMNS = 2

masked_score = -1e30
VMEM_LIMIT = 48 * 1024 * 1024


def attention_kernel(heads, index_ref, count_ref, q_ref, k_ref, v_ref, before_ref, after_ref, gate_ref, o_ref, ext_k, ext_v):
    slots, rows, width = q_ref.shape
    head_dim = width // heads
    places = slots + 2 * HALO
    picks = index_ref.shape[0] // slots
    ext_k[0:HALO] = before_ref[0]
    ext_v[0:HALO] = before_ref[1]
    ext_k[HALO : HALO + slots] = k_ref[...]
    ext_v[HALO : HALO + slots] = v_ref[...]
    ext_k[HALO + slots : places] = after_ref[0]
    ext_v[HALO + slots : places] = after_ref[1]
    for slot in range(slots):

        @pl.when(slot < count_ref[0])
        def _():
            place = [index_ref[slot * picks + j] for j in range(picks)]
            held = [jnp.minimum(p, places - 1) for p in place]
            for h in range(heads):
                at = pl.ds(h * head_dim, head_dim)
                query = q_ref[slot, :, at]
                scores = []
                for j in range(picks):
                    s = lax.dot_general(
                        query,
                        ext_k[held[j], :, at],
                        (((1,), (1,)), ((), ())),
                        preferred_element_type=jnp.float32,
                    ) * (1.0 / math.sqrt(head_dim))
                    scores.append(jnp.where(place[j] < places, s, masked_score))
                scores = jnp.concatenate(scores, axis=1)
                raw = jnp.exp(scores - jnp.max(scores, axis=1, keepdims=True))
                denominator = jnp.sum(raw, axis=1, keepdims=True)
                vals = jnp.concatenate([ext_v[held[j], :, at] for j in range(picks)], axis=0)
                summed = jnp.dot(raw.astype(jnp.bfloat16), vals, preferred_element_type=jnp.float32)
                o_ref[slot, :, at] = (summed / denominator * gate_ref[:, at]).astype(o_ref.dtype)

        @pl.when(slot >= count_ref[0])
        def _():
            o_ref[slot] = jnp.zeros((rows, width), o_ref.dtype)


def attend(queries, keys, values, before, after, neighbours, counts, gate_row):
    slots, rows, channels = queries.shape
    head_dim = channels // HEADS
    heads = 4 if HEADS % 4 == 0 else 1
    width = heads * head_dim
    places = slots + 2 * HALO
    whole = lambda lead: pl.BlockSpec((lead, rows, width), lambda g, *_: (0, 0, g))
    edge = pl.BlockSpec((2, HALO, rows, width), lambda g, *_: (0, 0, 0, g))
    pairs = slots * HEADS * rows * neighbours.shape[1] * rows
    return pl.pallas_call(
        functools.partial(attention_kernel, heads),
        out_shape=jax.ShapeDtypeStruct((slots, rows, channels), jnp.bfloat16),
        grid_spec=pltpu.PrefetchScalarGridSpec(
            num_scalar_prefetch=2,
            grid=(HEADS // heads,),
            in_specs=[whole(slots), whole(slots), whole(slots), edge, edge, pl.BlockSpec((1, width), lambda g, *_: (0, g))],
            out_specs=whole(slots),
            scratch_shapes=[pltpu.VMEM((places, rows, width), jnp.bfloat16)] * 2,
        ),
        compiler_params=pltpu.CompilerParams(vmem_limit_bytes=VMEM_LIMIT),
        cost_estimate=pl.CostEstimate(
            flops=4 * pairs * head_dim, bytes_accessed=2 * 6 * slots * rows * channels, transcendentals=pairs
        ),
        name="attention",
    )(neighbours.reshape(-1), counts, queries, keys, values, before, after, gate_row)


def project_kernel(pieces_of, has_old, scalars, *refs):
    blocks = len(pieces_of)
    n = sum(pieces_of)
    att_ref, pieces, out_ref = refs[0], refs[1 : 1 + n], refs[1 + n + has_old]
    wbuf, obuf, in_sem, out_sem = refs[2 + n + has_old :]
    shard_rows = wbuf.shape[1] // CORES
    core, group = scalars[0], scalars[1]
    copies = []
    at = 0
    for b in range(blocks):
        mine = []
        for i in range(pieces_of[b]):
            rows = pieces[at].shape[0]
            halves = pieces_of[b] // CORES
            owner = core if i < halves else 1 - core
            start = owner * shard_rows
            if halves == 2:
                half = group if i % 2 == 0 else 1 - group
                start = start + half * rows
            start = pl.multiple_of(start, rows)
            mine.append(pltpu.make_async_copy(pieces[at], wbuf.at[b, pl.ds(start, rows)], in_sem.at[b, i]))
            at += 1
        for c in mine:
            c.start()
        copies.append(mine)
    stores = []
    width = wbuf.shape[1]
    for b in range(blocks):
        for c in copies[b]:
            c.wait()
        if b >= 2:
            stores[b - 2].wait()
        done = 0
        while done < width:
            step = min(256, width - done)
            obuf[b % 2, :, done : done + step] = lax.dot_general(
                att_ref[...],
                wbuf[b, done : done + step],
                (((1,), (1,)), ((), ())),
                preferred_element_type=jnp.float32,
            ).astype(obuf.dtype)
            done += step
        where = pl.ds(pl.multiple_of(scalars[2 + b] * width, width), width)
        store = pltpu.make_async_copy(obuf.at[b % 2], out_ref.at[:, where], out_sem.at[b])
        store.start()
        stores.append(store)
    for store in stores[-2:]:
        store.wait()


def project(att, blocks, chips, core, group, columns, old=None):
    rows, channels = att.shape
    pieces = [p for b in blocks for p in b]
    width = sum(p.shape[0] for p in blocks[0])
    has_old = int(old is not None)
    scalars = jnp.stack([core, group] + list(chips)).astype(jnp.int32)
    anywhere = pl.BlockSpec(memory_space=pl.ANY)
    return pl.pallas_call(
        functools.partial(project_kernel, tuple(len(b) for b in blocks), has_old),
        out_shape=jax.ShapeDtypeStruct((rows, columns), jnp.bfloat16),
        grid_spec=pltpu.PrefetchScalarGridSpec(
            num_scalar_prefetch=1,
            grid=(1,),
            in_specs=[pl.BlockSpec((rows, channels), lambda i, *_: (0, 0))] + [anywhere] * (len(pieces) + has_old),
            out_specs=anywhere,
            scratch_shapes=[
                pltpu.VMEM((len(blocks), width, channels), jnp.bfloat16),
                pltpu.VMEM((2, rows, width), jnp.bfloat16),
                pltpu.SemaphoreType.DMA((len(blocks), 4)),
                pltpu.SemaphoreType.DMA((len(blocks),)),
            ],
        ),
        input_output_aliases={2 + len(pieces): 0} if has_old else {},
        compiler_params=pltpu.CompilerParams(vmem_limit_bytes=VMEM_LIMIT),
        cost_estimate=pl.CostEstimate(
            flops=2 * rows * channels * width * len(blocks),
            bytes_accessed=2 * (channels * width + rows * width) * len(blocks) + 2 * rows * channels,
            transcendentals=0,
        ),
        name="project",
    )(scalars, att, *pieces, *([old] if has_old else []))


def on_device(groups, devices, queries, keys, values, counts, neighbours, gate_table, step, out_weight):
    slots, rows, channels = queries.shape
    shard = out_weight.shape[1]
    columns = shard * devices
    chips = devices // CORES
    length = chips // COLUMNS

    def permute(array, target):
        pairs = []
        for g in range(groups):
            for d in range(devices):
                to = target(g, d // (CORES * COLUMNS), d // CORES % COLUMNS, d % CORES)
                if to is not None:
                    tg, tz, tx, tc = to
                    pairs.append((g * devices + d, tg * devices + (tz * COLUMNS + tx) * CORES + tc))
        return lax.ppermute(array, ("groups", "dp"), pairs)

    def within_member(array, by):
        pairs = []
        for d in range(devices):
            first, second = (d, (d + by) % devices) if by > 0 else ((d + by) % devices, d)
            if (first - MEMBER_DEVS // 2) % MEMBER_DEVS != MEMBER_DEVS - 1:
                pairs.append((d, (d + by) % devices))
        return lax.ppermute(array, "dp", pairs)

    tail_start = jnp.maximum(counts[0] - HALO, 0)
    tail = jnp.stack([lax.dynamic_slice_in_dim(a, tail_start, HALO, 0) for a in (keys, values)])
    lead = jnp.stack([keys[:HALO], values[:HALO]])
    gate_row = lax.dynamic_slice_in_dim(gate_table, step[0], 1, 0)
    weight = out_weight.T

    if not (groups == 2 and devices % (CORES * COLUMNS) == 0 and length >= 3 and shard % 32 == 0 and (CORES * shard) % 128 == 0):
        before, after = within_member(tail, 1), within_member(lead, -1)
        att = attend(queries, keys, values, before, after, neighbours, counts, gate_row)
        full = lax.all_gather(weight, "dp", axis=0, tiled=True)
        mixed = lax.dot_general(
            att.reshape(slots * rows, channels), full, (((1,), (1,)), ((), ())), preferred_element_type=jnp.float32
        )
        return mixed.astype(jnp.bfloat16).reshape(slots, rows, columns)

    over = {
        "z": lambda g, z, x, c: (g, (z + 1) % length, x, c),
        "x": lambda g, z, x, c: (g, z, (x + 1) % COLUMNS, c),
        "y": lambda g, z, x, c: (1 - g, z, x, c),
        "s": lambda g, z, x, c: (g, z, x, 1 - c),
    }
    group = lax.axis_index("groups")
    device = lax.axis_index("dp")
    core = device % CORES
    my_x, my_z = device // CORES % COLUMNS, device // (CORES * COLUMNS)

    half = shard // 2
    have = {
        ("z", "p", 0): lax.dynamic_slice_in_dim(weight, group * half, half, 0),
        ("z", "q", 0): lax.dynamic_slice_in_dim(weight, (1 - group) * half, half, 0),
        "weight": weight,
    }
    sends = {
        "z": [(("z", "p", s), ("z", "p", s + 1)) for s in range(length - 1)]
        + [(("z", "q", s), ("z", "q", s + 1)) for s in range(1, length - 1)],
        "x": [(("z", "p", s), ("x", "p", s)) for s in range(length)] + [(("z", "q", 0), ("x", "q", 0))],
        "y": [None, (("z", "p", 1), ("z", "q", 1))] + [(("x", "p", s), ("x", "q", s)) for s in range(1, length)],
    }
    rounds = max(len(v) for v in sends.values())
    blocks = [("z", s) for s in range(length)] + [("x", s) for s in range(length)]
    todo = list(blocks)

    def ready():
        full = []
        for b in todo:
            if b == ("z", 0):
                ok = "s_weight" in have
            else:
                ok = all(("s", (b[0], h, b[1])) in have for h in "pq")
            if ok:
                full.append(b)
        return full

    def run_project(which, att, old):
        pieces, chip_of = [], []
        for b in which:
            col, s = b
            todo.remove(b)
            if b == ("z", 0):
                pieces.append([have["weight"], have["s_weight"]])
            else:
                mine = [(col, h, s) for h in "pq"]
                pieces.append([have[m] for m in mine] + [have[("s", m)] for m in mine])
            x = my_x if col == "z" else (my_x + 1) % COLUMNS
            chip_of.append((my_z - s) % length * COLUMNS + x)
        return project(att, pieces, chip_of, core, group, columns, old)

    att = out = None
    arrived = []
    swap = []
    for r in range(rounds + 1):
        names = list(arrived)
        keep = [have[n] for n in names]
        items = [(link, *sends[link][r]) for link in ("z", "x", "y") if r < len(sends[link]) and sends[link][r]]
        sources = [have[src] for _, src, _ in items]
        bar = lax.optimization_barrier((keep, sources, [a for a in (att, out) if a is not None], [have[n] for n in swap]))
        for n, a in zip(names, bar[0]):
            have[n] = a
        if att is not None:
            att = bar[2][0]
        if out is not None:
            out = bar[2][1]
        work = ready() if att is not None else []
        arrived = []
        for (link, _, dst), a in zip(items, bar[1]):
            have[dst] = permute(a, over[link])
            arrived.append(dst)
        if r == 0:
            have["before"], have["after"] = within_member(tail, 1), within_member(lead, -1)
        for n, a in zip(swap, bar[3]):
            to = "s_weight" if n == "weight" else ("s", n)
            have[to] = permute(a, over["s"])
            arrived.append(to)
        swap = [d for d in arrived if isinstance(d, tuple) and d[0] != "s"]
        if r == 0:
            swap.append("weight")
        if r == 1:
            arrived += ["before", "after"]
        if r == 2:
            att = attend(queries, keys, values, have["before"], have["after"], neighbours, counts, gate_row)
            att = att.reshape(slots * rows, channels)
        elif work:
            out = run_project(work, att, out)
    out = run_project(list(todo), att, out)
    return out.reshape(slots, rows, columns)


def solution(mesh):
    both = P(("groups", "dp"), None, None)
    placed = (both, both, both, P(("groups", "dp")), P(("groups", "dp"), None), P(), P(), P(None, "dp"))
    return jax.shard_map(
        functools.partial(on_device, mesh.shape["groups"], mesh.shape["dp"]),
        mesh=mesh,
        in_specs=placed,
        out_specs=both,
        check_vma=False,
    )
```

profile of v0, /device:TPU:0, one launch (start us, length us, event | category | flops | bytes accessed | tf_op | source)
XLA Modules:
  0.0 194.8 jit_solution(1494502426151389012)
XLA Ops:
  0.0 2.6 %dynamic-slice_bitcast_fusion = (bf16[160,2560]{1,0:T(8,128)(2,1)}, bf16[160,2560]{1,0:T(8,128)(2,1)S(1)}) fusion(bf16[2560,320]{0,1:T(8,128)(2,1)} %param.15, s32[]{:T(128)S(6)} %select_n.72, s32[]{:T(128)S(6)} %select_n.70), kind=kLoop, calls=%fused_computation.2 | loop fusion | bytes 3276808 | tf_op jit(solution)/shard_map/dynamic_slice | solution.py:226
  2.6 3.0 %collective-permute-start = (bf16[160,2560]{1,0:T(8,128)(2,1)S(1)}, bf16[160,2560]{1,0:T(8,128)(2,1)S(1)}, u32[]{:S(2)}, u32[]{:S(2)}) collective-permute-start(bf16[160,2560]{1,0:T(8,128)(2,1)S(1)} %get-tuple-element.68), channel_id=1, source_target_pairs={{0,4},{1,5},{2,6},{3,7},{4,8},{5,9},{6,10},{7,11},{8,12},{9,13},{1... | collective-permute-start | bytes 2457608 | tf_op jit(solution)/shard_map/ppermute | solution.py:187
  5.6 1.5 collective-permute-start.1
  7.7 1.6 slice_bitcast_fusion
  9.5 2.1 %collective-permute-start.8 = (bf16[2,1,128,2560]{3,2,1,0:T(8,128)(2,1)S(1)}, bf16[2,1,128,2560]{3,2,1,0:T(8,128)(2,1)S(1)}, u32[]{:S(2)}, u32[]{:S(2)}) collective-permute-start(bf16[2,1,128,2560]{3,2,1,0:T(8,128)(2,1)S(1)} %pad_maximum_fusion), channel_id=1, source_target_pairs={{0,1},{2,3},{3,4},{4,5},{6,7},{7,8},{8,9},{10,11},{11,12},{12,13},... | collective-permute-start | bytes 3932168 | tf_op jit(solution)/shard_map/ppermute | solution.py:195
  11.6 6.3 %collective-permute-start.9 = (bf16[2,1,128,2560]{3,2,1,0:T(8,128)(2,1)S(1)}, bf16[2,1,128,2560]{3,2,1,0:T(8,128)(2,1)S(1)}, u32[]{:S(2)}, u32[]{:S(2)}) collective-permute-start(bf16[2,1,128,2560]{3,2,1,0:T(8,128)(2,1)S(1)} %pad_maximum_fusion.1), channel_id=1, source_target_pairs={{0,15},{1,0},{3,2},{4,3},{5,4},{7,6},{8,7},{9,8},{11,10},{12,11},{... | collective-permute-start | bytes 3932168 | tf_op jit(solution)/shard_map/ppermute | solution.py:195
  18.0 8.0 %collective-permute-done.refs_3_ = bf16[160,2560]{1,0:T(8,128)(2,1)S(1)} collective-permute-done((bf16[160,2560]{1,0:T(8,128)(2,1)S(1)}, bf16[160,2560]{1,0:T(8,128)(2,1)S(1)}, u32[]{:S(2)}, u32[]{:S(2)}) %collective-permute-start) | collective-permute-done | bytes 819232 | tf_op jit(solution)/shard_map/ppermute | solution.py:187
  26.0 15.0 %collective-permute-start.2 = (bf16[160,2560]{1,0:T(8,128)(2,1)S(1)}, bf16[160,2560]{1,0:T(8,128)(2,1)}, u32[]{:S(2)}, u32[]{:S(2)}) collective-permute-start(bf16[160,2560]{1,0:T(8,128)(2,1)S(1)} %collective-permute-done.refs_3_), channel_id=1, source_target_pairs={{0,4},{1,5},{2,6},{3,7},{4,8},{5,9},{6,10},{7,11},{8,12},{9,13},{1... | collective-permute-start | bytes 2457608 | tf_op jit(solution)/shard_map/ppermute | solution.py:187
  40.9 7.4 %collective-permute-done.8.before_ref = bf16[2,1,128,2560]{3,2,1,0:T(8,128)(2,1)S(1)} collective-permute-done((bf16[2,1,128,2560]{3,2,1,0:T(8,128)(2,1)S(1)}, bf16[2,1,128,2560]{3,2,1,0:T(8,128)(2,1)S(1)}, u32[]{:S(2)}, u32[]{:S(2)}) %collective-permute-start.8) | collective-permute-done | bytes 1310752 | tf_op jit(solution)/shard_map/ppermute | solution.py:195
  48.4 1.5 collective-permute-start.4
  50.8 6.9 %collective-permute-done.2.refs_1_ = bf16[160,2560]{1,0:T(8,128)(2,1)} collective-permute-done((bf16[160,2560]{1,0:T(8,128)(2,1)S(1)}, bf16[160,2560]{1,0:T(8,128)(2,1)}, u32[]{:S(2)}, u32[]{:S(2)}) %collective-permute-start.2) | collective-permute-done | bytes 819232 | tf_op jit(solution)/shard_map/ppermute | solution.py:187
  58.5 5.3 %collective-permute-done.3.refs_1_ = bf16[160,2560]{1,0:T(8,128)(2,1)} collective-permute-done((bf16[160,2560]{1,0:T(8,128)(2,1)S(1)}, bf16[160,2560]{1,0:T(8,128)(2,1)}, u32[]{:S(2)}, u32[]{:S(2)}) %collective-permute-start.3) | collective-permute-done | bytes 819232 | tf_op jit(solution)/shard_map/ppermute | solution.py:187
  65.7 1.2 copy-done.14
  67.2 2.6 %collective-permute-start.11 = (bf16[160,2560]{1,0:T(8,128)(2,1)}, bf16[160,2560]{1,0:T(8,128)(2,1)}, u32[]{:S(2)}, u32[]{:S(2)}) collective-permute-start(bf16[160,2560]{1,0:T(8,128)(2,1)} %collective-permute-done.2.refs_1_), channel_id=1, source_target_pairs={{0,2},{1,3},{2,0},{3,1},{4,6},{5,7},{6,4},{7,5},{8,10},{9,11},{10,... | collective-permute-start | bytes 2457608 | tf_op jit(solution)/shard_map/ppermute | solution.py:187
  69.8 1.6 collective-permute-start.12
  71.9 17.1 %collective-permute-done.10.refs_1_ = bf16[160,2560]{1,0:T(8,128)(2,1)} collective-permute-done((bf16[160,2560]{1,0:T(8,128)(2,1)}, bf16[160,2560]{1,0:T(8,128)(2,1)}, u32[]{:S(2)}, u32[]{:S(2)}) %collective-permute-start.10) | collective-permute-done | bytes 819232 | tf_op jit(solution)/shard_map/ppermute | solution.py:187
  89.8 9.3 %attention.1 = bf16[3,128,2560]{2,1,0:T(8,128)(2,1)S(1)} custom-call(s32[9]{0:T(128)S(1)} %reshape.13.index_ref, s32[1]{0:T(128)S(6)} %copy.15.count_ref, bf16[3,128,2560]{2,1,0:T(8,128)(2,1)} %q_ref.1, bf16[3,128,2560]{2,1,0:T(8,128)(2,1)} %k_ref.1, bf16[3,128,2560]{2,1,0:T(8,128)(2,1)} %v_ref.1, ...), custom_call_target="tpu_custom_call" | custom-call | flops 1509949440 | bytes 11796480 | tf_op jit(solution)/shard_map/attention/pallas_call | solution.py:71
  99.1 1.3 copy-done.1
  100.5 5.1 %collective-permute-start.16 = (bf16[160,2560]{1,0:T(8,128)(2,1)}, bf16[160,2560]{1,0:T(8,128)(2,1)}, u32[]{:S(2)}, u32[]{:S(2)}) collective-permute-start(bf16[160,2560]{1,0:T(8,128)(2,1)} %collective-permute-done.4.refs_4_), channel_id=1, source_target_pairs={{0,4},{1,5},{2,6},{3,7},{4,8},{5,9},{6,10},{7,11},{8,12},{9,13},{1... | collective-permute-start | bytes 2457608 | tf_op jit(solution)/shard_map/ppermute | solution.py:187
  105.5 9.7 %collective-permute-start.17 = (bf16[160,2560]{1,0:T(8,128)(2,1)}, bf16[160,2560]{1,0:T(8,128)(2,1)}, u32[]{:S(2)}, u32[]{:S(2)}) collective-permute-start(bf16[160,2560]{1,0:T(8,128)(2,1)} %collective-permute-done.10.refs_1_), channel_id=1, source_target_pairs={{0,2},{1,3},{2,0},{3,1},{4,6},{5,7},{6,4},{7,5},{8,10},{9,11},{10,... | collective-permute-start | bytes 2457608 | tf_op jit(solution)/shard_map/ppermute | solution.py:187
  116.7 5.1 %collective-permute-done.16.refs_2_ = bf16[160,2560]{1,0:T(8,128)(2,1)} collective-permute-done((bf16[160,2560]{1,0:T(8,128)(2,1)}, bf16[160,2560]{1,0:T(8,128)(2,1)}, u32[]{:S(2)}, u32[]{:S(2)}) %collective-permute-start.16) | collective-permute-done | bytes 819232 | tf_op jit(solution)/shard_map/ppermute | solution.py:187
  121.8 2.8 %collective-permute-start.21 = (bf16[160,2560]{1,0:T(8,128)(2,1)}, bf16[160,2560]{1,0:T(8,128)(2,1)S(1)}, u32[]{:S(2)}, u32[]{:S(2)}) collective-permute-start(bf16[160,2560]{1,0:T(8,128)(2,1)} %collective-permute-done.12.refs_2_), channel_id=1, source_target_pairs={{0,1},{1,0},{2,3},{3,2},{4,5},{5,4},{6,7},{7,6},{8,9},{9,8},{10,11... | collective-permute-start | bytes 2457608 | tf_op jit(solution)/shard_map/ppermute | solution.py:187
  124.7 1.4 copy-done.4
  128.4 9.1 %project.4.refs_5_ = bf16[384,5120]{1,0:T(8,128)(2,1)} custom-call(s32[4]{0:T(128)S(1)} %pad_add_fusion.scalars, bf16[384,2560]{1,0:T(8,128)(2,1)} %bitcast.30, bf16[320,2560]{1,0:T(8,128)(2,1)S(1)} %bitcast.35, bf16[320,2560]{1,0:T(8,128)(2,1)} %copy-done.14, bf16[160,2560]{1,0:T(8,128)(2,1)S(1)} %copy-done.6, ...), custom_call_target="tpu_custom_call" | custom-call | flops 2516582400 | bytes 9502720 | tf_op jit(solution)/shard_map/project/pallas_call | solution.py:146
  137.5 2.7 %collective-permute-start.22 = (bf16[160,2560]{1,0:T(8,128)(2,1)}, bf16[160,2560]{1,0:T(8,128)(2,1)}, u32[]{:S(2)}, u32[]{:S(2)}) collective-permute-start(bf16[160,2560]{1,0:T(8,128)(2,1)} %collective-permute-done.16.refs_2_), channel_id=1, source_target_pairs={{0,4},{1,5},{2,6},{3,7},{4,8},{5,9},{6,10},{7,11},{8,12},{9,13},{1... | collective-permute-start | bytes 2457608 | tf_op jit(solution)/shard_map/ppermute | solution.py:187
  140.3 11.0 %collective-permute-start.23 = (bf16[160,2560]{1,0:T(8,128)(2,1)}, bf16[160,2560]{1,0:T(8,128)(2,1)}, u32[]{:S(2)}, u32[]{:S(2)}) collective-permute-start(bf16[160,2560]{1,0:T(8,128)(2,1)} %get-tuple-element.96), channel_id=1, source_target_pairs={{0,2},{1,3},{2,0},{3,1},{4,6},{5,7},{6,4},{7,5},{8,10},{9,11},{10,... | collective-permute-start | bytes 2457608 | tf_op jit(solution)/shard_map/ppermute | solution.py:187
  151.7 8.3 %collective-permute-done.22.refs_2_ = bf16[160,2560]{1,0:T(8,128)(2,1)} collective-permute-done((bf16[160,2560]{1,0:T(8,128)(2,1)}, bf16[160,2560]{1,0:T(8,128)(2,1)}, u32[]{:S(2)}, u32[]{:S(2)}) %collective-permute-start.22) | collective-permute-done | bytes 819232 | tf_op jit(solution)/shard_map/ppermute | solution.py:187
  160.1 4.7 %project.5.refs_9_ = bf16[384,5120]{1,0:T(8,128)(2,1)} custom-call(s32[3]{0:T(128)S(1)} %pad_add_fusion.2.scalars, bf16[384,2560]{1,0:T(8,128)(2,1)S(1)} %bitcast.33, bf16[160,2560]{1,0:T(8,128)(2,1)} %collective-permute-done.3.refs_1_, bf16[160,2560]{1,0:T(8,128)(2,1)} %collective-permute-done.12.refs_2_, ...), custom_call_target="tpu_custom_call", output_to_operand_aliasing={{}: (6, {})} | custom-call | flops 1258291200 | bytes 5734400 | tf_op jit(solution)/shard_map/project/pallas_call | solution.py:146
  164.8 5.6 %collective-permute-done.23.refs_6_ = bf16[160,2560]{1,0:T(8,128)(2,1)} collective-permute-done((bf16[160,2560]{1,0:T(8,128)(2,1)}, bf16[160,2560]{1,0:T(8,128)(2,1)}, u32[]{:S(2)}, u32[]{:S(2)}) %collective-permute-start.23) | collective-permute-done | bytes 819232 | tf_op jit(solution)/shard_map/ppermute | solution.py:187
  170.4 1.5 collective-permute-done.24.refs_10_
  172.7 9.3 %project.6.refs_13_ = bf16[384,5120]{1,0:T(8,128)(2,1)} custom-call(s32[4]{0:T(128)S(1)} %pad_add_fusion.3.scalars, bf16[384,2560]{1,0:T(8,128)(2,1)} %bitcast.31, bf16[160,2560]{1,0:T(8,128)(2,1)} %collective-permute-done.2.refs_1_, bf16[160,2560]{1,0:T(8,128)(2,1)} %collective-permute-done.16.refs_2_, ...), custom_call_target="tpu_custom_call", output_to_operand_aliasing={{}: (10, {})} | custom-call | flops 2516582400 | bytes 9502720 | tf_op jit(solution)/shard_map/project/pallas_call | solution.py:146
  183.8 10.8 %project.7 = bf16[384,5120]{1,0:T(8,128)(2,1)} custom-call(s32[5]{0:T(128)S(1)} %stack.71.scalars, bf16[384,2560]{1,0:T(8,128)(2,1)} %bitcast.32, bf16[160,2560]{1,0:T(8,128)(2,1)} %collective-permute-done.10.refs_1_, bf16[160,2560]{1,0:T(8,128)(2,1)} %collective-permute-done.22.refs_2_, ...), custom_call_target="tpu_custom_call", output_to_operand_aliasing={{}: (14, {})} | custom-call | flops 3774873600 | bytes 13271040 | tf_op jit(solution)/shard_map/project/pallas_call | solution.py:146
  (81 shorter events, 11.8 us)
Async XLA Ops:
  0.0 89.8 %copy-start = (f32[50,2560]{1,0:T(8,128)S(1)}, f32[50,2560]{1,0:T(8,128)}, u32[]{:S(2)}) copy-start(f32[50,2560]{1,0:T(8,128)} %param.13) | copy-start | bytes 1536004
  2.6 23.4 %collective-permute-start = (bf16[160,2560]{1,0:T(8,128)(2,1)S(1)}, bf16[160,2560]{1,0:T(8,128)(2,1)S(1)}, u32[]{:S(2)}, u32[]{:S(2)}) collective-permute-start(bf16[160,2560]{1,0:T(8,128)(2,1)S(1)} %get-tuple-element.68), channel_id=1, source_target_pairs={{0,4},{1,5},{2,6},{3,7},{4,8},{5,9},{6,10},{7,11},{8,12},{9,13},{1... | collective-permute-start | bytes 2457608 | tf_op jit(solution)/shard_map/ppermute | solution.py:187
  5.6 20.4 %collective-permute-start.1 = (bf16[160,2560]{1,0:T(8,128)(2,1)S(1)}, bf16[160,2560]{1,0:T(8,128)(2,1)S(1)}, u32[]{:S(2)}, u32[]{:S(2)}) collective-permute-start(bf16[160,2560]{1,0:T(8,128)(2,1)S(1)} %get-tuple-element.68), channel_id=1, source_target_pairs={{0,2},{1,3},{2,0},{3,1},{4,6},{5,7},{6,4},{7,5},{8,10},{9,11},{10,... | collective-permute-start | bytes 2457608 | tf_op jit(solution)/shard_map/ppermute | solution.py:187
  9.5 38.9 %collective-permute-start.8 = (bf16[2,1,128,2560]{3,2,1,0:T(8,128)(2,1)S(1)}, bf16[2,1,128,2560]{3,2,1,0:T(8,128)(2,1)S(1)}, u32[]{:S(2)}, u32[]{:S(2)}) collective-permute-start(bf16[2,1,128,2560]{3,2,1,0:T(8,128)(2,1)S(1)} %pad_maximum_fusion), channel_id=1, source_target_pairs={{0,1},{2,3},{3,4},{4,5},{6,7},{7,8},{8,9},{10,11},{11,12},{12,13},... | collective-permute-start | bytes 3932168 | tf_op jit(solution)/shard_map/ppermute | solution.py:195
  11.6 38.2 %collective-permute-start.9 = (bf16[2,1,128,2560]{3,2,1,0:T(8,128)(2,1)S(1)}, bf16[2,1,128,2560]{3,2,1,0:T(8,128)(2,1)S(1)}, u32[]{:S(2)}, u32[]{:S(2)}) collective-permute-start(bf16[2,1,128,2560]{3,2,1,0:T(8,128)(2,1)S(1)} %pad_maximum_fusion.1), channel_id=1, source_target_pairs={{0,15},{1,0},{3,2},{4,3},{5,4},{7,6},{8,7},{9,8},{11,10},{12,11},{... | collective-permute-start | bytes 3932168 | tf_op jit(solution)/shard_map/ppermute | solution.py:195
  26.0 31.7 %collective-permute-start.2 = (bf16[160,2560]{1,0:T(8,128)(2,1)S(1)}, bf16[160,2560]{1,0:T(8,128)(2,1)}, u32[]{:S(2)}, u32[]{:S(2)}) collective-permute-start(bf16[160,2560]{1,0:T(8,128)(2,1)S(1)} %collective-permute-done.refs_3_), channel_id=1, source_target_pairs={{0,4},{1,5},{2,6},{3,7},{4,8},{5,9},{6,10},{7,11},{8,12},{9,13},{1... | collective-permute-start | bytes 2457608 | tf_op jit(solution)/shard_map/ppermute | solution.py:187
  40.9 24.8 %collective-permute-start.7 = (bf16[320,2560]{1,0:T(8,128)(2,1)S(1)}, bf16[320,2560]{1,0:T(8,128)(2,1)S(1)}, u32[]{:S(2)}, u32[]{:S(2)}) collective-permute-start(bf16[320,2560]{1,0:T(8,128)(2,1)S(1)} %bitcast.34), channel_id=1, source_target_pairs={{0,1},{1,0},{2,3},{3,2},{4,5},{5,4},{6,7},{7,6},{8,9},{9,8},{10,11... | collective-permute-start | bytes 4915208 | tf_op jit(solution)/shard_map/ppermute | solution.py:187
  40.9 22.9 %collective-permute-start.3 = (bf16[160,2560]{1,0:T(8,128)(2,1)S(1)}, bf16[160,2560]{1,0:T(8,128)(2,1)}, u32[]{:S(2)}, u32[]{:S(2)}) collective-permute-start(bf16[160,2560]{1,0:T(8,128)(2,1)S(1)} %collective-permute-done.refs_3_), channel_id=1, source_target_pairs={{0,2},{1,3},{2,0},{3,1},{4,6},{5,7},{6,4},{7,5},{8,10},{9,11},{10,... | collective-permute-start | bytes 2457608 | tf_op jit(solution)/shard_map/ppermute | solution.py:187
  48.4 15.5 %collective-permute-start.4 = (bf16[160,2560]{1,0:T(8,128)(2,1)S(1)}, bf16[160,2560]{1,0:T(8,128)(2,1)}, u32[]{:S(2)}, u32[]{:S(2)}) collective-permute-start(bf16[160,2560]{1,0:T(8,128)(2,1)S(1)} %collective-permute-done.refs_3_), channel_id=1, source_target_pairs={{0,16},{1,17},{2,18},{3,19},{4,20},{5,21},{6,22},{7,23},{8,24},{9,... | collective-permute-start | bytes 2457608 | tf_op jit(solution)/shard_map/ppermute | solution.py:187
  49.9 14.0 %collective-permute-start.5 = (bf16[160,2560]{1,0:T(8,128)(2,1)S(1)}, bf16[160,2560]{1,0:T(8,128)(2,1)S(1)}, u32[]{:S(2)}, u32[]{:S(2)}) collective-permute-start(bf16[160,2560]{1,0:T(8,128)(2,1)S(1)} %collective-permute-done.refs_3_), channel_id=1, source_target_pairs={{0,1},{1,0},{2,3},{3,2},{4,5},{5,4},{6,7},{7,6},{8,9},{9,8},{10,11... | collective-permute-start | bytes 2457608 | tf_op jit(solution)/shard_map/ppermute | solution.py:187
  57.6 7.1 %collective-permute-start.6 = (bf16[160,2560]{1,0:T(8,128)(2,1)S(1)}, bf16[160,2560]{1,0:T(8,128)(2,1)S(1)}, u32[]{:S(2)}, u32[]{:S(2)}) collective-permute-start(bf16[160,2560]{1,0:T(8,128)(2,1)S(1)} %collective-permute-done.1.refs_5_), channel_id=1, source_target_pairs={{0,1},{1,0},{2,3},{3,2},{4,5},{5,4},{6,7},{7,6},{8,9},{9,8},{10,11... | collective-permute-start | bytes 2457608 | tf_op jit(solution)/shard_map/ppermute | solution.py:187
  66.9 22.1 %collective-permute-start.10 = (bf16[160,2560]{1,0:T(8,128)(2,1)}, bf16[160,2560]{1,0:T(8,128)(2,1)}, u32[]{:S(2)}, u32[]{:S(2)}) collective-permute-start(bf16[160,2560]{1,0:T(8,128)(2,1)} %collective-permute-done.2.refs_1_), channel_id=1, source_target_pairs={{0,4},{1,5},{2,6},{3,7},{4,8},{5,9},{6,10},{7,11},{8,12},{9,13},{1... | collective-permute-start | bytes 2457608 | tf_op jit(solution)/shard_map/ppermute | solution.py:187
  67.2 33.2 %collective-permute-start.11 = (bf16[160,2560]{1,0:T(8,128)(2,1)}, bf16[160,2560]{1,0:T(8,128)(2,1)}, u32[]{:S(2)}, u32[]{:S(2)}) collective-permute-start(bf16[160,2560]{1,0:T(8,128)(2,1)} %collective-permute-done.2.refs_1_), channel_id=1, source_target_pairs={{0,2},{1,3},{2,0},{3,1},{4,6},{5,7},{6,4},{7,5},{8,10},{9,11},{10,... | collective-permute-start | bytes 2457608 | tf_op jit(solution)/shard_map/ppermute | solution.py:187
  69.8 30.7 %collective-permute-start.12 = (bf16[160,2560]{1,0:T(8,128)(2,1)}, bf16[160,2560]{1,0:T(8,128)(2,1)}, u32[]{:S(2)}, u32[]{:S(2)}) collective-permute-start(bf16[160,2560]{1,0:T(8,128)(2,1)} %collective-permute-done.3.refs_1_), channel_id=1, source_target_pairs={{0,16},{1,17},{2,18},{3,19},{4,20},{5,21},{6,22},{7,23},{8,24},{9,... | collective-permute-start | bytes 2457608 | tf_op jit(solution)/shard_map/ppermute | solution.py:187
  71.4 29.0 %collective-permute-start.13 = (bf16[160,2560]{1,0:T(8,128)(2,1)}, bf16[160,2560]{1,0:T(8,128)(2,1)}, u32[]{:S(2)}, u32[]{:S(2)}) collective-permute-start(bf16[160,2560]{1,0:T(8,128)(2,1)} %collective-permute-done.2.refs_1_), channel_id=1, source_target_pairs={{0,1},{1,0},{2,3},{3,2},{4,5},{5,4},{6,7},{7,6},{8,9},{9,8},{10,11... | collective-permute-start | bytes 2457608 | tf_op jit(solution)/shard_map/ppermute | solution.py:187
  71.4 29.0 %collective-permute-start.14 = (bf16[160,2560]{1,0:T(8,128)(2,1)}, bf16[160,2560]{1,0:T(8,128)(2,1)}, u32[]{:S(2)}, u32[]{:S(2)}) collective-permute-start(bf16[160,2560]{1,0:T(8,128)(2,1)} %collective-permute-done.3.refs_1_), channel_id=1, source_target_pairs={{0,1},{1,0},{2,3},{3,2},{4,5},{5,4},{6,7},{7,6},{8,9},{9,8},{10,11... | collective-permute-start | bytes 2457608 | tf_op jit(solution)/shard_map/ppermute | solution.py:187
  89.0 11.4 %collective-permute-start.15 = (bf16[160,2560]{1,0:T(8,128)(2,1)}, bf16[160,2560]{1,0:T(8,128)(2,1)}, u32[]{:S(2)}, u32[]{:S(2)}) collective-permute-start(bf16[160,2560]{1,0:T(8,128)(2,1)} %collective-permute-done.4.refs_4_), channel_id=1, source_target_pairs={{0,1},{1,0},{2,3},{3,2},{4,5},{5,4},{6,7},{7,6},{8,9},{9,8},{10,11... | collective-permute-start | bytes 2457608 | tf_op jit(solution)/shard_map/ppermute | solution.py:187
  100.5 21.3 %collective-permute-start.16 = (bf16[160,2560]{1,0:T(8,128)(2,1)}, bf16[160,2560]{1,0:T(8,128)(2,1)}, u32[]{:S(2)}, u32[]{:S(2)}) collective-permute-start(bf16[160,2560]{1,0:T(8,128)(2,1)} %collective-permute-done.4.refs_4_), channel_id=1, source_target_pairs={{0,4},{1,5},{2,6},{3,7},{4,8},{5,9},{6,10},{7,11},{8,12},{9,13},{1... | collective-permute-start | bytes 2457608 | tf_op jit(solution)/shard_map/ppermute | solution.py:187
  105.5 32.0 %collective-permute-start.17 = (bf16[160,2560]{1,0:T(8,128)(2,1)}, bf16[160,2560]{1,0:T(8,128)(2,1)}, u32[]{:S(2)}, u32[]{:S(2)}) collective-permute-start(bf16[160,2560]{1,0:T(8,128)(2,1)} %collective-permute-done.10.refs_1_), channel_id=1, source_target_pairs={{0,2},{1,3},{2,0},{3,1},{4,6},{5,7},{6,4},{7,5},{8,10},{9,11},{10,... | collective-permute-start | bytes 2457608 | tf_op jit(solution)/shard_map/ppermute | solution.py:187
  115.3 22.2 %collective-permute-start.18 = (bf16[160,2560]{1,0:T(8,128)(2,1)}, bf16[160,2560]{1,0:T(8,128)(2,1)}, u32[]{:S(2)}, u32[]{:S(2)}) collective-permute-start(bf16[160,2560]{1,0:T(8,128)(2,1)} %collective-permute-done.11.refs_5_), channel_id=1, source_target_pairs={{0,16},{1,17},{2,18},{3,19},{4,20},{5,21},{6,22},{7,23},{8,24},{9,... | collective-permute-start | bytes 2457608 | tf_op jit(solution)/shard_map/ppermute | solution.py:187
  116.2 21.4 %collective-permute-start.19 = (bf16[160,2560]{1,0:T(8,128)(2,1)}, bf16[160,2560]{1,0:T(8,128)(2,1)}, u32[]{:S(2)}, u32[]{:S(2)}) collective-permute-start(bf16[160,2560]{1,0:T(8,128)(2,1)} %collective-permute-done.10.refs_1_), channel_id=1, source_target_pairs={{0,1},{1,0},{2,3},{3,2},{4,5},{5,4},{6,7},{7,6},{8,9},{9,8},{10,11... | collective-permute-start | bytes 2457608 | tf_op jit(solution)/shard_map/ppermute | solution.py:187
  116.2 21.4 %collective-permute-start.20 = (bf16[160,2560]{1,0:T(8,128)(2,1)}, bf16[160,2560]{1,0:T(8,128)(2,1)}, u32[]{:S(2)}, u32[]{:S(2)}) collective-permute-start(bf16[160,2560]{1,0:T(8,128)(2,1)} %collective-permute-done.11.refs_5_), channel_id=1, source_target_pairs={{0,1},{1,0},{2,3},{3,2},{4,5},{5,4},{6,7},{7,6},{8,9},{9,8},{10,11... | collective-permute-start | bytes 2457608 | tf_op jit(solution)/shard_map/ppermute | solution.py:187
  121.8 15.8 %collective-permute-start.21 = (bf16[160,2560]{1,0:T(8,128)(2,1)}, bf16[160,2560]{1,0:T(8,128)(2,1)S(1)}, u32[]{:S(2)}, u32[]{:S(2)}) collective-permute-start(bf16[160,2560]{1,0:T(8,128)(2,1)} %collective-permute-done.12.refs_2_), channel_id=1, source_target_pairs={{0,1},{1,0},{2,3},{3,2},{4,5},{5,4},{6,7},{7,6},{8,9},{9,8},{10,11... | collective-permute-start | bytes 2457608 | tf_op jit(solution)/shard_map/ppermute | solution.py:187
  137.5 22.5 %collective-permute-start.22 = (bf16[160,2560]{1,0:T(8,128)(2,1)}, bf16[160,2560]{1,0:T(8,128)(2,1)}, u32[]{:S(2)}, u32[]{:S(2)}) collective-permute-start(bf16[160,2560]{1,0:T(8,128)(2,1)} %collective-permute-done.16.refs_2_), channel_id=1, source_target_pairs={{0,4},{1,5},{2,6},{3,7},{4,8},{5,9},{6,10},{7,11},{8,12},{9,13},{1... | collective-permute-start | bytes 2457608 | tf_op jit(solution)/shard_map/ppermute | solution.py:187
  140.3 30.2 %collective-permute-start.23 = (bf16[160,2560]{1,0:T(8,128)(2,1)}, bf16[160,2560]{1,0:T(8,128)(2,1)}, u32[]{:S(2)}, u32[]{:S(2)}) collective-permute-start(bf16[160,2560]{1,0:T(8,128)(2,1)} %get-tuple-element.96), channel_id=1, source_target_pairs={{0,2},{1,3},{2,0},{3,1},{4,6},{5,7},{6,4},{7,5},{8,10},{9,11},{10,... | collective-permute-start | bytes 2457608 | tf_op jit(solution)/shard_map/ppermute | solution.py:187
  151.2 20.7 %collective-permute-start.24 = (bf16[160,2560]{1,0:T(8,128)(2,1)}, bf16[160,2560]{1,0:T(8,128)(2,1)}, u32[]{:S(2)}, u32[]{:S(2)}) collective-permute-start(bf16[160,2560]{1,0:T(8,128)(2,1)} %collective-permute-done.17.refs_9_), channel_id=1, source_target_pairs={{0,16},{1,17},{2,18},{3,19},{4,20},{5,21},{6,22},{7,23},{8,24},{9,... | collective-permute-start | bytes 2457608 | tf_op jit(solution)/shard_map/ppermute | solution.py:187
  151.2 20.7 %collective-permute-start.25 = (bf16[160,2560]{1,0:T(8,128)(2,1)}, bf16[160,2560]{1,0:T(8,128)(2,1)}, u32[]{:S(2)}, u32[]{:S(2)}) collective-permute-start(bf16[160,2560]{1,0:T(8,128)(2,1)} %collective-permute-done.16.refs_2_), channel_id=1, source_target_pairs={{0,1},{1,0},{2,3},{3,2},{4,5},{5,4},{6,7},{7,6},{8,9},{9,8},{10,11... | collective-permute-start | bytes 2457608 | tf_op jit(solution)/shard_map/ppermute | solution.py:187
  151.4 20.5 %collective-permute-start.26 = (bf16[160,2560]{1,0:T(8,128)(2,1)}, bf16[160,2560]{1,0:T(8,128)(2,1)}, u32[]{:S(2)}, u32[]{:S(2)}) collective-permute-start(bf16[160,2560]{1,0:T(8,128)(2,1)} %collective-permute-done.17.refs_9_), channel_id=1, source_target_pairs={{0,1},{1,0},{2,3},{3,2},{4,5},{5,4},{6,7},{7,6},{8,9},{9,8},{10,11... | collective-permute-start | bytes 2457608 | tf_op jit(solution)/shard_map/ppermute | solution.py:187
  160.0 11.9 %collective-permute-start.27 = (bf16[160,2560]{1,0:T(8,128)(2,1)}, bf16[160,2560]{1,0:T(8,128)(2,1)}, u32[]{:S(2)}, u32[]{:S(2)}) collective-permute-start(bf16[160,2560]{1,0:T(8,128)(2,1)} %collective-permute-done.18.refs_6_), channel_id=1, source_target_pairs={{0,1},{1,0},{2,3},{3,2},{4,5},{5,4},{6,7},{7,6},{8,9},{9,8},{10,11... | collective-permute-start | bytes 2457608 | tf_op jit(solution)/shard_map/ppermute | solution.py:187
  171.9 10.1 %collective-permute-start.28 = (bf16[160,2560]{1,0:T(8,128)(2,1)}, bf16[160,2560]{1,0:T(8,128)(2,1)S(1)}, u32[]{:S(2)}, u32[]{:S(2)}) collective-permute-start(bf16[160,2560]{1,0:T(8,128)(2,1)} %collective-permute-done.22.refs_2_), channel_id=1, source_target_pairs={{0,1},{1,0},{2,3},{3,2},{4,5},{5,4},{6,7},{7,6},{8,9},{9,8},{10,11... | collective-permute-start | bytes 2457608 | tf_op jit(solution)/shard_map/ppermute | solution.py:187
  172.0 10.0 %collective-permute-start.29 = (bf16[160,2560]{1,0:T(8,128)(2,1)}, bf16[160,2560]{1,0:T(8,128)(2,1)S(1)}, u32[]{:S(2)}, u32[]{:S(2)}) collective-permute-start(bf16[160,2560]{1,0:T(8,128)(2,1)} %collective-permute-done.23.refs_6_), channel_id=1, source_target_pairs={{0,1},{1,0},{2,3},{3,2},{4,5},{5,4},{6,7},{7,6},{8,9},{9,8},{10,11... | collective-permute-start | bytes 2457608 | tf_op jit(solution)/shard_map/ppermute | solution.py:187
  172.5 9.6 %collective-permute-start.30 = (bf16[160,2560]{1,0:T(8,128)(2,1)}, bf16[160,2560]{1,0:T(8,128)(2,1)S(1)}, u32[]{:S(2)}, u32[]{:S(2)}) collective-permute-start(bf16[160,2560]{1,0:T(8,128)(2,1)} %collective-permute-done.24.refs_10_), channel_id=1, source_target_pairs={{0,1},{1,0},{2,3},{3,2},{4,5},{5,4},{6,7},{7,6},{8,9},{9,8},{10,11... | collective-permute-start | bytes 2457608 | tf_op jit(solution)/shard_map/ppermute | solution.py:187
  (17 other events, 185.0 us)
where the time goes:
time: 198 us; the launch traced here: 195 us
  starting transfers between devices  68.3 us (34%)
  waiting for transfers between devices  65.2 us (33%)
  Pallas kernels  43.2 us (22%)
  local copies, waits for them, and re-layouts  15.9 us (8%)
    ppermute x29, starting transfers between devices, permute(): return lax.ppermute(array, ('groups', 'dp'), pairs)  59.9 us
    ppermute x29, waiting for transfers between devices, permute(): return lax.ppermute(array, ('groups', 'dp'), pairs)  57.8 us
    pallas_call x4, Pallas kernels, project(): pl.pallas_call(functools.partial(project_kernel, tuple((len(b) for b in b...  33.9 us
    unnamed x36, local copies, waits for them, and re-layouts  11.6 us
    pallas_call x1, Pallas kernels, attend(): pl.pallas_call(functools.partial(attention_kernel, heads), out_shape=jax....  9.29 us
    ppermute x2, starting transfers between devices, within_member(): return lax.ppermute(array, 'dp', pairs)  8.39 us
    ppermute x2, waiting for transfers between devices, within_member(): return lax.ppermute(array, 'dp', pairs)  7.43 us
  transfers between devices with their start and end apart: 31, of which 9 were waited for; matrix products, arithmetic and copies ran while one was open for 1% of the time, Pallas kernels for 17%

commit v1 on v0

v1 whole, which is shorter than its diff:
```python
import functools
import math

import jax
import jax.numpy as jnp
from jax import lax
from jax.experimental import pallas as pl
from jax.experimental.pallas import tpu as pltpu
from jax.sharding import PartitionSpec as P

HEADS = 20
HALO = 1
MEMBER_DEVS = 4
CORES = 2
COLUMNS = 2

masked_score = -1e30
HALO_ROUND = 1
VMEM_LIMIT = 60 * 1024 * 1024


def attention_kernel(first, index_ref, count_ref, q_hbm, k_hbm, v_hbm, before_hbm, after_hbm, gate_ref, o_ref, q_ref, ext_k, ext_v, sems):
    groups, slots, rows, width = q_ref.shape
    head_dim = q_hbm.shape[2] // HEADS
    places = slots + 2 * HALO
    picks = index_ref.shape[0] // slots
    to_exponent = math.log2(math.e) / math.sqrt(head_dim)

    def loads(g):
        at = pl.ds(pl.multiple_of((first + g) * width, width), width)
        pairs = [(q_hbm.at[:, :, at], q_ref.at[g])]
        for i, (own, ext) in enumerate(((k_hbm, ext_k), (v_hbm, ext_v))):
            pairs.append((before_hbm.at[i, :, :, at], ext.at[g, pl.ds(0, HALO)]))
            pairs.append((own.at[:, :, at], ext.at[g, pl.ds(HALO, slots)]))
            pairs.append((after_hbm.at[i, :, :, at], ext.at[g, pl.ds(HALO + slots, HALO)]))
        return [pltpu.make_async_copy(src, dst, sems.at[g, i]) for i, (src, dst) in enumerate(pairs)]

    for c in loads(0):
        c.start()

    def head_group(g, _):
        for c in loads(g):
            c.wait()

        @pl.when(g + 1 < groups)
        def _():
            for c in loads(g + 1):
                c.start()

        base = pl.multiple_of(g * width, width)
        for slot in range(slots):

            @pl.when(slot < count_ref[0])
            def _():
                place = [index_ref[slot * picks + j] for j in range(picks)]
                held = [jnp.minimum(p, places - 1) for p in place]
                ats = [pl.ds(h * head_dim, head_dim) for h in range(width // head_dim)]
                scored, weighed = [], []
                for at in ats:
                    query = q_ref[g, slot, :, at]
                    keyv = jnp.concatenate([ext_k[g, held[j], :, at] for j in range(picks)], axis=0)
                    scored.append(lax.dot_general(query, keyv, (((1,), (1,)), ((), ())), preferred_element_type=jnp.float32))
                for sc in scored:
                    sc = [jnp.where(place[j] < places, sc[:, j * rows : (j + 1) * rows], masked_score) for j in range(picks)]
                    top = jnp.max(functools.reduce(jnp.maximum, sc), axis=1, keepdims=True)
                    raw = [jnp.exp2((s - top) * to_exponent) for s in sc]
                    den = jnp.sum(functools.reduce(jnp.add, raw), axis=1, keepdims=True)
                    weighed.append((jnp.concatenate([r.astype(jnp.bfloat16) for r in raw], axis=1), den))
                for h, at in enumerate(ats):
                    out_at = pl.ds(pl.multiple_of(base + h * head_dim, head_dim), head_dim)
                    vals = jnp.concatenate([ext_v[g, held[j], :, at] for j in range(picks)], axis=0)
                    summed = jnp.dot(weighed[h][0], vals, preferred_element_type=jnp.float32)
                    o_ref[slot, :, out_at] = (summed * (1.0 / weighed[h][1]) * gate_ref[:, out_at]).astype(o_ref.dtype)

            @pl.when(slot >= count_ref[0])
            def _():
                o_ref[slot, :, pl.ds(base, width)] = jnp.zeros((rows, width), o_ref.dtype)

        return 0

    lax.fori_loop(0, groups, head_group, 0)


def attend(queries, keys, values, before, after, neighbours, counts, gate_row, part=0, parts=1):
    slots, rows, channels = queries.shape
    head_dim = channels // HEADS
    heads = 4 if HEADS % 4 == 0 else 1
    width = heads * head_dim
    places = slots + 2 * HALO
    first, last = (-(-(HEADS // heads) * p // parts) for p in (part, part + 1))
    groups = last - first
    gate_row = gate_row[:, first * width : last * width]
    hbm = pl.BlockSpec(memory_space=pltpu.HBM)
    pairs = slots * groups * heads * rows * (neighbours.shape[0] // slots) * rows
    return pl.pallas_call(
        functools.partial(attention_kernel, first),
        out_shape=jax.ShapeDtypeStruct((slots, rows, groups * width), jnp.bfloat16),
        grid_spec=pltpu.PrefetchScalarGridSpec(
            num_scalar_prefetch=2,
            grid=(1,),
            in_specs=[hbm] * 5 + [pl.BlockSpec((1, groups * width), lambda i, *_: (0, 0))],
            out_specs=pl.BlockSpec((slots, rows, groups * width), lambda i, *_: (0, 0, 0)),
            scratch_shapes=[
                pltpu.VMEM((groups, slots, rows, width), jnp.bfloat16),
                pltpu.VMEM((groups, places, rows, width), jnp.bfloat16),
                pltpu.VMEM((groups, places, rows, width), jnp.bfloat16),
                pltpu.SemaphoreType.DMA((groups, 7)),
            ],
        ),
        compiler_params=pltpu.CompilerParams(vmem_limit_bytes=VMEM_LIMIT),
        cost_estimate=pl.CostEstimate(
            flops=4 * pairs * head_dim, bytes_accessed=12 * slots * rows * groups * width, transcendentals=pairs
        ),
        name="attention",
    )(neighbours, counts, queries, keys, values, before, after, gate_row)


def project_kernel(pieces_of, group_ref, own_hbm, sibling_hbm, *refs):
    n = sum(pieces_of)
    own_ref, sibling_ref, att_ref, wbuf, att_sem, in_sem = refs[n:]
    rows = own_hbm.shape[0]
    group = group_ref[0]
    begins, loads, at = [], [], 0
    for b, count in enumerate(pieces_of):
        begins.append(at)
        copies = []
        first = sum(pieces_of[:b])
        for i, piece in enumerate(refs[first : first + count]):
            high = piece.shape[0]
            start = begins[-1]
            if count == 2:
                start = start + (group if i == 0 else 1 - group) * high
            start = pl.multiple_of(start, high)
            copies.append(pltpu.make_async_copy(piece, wbuf.at[pl.ds(start, high)], in_sem.at[b, i]))
            at += high
        loads.append(copies)
    att_loads = [
        pltpu.make_async_copy(src, att_ref.at[pl.ds(i * rows, rows)], att_sem.at[i])
        for i, src in enumerate((own_hbm, sibling_hbm))
    ]
    for c in loads[0] + att_loads:
        c.start()
    asked, arrived, done = 1, 0, 0
    while done < at:
        step = min(256, at - done)
        while arrived < len(loads) and begins[arrived] < done + step:
            for c in loads[arrived]:
                c.wait()
            arrived += 1
            if asked < len(loads):
                for c in loads[asked]:
                    c.start()
                asked += 1
        if done == 0:
            for c in att_loads:
                c.wait()
        for i, ref in enumerate((own_ref, sibling_ref)):
            ref[:, done : done + step] = lax.dot_general(
                att_ref[i * rows : (i + 1) * rows],
                wbuf[done : done + step],
                (((1,), (1,)), ((), ())),
                preferred_element_type=jnp.float32,
            ).astype(ref.dtype)
        done += step


def project(own, sibling, blocks, group):
    rows, channels = own.shape
    pieces = [p for b in blocks for p in b]
    width = sum(p.shape[0] for p in pieces)
    padded = -(-width // 128) * 128
    hbm = pl.BlockSpec(memory_space=pltpu.HBM)
    result = jax.ShapeDtypeStruct((rows, padded), jnp.bfloat16)
    return pl.pallas_call(
        functools.partial(project_kernel, tuple(len(b) for b in blocks)),
        out_shape=(result, result),
        grid_spec=pltpu.PrefetchScalarGridSpec(
            num_scalar_prefetch=1,
            grid=(1,),
            in_specs=[hbm] * (2 + len(pieces)),
            out_specs=(pl.BlockSpec((rows, padded), lambda i, *_: (0, 0)),) * 2,
            scratch_shapes=[
                pltpu.VMEM((2 * rows, channels), jnp.bfloat16),
                pltpu.VMEM((width, channels), jnp.bfloat16),
                pltpu.SemaphoreType.DMA((2,)),
                pltpu.SemaphoreType.DMA((len(blocks), 2)),
            ],
        ),
        compiler_params=pltpu.CompilerParams(vmem_limit_bytes=VMEM_LIMIT),
        cost_estimate=pl.CostEstimate(
            flops=4 * rows * channels * width,
            bytes_accessed=2 * (channels * width + 2 * rows * (channels + width)),
            transcendentals=0,
        ),
        name="project",
    )(group.reshape(1), own, sibling, *pieces)


def assemble_kernel(places, shard, has_old, scalars, *refs):
    arrays, (out_ref, buf, sem) = refs[: len(refs) - 3 - has_old], refs[-3:]
    half = shard // 2
    stores = []
    for b, parts in enumerate(places):
        if b >= 2:
            stores[b - 2].wait()

        def place(first_core, group):
            for c in range(CORES):
                for i, (array, lane) in enumerate(parts):
                    src = arrays[2 * array + (0 if c == first_core else 1)]
                    high = shard if len(parts) == 1 else half
                    to = c * shard + (0 if len(parts) == 1 else (group if i == 0 else 1 - group) * half)
                    buf[b % 2, :, to : to + high] = src[:, lane : lane + high]

        if len(parts) == 1:
            for c in range(CORES):
                pl.when(scalars[0] == c)(functools.partial(place, c, 0))
        else:
            for c in range(CORES):
                for g in range(2):
                    pl.when((scalars[0] == c) & (scalars[1] == g))(functools.partial(place, c, g))
        where = pl.ds(pl.multiple_of(scalars[2 + b] * CORES * shard, CORES * shard), CORES * shard)
        store = pltpu.make_async_copy(buf.at[b % 2], out_ref.at[:, where], sem.at[b % 2])
        store.start()
        stores.append(store)
    for store in stores[-2:]:
        store.wait()


def assemble(arrays, places, scalars, shard, columns, old=None):
    rows = arrays[0].shape[0]
    has_old = int(old is not None)
    hbm = pl.BlockSpec(memory_space=pltpu.HBM)
    return pl.pallas_call(
        functools.partial(assemble_kernel, places, shard, has_old),
        out_shape=jax.ShapeDtypeStruct((rows, columns), jnp.bfloat16),
        grid_spec=pltpu.PrefetchScalarGridSpec(
            num_scalar_prefetch=1,
            grid=(1,),
            in_specs=[pl.BlockSpec(a.shape, lambda i, *_: (0, 0)) for a in arrays] + [hbm] * has_old,
            out_specs=hbm,
            scratch_shapes=[pltpu.VMEM((2, rows, CORES * shard), jnp.bfloat16), pltpu.SemaphoreType.DMA((2,))],
        ),
        input_output_aliases={1 + len(arrays): 0} if has_old else {},
        compiler_params=pltpu.CompilerParams(vmem_limit_bytes=VMEM_LIMIT),
        cost_estimate=pl.CostEstimate(
            flops=0, bytes_accessed=4 * rows * (CORES * shard * len(places)), transcendentals=0
        ),
        name="assemble",
    )(scalars, *arrays, *([old] if has_old else []))


def on_device(groups, devices, queries, keys, values, counts, neighbours, gate_table, step, out_weight):
    slots, rows, channels = queries.shape
    shard = out_weight.shape[1]
    columns = shard * devices
    chips = devices // CORES
    length = chips // COLUMNS

    def permute(array, target):
        pairs = []
        for g in range(groups):
            for d in range(devices):
                to = target(g, d // (CORES * COLUMNS), d // CORES % COLUMNS, d % CORES)
                if to is not None:
                    tg, tz, tx, tc = to
                    pairs.append((g * devices + d, tg * devices + (tz * COLUMNS + tx) * CORES + tc))
        return lax.ppermute(array, ("groups", "dp"), pairs)

    def within_member(array, by):
        pairs = []
        for d in range(devices):
            first, second = (d, (d + by) % devices) if by > 0 else ((d + by) % devices, d)
            if (first - MEMBER_DEVS // 2) % MEMBER_DEVS != MEMBER_DEVS - 1:
                pairs.append((d, (d + by) % devices))
        return lax.ppermute(array, "dp", pairs)

    tail_start = jnp.maximum(counts[0] - HALO, 0)
    tail = jnp.stack([lax.dynamic_slice_in_dim(a, tail_start, HALO, 0) for a in (keys, values)])
    lead = jnp.stack([keys[:HALO], values[:HALO]])
    gate_row = lax.dynamic_slice_in_dim(gate_table, step[0], 1, 0)
    weight = out_weight.T

    if not (groups == 2 and devices % (CORES * COLUMNS) == 0 and length >= 3 and shard % 32 == 0 and (CORES * shard) % 128 == 0):
        before, after = within_member(tail, 1), within_member(lead, -1)
        att = attend(queries, keys, values, before, after, neighbours.reshape(-1), counts, gate_row)
        full = lax.all_gather(weight, "dp", axis=0, tiled=True)
        mixed = lax.dot_general(
            att.reshape(slots * rows, channels), full, (((1,), (1,)), ((), ())), preferred_element_type=jnp.float32
        )
        return mixed.astype(jnp.bfloat16).reshape(slots, rows, columns)

    over = {
        "z": lambda g, z, x, c: (g, (z + 1) % length, x, c),
        "x": lambda g, z, x, c: (g, z, (x + 1) % COLUMNS, c),
        "y": lambda g, z, x, c: (1 - g, z, x, c),
        "s": lambda g, z, x, c: (g, z, x, 1 - c),
    }
    group = lax.axis_index("groups")
    device = lax.axis_index("dp")
    core = device % CORES
    my_x, my_z = device // CORES % COLUMNS, device // (CORES * COLUMNS)

    half = shard // 2
    have = {
        ("z", "p", 0): lax.dynamic_slice_in_dim(weight, group * half, half, 0),
        "weight": weight,
    }
    sends = {
        "z": [(("z", "p", s), ("z", "p", s + 1)) for s in range(length - 1)]
        + [(("z", "q", s), ("z", "q", s + 1)) for s in range(1, length - 1)],
        "x": [(("z", "p", s), ("x", "p", s)) for s in range(length)] + [(("z", "q", 0), ("x", "q", 0))],
        "y": [None, (("z", "p", 1), ("z", "q", 1))] + [(("x", "p", s), ("x", "q", s)) for s in range(1, length)],
    }
    rounds = max(len(v) for v in sends.values())
    every = [("z", s) for s in range(length)] + [("x", s) for s in range(length)]

    def names_of(b):
        return ["weight"] if b == ("z", 0) else [(b[0], h, b[1]) for h in "pq"]

    def chip_of(b):
        x = my_x if b[0] == "z" else (my_x + 1) % COLUMNS
        return (my_z - b[1]) % length * COLUMNS + x

    by_then = {"weight", ("z", "p", 0)} | {s[1] for link in sends.values() for s in link[: rounds - 1] if s}
    whole = [b for b in every if all(n in by_then for n in names_of(b))]
    halves = [b for b in every if b not in whole]
    scalars = [jnp.stack([core, group] + [chip_of(b) for b in bs]).astype(jnp.int32) for bs in (whole, halves)]
    small = [neighbours.reshape(-1), gate_row, scalars, group.reshape(1)]

    arrived, att, att_sibling, early = [], None, None, None
    for r in range(rounds):
        names = list(arrived)
        items = [(link, *sends[link][r]) for link in ("z", "x", "y") if r < len(sends[link]) and sends[link][r]]
        halo = [tail, lead] if r == HALO_ROUND else []
        if r == rounds - 1:
            have[("z", "q", 0)] = weight
        bar = lax.optimization_barrier(
            ([have[n] for n in names], [have[src] for _, src, _ in items], att, att_sibling, halo, small if r else [])
        )
        for n, a in zip(names, bar[0]):
            have[n] = a
        _, sources, att, att_sibling, halo, small = (*bar[:5], bar[5] if r else small)
        arrived = []
        for (link, src, dst), a in zip(items, sources):
            if src == ("z", "q", 0):
                a = lax.dynamic_slice_in_dim(a, (1 - group) * half, half, 0)
            have[dst] = permute(a, over[link])
            arrived.append(dst)
        if halo:
            have["before"], have["after"] = within_member(halo[0], 1), within_member(halo[1], -1)
            arrived += ["before", "after"]
        if r == HALO_ROUND + 1:
            att = attend(queries, keys, values, have["before"], have["after"], small[0], counts, small[1])
            att = att.reshape(slots * rows, channels)
        elif r == HALO_ROUND + 2:
            att_sibling = permute(att, over["s"])
        if r == rounds - 1:
            pieces = [[have[n] for n in names_of(b)] for b in whole] + [[have[(b[0], "p", b[1])]] for b in halves]
            early = project(att, att_sibling, pieces, small[3])
    names = list(arrived)
    bar, early, att, att_sibling = lax.optimization_barrier(([have[n] for n in names], early, att, att_sibling))
    for n, a in zip(names, bar):
        have[n] = a
    early = [early[0], permute(early[1], over["s"])]
    late = project(att, att_sibling, [[have[(b[0], "q", b[1])]] for b in halves], small[3])
    late = [late[0], permute(late[1], over["s"])]
    out = assemble(early, tuple(((0, i * shard),) for i in range(len(whole))), small[2][0], shard, columns)
    at = len(whole) * shard
    places = tuple(((0, at + i * half), (1, i * half)) for i in range(len(halves)))
    out = assemble(early + late, places, small[2][1], shard, columns, out)
    return out.reshape(slots, rows, columns)


def solution(mesh):
    both = P(("groups", "dp"), None, None)
    placed = (both, both, both, P(("groups", "dp")), P(("groups", "dp"), None), P(), P(), P(None, "dp"))
    return jax.shard_map(
        functools.partial(on_device, mesh.shape["groups"], mesh.shape["dp"]),
        mesh=mesh,
        in_specs=placed,
        out_specs=both,
        check_vma=False,
    )
```

time: 198 us -> 156 us (0.79); the launches traced: 195 us -> 156 us
  starting transfers between devices: 68.3 us -> 24.7 us
  waiting for transfers between devices: 65.2 us -> 73.9 us
  local copies, waits for them, and re-layouts: 15.9 us -> 11.4 us
    ppermute x29 -> x17, starting transfers between devices: 59.9 us -> 16.4 us  [permute(): return lax.ppermute(array, ('groups', 'dp'), pairs)]
    ppermute x29 -> x17, waiting for transfers between devices: 57.8 us -> 73.9 us  [permute(): return lax.ppermute(array, ('groups', 'dp'), pairs)]
    pallas_call x1 -> x3, Pallas kernels: 9.29 us -> 20.9 us  [the longest x1 10.6 us: attend(): pl.pallas_call(functools.partial(attention_kernel, first), out_shape=jax....]
    pallas_call x4 -> x2, Pallas kernels: 33.9 us -> 23.2 us  [project(): pl.pallas_call(functools.partial(project_kernel, tuple((len(b) for b in b...]
    ppermute x2, waiting for transfers between devices: 7.43 us -> 0.01 us  [within_member(): return lax.ppermute(array, 'dp', pairs)]
    unnamed x36 -> x20, local copies, waits for them, and re-layouts: 11.6 us -> 4.83 us
  transfers between devices with their start and end apart: 31 -> 19, of which waited for: 9 -> 8; matrix products, arithmetic and copies ran while one was open for 1% -> 3% of each run, Pallas kernels for 17% -> 25%
where the time goes in v1:
time: 156 us
  waiting for transfers between devices  73.9 us (47%)
  Pallas kernels  44.1 us (28%)
  starting transfers between devices  24.7 us (16%)
  local copies, waits for them, and re-layouts  11.4 us (7%)
    ppermute x17, waiting for transfers between devices, permute(): return lax.ppermute(array, ('groups', 'dp'), pairs)  73.9 us
    pallas_call x2, Pallas kernels, project(): pl.pallas_call(functools.partial(project_kernel, tuple((len(b) for b in b...  23.2 us
    ppermute x17, starting transfers between devices, permute(): return lax.ppermute(array, ('groups', 'dp'), pairs)  16.4 us
    pallas_call x1, Pallas kernels, attend(): pl.pallas_call(functools.partial(attention_kernel, first), out_shape=jax....  10.6 us
    pallas_call x2, Pallas kernels, assemble(): pl.pallas_call(functools.partial(assemble_kernel, places, shard, has_old)...  10.3 us
    ppermute x2, starting transfers between devices, within_member(): return lax.ppermute(array, 'dp', pairs)  8.25 us
    unnamed x20, local copies, waits for them, and re-layouts  4.83 us
  transfers between devices with their start and end apart: 19, of which 8 were waited for; matrix products, arithmetic and copies ran while one was open for 3% of the time, Pallas kernels for 25%

profile of v1, /device:TPU:0, one launch (start us, length us, event | category | flops | bytes accessed | tf_op | source)
XLA Modules:
  0.0 155.8 jit_solution(6571569458317664075)
XLA Ops:
  0.0 2.1 %dynamic-slice_bitcast_fusion = bf16[160,2560]{1,0:T(8,128)(2,1)} fusion(bf16[2560,320]{0,1:T(8,128)(2,1)} %param.15, s32[]{:T(128)S(6)} %select_n.63), kind=kLoop, calls=%fused_computation.2 | loop fusion | bytes 1638404 | tf_op jit(solution)/shard_map/dynamic_slice | solution.py:306
  2.2 3.0 %collective-permute-start = (bf16[160,2560]{1,0:T(8,128)(2,1)}, bf16[160,2560]{1,0:T(8,128)(2,1)}, u32[]{:S(2)}, u32[]{:S(2)}) collective-permute-start(bf16[160,2560]{1,0:T(8,128)(2,1)} %dynamic-slice_bitcast_fusion), channel_id=1, source_target_pairs={{0,4},{1,5},{2,6},{3,7},{4,8},{5,9},{6,10},{7,11},{8,12},{9,13},{1... | collective-permute-start | bytes 2457608 | tf_op jit(solution)/shard_map/ppermute | solution.py:268
  5.2 1.5 collective-permute-start.1
  8.0 1.9 %slice_bitcast_fusion = (bf16[1,1,128,2560]{3,2,1,0:T(8,128)(2,1)S(1)}, bf16[1,1,128,2560]{3,2,1,0:T(8,128)(2,1)S(1)}, bf16[1,1,128,2560]{3,2,1,0:T(8,128)(2,1)S(1)}, bf16[1,1,128,2560]{3,2,1,0:T(8,128)(2,1)S(1)}) fusion(bf16[3,128,2560]{2,1,0:T(8,128)(2,1)} %v_hbm.1, s32[]{:T(128)} %bitcast.1, bf16[3,128,2560]{2,1,0:T(8,128)(2,1)} %k_hbm.1), kind=kLoop, calls=%fused_computation.3 | loop fusion | bytes 5242884 | tf_op jit(solution)/shard_map/stack | solution.py:280
  10.5 0.6 reshape.14.index_ref
  11.1 0.6 stack.73.scalars
  11.7 0.7 stack.69.scalars
  12.7 13.1 %collective-permute-done.refs_1_ = bf16[160,2560]{1,0:T(8,128)(2,1)} collective-permute-done((bf16[160,2560]{1,0:T(8,128)(2,1)}, bf16[160,2560]{1,0:T(8,128)(2,1)}, u32[]{:S(2)}, u32[]{:S(2)}) %collective-permute-start) | collective-permute-done | bytes 819232 | tf_op jit(solution)/shard_map/ppermute | solution.py:268
  25.8 1.9 %collective-permute-start.5 = (bf16[2,1,128,2560]{3,2,1,0:T(8,128)(2,1)S(1)}, bf16[2,1,128,2560]{3,2,1,0:T(8,128)(2,1)S(1)}, u32[]{:S(2)}, u32[]{:S(2)}) collective-permute-start(bf16[2,1,128,2560]{3,2,1,0:T(8,128)(2,1)S(1)} %pad_maximum_fusion), channel_id=1, source_target_pairs={{0,1},{2,3},{3,4},{4,5},{6,7},{7,8},{8,9},{10,11},{11,12},{12,13},... | collective-permute-start | bytes 3932168 | tf_op jit(solution)/shard_map/ppermute | solution.py:276
  27.7 6.3 %collective-permute-start.6 = (bf16[2,1,128,2560]{3,2,1,0:T(8,128)(2,1)S(1)}, bf16[2,1,128,2560]{3,2,1,0:T(8,128)(2,1)S(1)}, u32[]{:S(2)}, u32[]{:S(2)}) collective-permute-start(bf16[2,1,128,2560]{3,2,1,0:T(8,128)(2,1)S(1)} %pad_maximum_fusion.1), channel_id=1, source_target_pairs={{0,15},{1,0},{3,2},{4,3},{5,4},{7,6},{8,7},{9,8},{11,10},{12,11},{... | collective-permute-start | bytes 3932168 | tf_op jit(solution)/shard_map/ppermute | solution.py:276
  34.2 1.6 %collective-permute-start.4 = (bf16[160,2560]{1,0:T(8,128)(2,1)}, bf16[160,2560]{1,0:T(8,128)(2,1)}, u32[]{:S(2)}, u32[]{:S(2)}) collective-permute-start(bf16[160,2560]{1,0:T(8,128)(2,1)} %collective-permute-done.refs_1_), channel_id=1, source_target_pairs={{0,16},{1,17},{2,18},{3,19},{4,20},{5,21},{6,22},{7,23},{8,24},{9,... | collective-permute-start | bytes 2457608 | tf_op jit(solution)/shard_map/ppermute | solution.py:268
  35.8 30.9 %collective-permute-done.2.refs_3_ = bf16[160,2560]{1,0:T(8,128)(2,1)} collective-permute-done((bf16[160,2560]{1,0:T(8,128)(2,1)}, bf16[160,2560]{1,0:T(8,128)(2,1)}, u32[]{:S(2)}, u32[]{:S(2)}) %collective-permute-start.2) | collective-permute-done | bytes 819232 | tf_op jit(solution)/shard_map/ppermute | solution.py:268
  66.7 1.1 copy-done.4
  67.8 1.6 %collective-permute-start.8 = (bf16[160,2560]{1,0:T(8,128)(2,1)}, bf16[160,2560]{1,0:T(8,128)(2,1)}, u32[]{:S(2)}, u32[]{:S(2)}) collective-permute-start(bf16[160,2560]{1,0:T(8,128)(2,1)} %collective-permute-done.2.refs_3_), channel_id=1, source_target_pairs={{0,2},{1,3},{2,0},{3,1},{4,6},{5,7},{6,4},{7,5},{8,10},{9,11},{10,... | collective-permute-start | bytes 2457608 | tf_op jit(solution)/shard_map/ppermute | solution.py:268
  69.5 1.5 collective-permute-start.9
  71.0 10.6 %attention.1 = bf16[3,128,2560]{2,1,0:T(8,128)(2,1)} custom-call(s32[9]{0:T(128)} %reshape.14.index_ref, s32[1]{0:T(128)S(6)} %copy.11.count_ref, bf16[3,128,2560]{2,1,0:T(8,128)(2,1)} %q_hbm.1, bf16[3,128,2560]{2,1,0:T(8,128)(2,1)} %k_hbm.1, bf16[3,128,2560]{2,1,0:T(8,128)(2,1)} %v_hbm.1, bf16[2,1,128,2560]{3,2,1,0:T(8,128)(2,1)} %copy-done.3, ...), custom_call_target="tpu_custom_call" | custom-call | flops 1509949440 | bytes 11796480 | tf_op jit(solution)/shard_map/attention/pallas_call | solution.py:95
  81.6 6.2 %collective-permute-done.7.refs_9_ = bf16[160,2560]{1,0:T(8,128)(2,1)} collective-permute-done((bf16[160,2560]{1,0:T(8,128)(2,1)}, bf16[160,2560]{1,0:T(8,128)(2,1)}, u32[]{:S(2)}, u32[]{:S(2)}) %collective-permute-start.7) | collective-permute-done | bytes 819232 | tf_op jit(solution)/shard_map/ppermute | solution.py:268
  88.0 1.4 collective-permute-done.9.refs_6_
  89.5 1.6 %collective-permute-start.10 = (bf16[160,2560]{1,0:T(8,128)(2,1)}, bf16[160,2560]{1,0:T(8,128)(2,1)}, u32[]{:S(2)}, u32[]{:S(2)}) collective-permute-start(bf16[160,2560]{1,0:T(8,128)(2,1)} %collective-permute-done.4.refs_2_), channel_id=1, source_target_pairs={{0,4},{1,5},{2,6},{3,7},{4,8},{5,9},{6,10},{7,11},{8,12},{9,13},{1... | collective-permute-start | bytes 2457608 | tf_op jit(solution)/shard_map/ppermute | solution.py:268
  91.4 1.5 collective-permute-start.12
  92.9 19.4 %collective-permute-done.10.refs_4_ = bf16[160,2560]{1,0:T(8,128)(2,1)} collective-permute-done((bf16[160,2560]{1,0:T(8,128)(2,1)}, bf16[160,2560]{1,0:T(8,128)(2,1)}, u32[]{:S(2)}, u32[]{:S(2)}) %collective-permute-start.10) | collective-permute-done | bytes 819232 | tf_op jit(solution)/shard_map/ppermute | solution.py:268
  112.3 0.9 copy-done.7
  113.2 1.2 collective-permute-start.15
  114.7 1.5 collective-permute-start.16
  116.2 16.7 %project.2 = (bf16[384,2176]{1,0:T(8,128)(2,1)}, bf16[384,2176]{1,0:T(8,128)(2,1)}) custom-call(s32[1]{0:T(128)} %bitcast.8.group_ref, bf16[384,2560]{1,0:T(8,128)(2,1)} %bitcast.29, bf16[384,2560]{1,0:T(8,128)(2,1)} %collective-permute-done.13.sibling_hbm, bf16[320,2560]{1,0:T(8,128)(2,1)} %bitcast.31, bf16[160,2560]{1,0:T(8,128)(2,1)} %collective-permute-done.refs_1_, ...), custom_call_target="tpu_custom_call" | custom-call | flops 8178892800 | bytes 17776640 | tf_op jit(solution)/shard_map/project/pallas_call | solution.py:174
  133.1 2.5 %collective-permute-done.14.refs_0_ = bf16[160,2560]{1,0:T(8,128)(2,1)S(1)} collective-permute-done((bf16[160,2560]{1,0:T(8,128)(2,1)}, bf16[160,2560]{1,0:T(8,128)(2,1)S(1)}, u32[]{:S(2)}, u32[]{:S(2)}) %collective-permute-start.14) | collective-permute-done | bytes 819232 | tf_op jit(solution)/shard_map/ppermute | solution.py:268
  135.6 0.9 copy-done.9
  136.5 6.4 %project.3 = (bf16[384,512]{1,0:T(8,128)(2,1)}, bf16[384,512]{1,0:T(8,128)(2,1)}) custom-call(s32[1]{0:T(128)} %bitcast.8.group_ref, bf16[384,2560]{1,0:T(8,128)(2,1)} %bitcast.30, bf16[384,2560]{1,0:T(8,128)(2,1)} %collective-permute-done.13.sibling_hbm, bf16[160,2560]{1,0:T(8,128)(2,1)} %copy-done.9, bf16[160,2560]{1,0:T(8,128)(2,1)} %copy-done.8, ...), custom_call_target="tpu_custom_call" | custom-call | flops 1887436800 | bytes 7127040 | tf_op jit(solution)/shard_map/project/pallas_call | solution.py:174
  143.5 1.2 copy-done.1
  144.7 5.5 %assemble.2.refs_4_ = bf16[384,5120]{1,0:T(8,128)(2,1)} custom-call(s32[7]{0:T(128)} %stack.69.scalars, bf16[384,2176]{1,0:T(8,128)(2,1)} %get-tuple-element.113.refs_0_, bf16[384,2176]{1,0:T(8,128)(2,1)} %copy-done.1), custom_call_target="tpu_custom_call" | custom-call | bytes 4915200 | tf_op jit(solution)/shard_map/assemble/pallas_call | solution.py:234
  150.2 0.7 copy-done.5
  151.0 4.8 %assemble.3 = bf16[384,5120]{1,0:T(8,128)(2,1)} custom-call(s32[5]{0:T(128)} %stack.73.scalars, bf16[384,2176]{1,0:T(8,128)(2,1)} %get-tuple-element.113.refs_0_, bf16[384,2176]{1,0:T(8,128)(2,1)} %copy-done.1, bf16[384,512]{1,0:T(8,128)(2,1)} %get-tuple-element.120.refs_2_, bf16[384,512]{1,0:T(8,128)(2,1)} %copy-done.5, ...), custom_call_target="tpu_custom_call", output_to_operand_aliasing={{}: (5, {})} | custom-call | bytes 2949120 | tf_op jit(solution)/shard_map/assemble/pallas_call | solution.py:234
  (40 shorter events, 2.7 us)
Async XLA Ops:
  0.0 9.9 %copy-start = (f32[50,2560]{1,0:T(8,128)S(1)}, f32[50,2560]{1,0:T(8,128)}, u32[]{:S(2)}) copy-start(f32[50,2560]{1,0:T(8,128)} %param.13) | copy-start | bytes 1536004
  2.2 23.6 %collective-permute-start = (bf16[160,2560]{1,0:T(8,128)(2,1)}, bf16[160,2560]{1,0:T(8,128)(2,1)}, u32[]{:S(2)}, u32[]{:S(2)}) collective-permute-start(bf16[160,2560]{1,0:T(8,128)(2,1)} %dynamic-slice_bitcast_fusion), channel_id=1, source_target_pairs={{0,4},{1,5},{2,6},{3,7},{4,8},{5,9},{6,10},{7,11},{8,12},{9,13},{1... | collective-permute-start | bytes 2457608 | tf_op jit(solution)/shard_map/ppermute | solution.py:268
  5.2 20.6 %collective-permute-start.1 = (bf16[160,2560]{1,0:T(8,128)(2,1)}, bf16[160,2560]{1,0:T(8,128)(2,1)}, u32[]{:S(2)}, u32[]{:S(2)}) collective-permute-start(bf16[160,2560]{1,0:T(8,128)(2,1)} %dynamic-slice_bitcast_fusion), channel_id=1, source_target_pairs={{0,2},{1,3},{2,0},{3,1},{4,6},{5,7},{6,4},{7,5},{8,10},{9,11},{10,... | collective-permute-start | bytes 2457608 | tf_op jit(solution)/shard_map/ppermute | solution.py:268
  8.0 2.5 %copy-start.6 = (s32[3,3]{1,0:T(4,128)S(1)}, s32[3,3]{1,0:T(4,128)}, u32[]{:S(2)}) copy-start(s32[3,3]{1,0:T(4,128)} %param.12) | copy-start | bytes 112
  12.7 100.5 %copy-start.2 = (bf16[2560,320]{0,1:T(8,128)(2,1)S(1)}, bf16[2560,320]{0,1:T(8,128)(2,1)}, u32[]{:S(2)}) copy-start(bf16[2560,320]{0,1:T(8,128)(2,1)} %param.15) | copy-start | bytes 4915204
  25.8 40.9 %collective-permute-start.5 = (bf16[2,1,128,2560]{3,2,1,0:T(8,128)(2,1)S(1)}, bf16[2,1,128,2560]{3,2,1,0:T(8,128)(2,1)S(1)}, u32[]{:S(2)}, u32[]{:S(2)}) collective-permute-start(bf16[2,1,128,2560]{3,2,1,0:T(8,128)(2,1)S(1)} %pad_maximum_fusion), channel_id=1, source_target_pairs={{0,1},{2,3},{3,4},{4,5},{6,7},{7,8},{8,9},{10,11},{11,12},{12,13},... | collective-permute-start | bytes 3932168 | tf_op jit(solution)/shard_map/ppermute | solution.py:276
  27.7 39.0 %collective-permute-start.6 = (bf16[2,1,128,2560]{3,2,1,0:T(8,128)(2,1)S(1)}, bf16[2,1,128,2560]{3,2,1,0:T(8,128)(2,1)S(1)}, u32[]{:S(2)}, u32[]{:S(2)}) collective-permute-start(bf16[2,1,128,2560]{3,2,1,0:T(8,128)(2,1)S(1)} %pad_maximum_fusion.1), channel_id=1, source_target_pairs={{0,15},{1,0},{3,2},{4,3},{5,4},{7,6},{8,7},{9,8},{11,10},{12,11},{... | collective-permute-start | bytes 3932168 | tf_op jit(solution)/shard_map/ppermute | solution.py:276
  34.0 32.7 %collective-permute-start.2 = (bf16[160,2560]{1,0:T(8,128)(2,1)}, bf16[160,2560]{1,0:T(8,128)(2,1)}, u32[]{:S(2)}, u32[]{:S(2)}) collective-permute-start(bf16[160,2560]{1,0:T(8,128)(2,1)} %collective-permute-done.refs_1_), channel_id=1, source_target_pairs={{0,4},{1,5},{2,6},{3,7},{4,8},{5,9},{6,10},{7,11},{8,12},{9,13},{1... | collective-permute-start | bytes 2457608 | tf_op jit(solution)/shard_map/ppermute | solution.py:268
  34.1 32.6 %collective-permute-start.3 = (bf16[160,2560]{1,0:T(8,128)(2,1)}, bf16[160,2560]{1,0:T(8,128)(2,1)}, u32[]{:S(2)}, u32[]{:S(2)}) collective-permute-start(bf16[160,2560]{1,0:T(8,128)(2,1)} %collective-permute-done.refs_1_), channel_id=1, source_target_pairs={{0,2},{1,3},{2,0},{3,1},{4,6},{5,7},{6,4},{7,5},{8,10},{9,11},{10,... | collective-permute-start | bytes 2457608 | tf_op jit(solution)/shard_map/ppermute | solution.py:268
  34.2 32.5 %collective-permute-start.4 = (bf16[160,2560]{1,0:T(8,128)(2,1)}, bf16[160,2560]{1,0:T(8,128)(2,1)}, u32[]{:S(2)}, u32[]{:S(2)}) collective-permute-start(bf16[160,2560]{1,0:T(8,128)(2,1)} %collective-permute-done.refs_1_), channel_id=1, source_target_pairs={{0,16},{1,17},{2,18},{3,19},{4,20},{5,21},{6,22},{7,23},{8,24},{9,... | collective-permute-start | bytes 2457608 | tf_op jit(solution)/shard_map/ppermute | solution.py:268
  66.7 4.3 %copy-start.3 = (bf16[2,1,128,2560]{3,2,1,0:T(8,128)(2,1)}, bf16[2,1,128,2560]{3,2,1,0:T(8,128)(2,1)S(1)}, u32[]{:S(2)}) copy-start(bf16[2,1,128,2560]{3,2,1,0:T(8,128)(2,1)S(1)} %collective-permute-done.5.before_hbm) | copy-start | bytes 3932164
  66.7 1.1 copy-start.4
  67.8 19.9 %collective-permute-start.7 = (bf16[160,2560]{1,0:T(8,128)(2,1)}, bf16[160,2560]{1,0:T(8,128)(2,1)}, u32[]{:S(2)}, u32[]{:S(2)}) collective-permute-start(bf16[160,2560]{1,0:T(8,128)(2,1)} %collective-permute-done.2.refs_3_), channel_id=1, source_target_pairs={{0,4},{1,5},{2,6},{3,7},{4,8},{5,9},{6,10},{7,11},{8,12},{9,13},{1... | collective-permute-start | bytes 2457608 | tf_op jit(solution)/shard_map/ppermute | solution.py:268
  67.8 20.2 %collective-permute-start.8 = (bf16[160,2560]{1,0:T(8,128)(2,1)}, bf16[160,2560]{1,0:T(8,128)(2,1)}, u32[]{:S(2)}, u32[]{:S(2)}) collective-permute-start(bf16[160,2560]{1,0:T(8,128)(2,1)} %collective-permute-done.2.refs_3_), channel_id=1, source_target_pairs={{0,2},{1,3},{2,0},{3,1},{4,6},{5,7},{6,4},{7,5},{8,10},{9,11},{10,... | collective-permute-start | bytes 2457608 | tf_op jit(solution)/shard_map/ppermute | solution.py:268
  69.5 20.0 %collective-permute-start.9 = (bf16[160,2560]{1,0:T(8,128)(2,1)}, bf16[160,2560]{1,0:T(8,128)(2,1)}, u32[]{:S(2)}, u32[]{:S(2)}) collective-permute-start(bf16[160,2560]{1,0:T(8,128)(2,1)} %collective-permute-done.3.refs_5_), channel_id=1, source_target_pairs={{0,16},{1,17},{2,18},{3,19},{4,20},{5,21},{6,22},{7,23},{8,24},{9,... | collective-permute-start | bytes 2457608 | tf_op jit(solution)/shard_map/ppermute | solution.py:268
  89.5 22.8 %collective-permute-start.13 = (bf16[384,2560]{1,0:T(8,128)(2,1)}, bf16[384,2560]{1,0:T(8,128)(2,1)}, u32[]{:S(2)}, u32[]{:S(2)}) collective-permute-start(bf16[384,2560]{1,0:T(8,128)(2,1)} %bitcast.28), channel_id=1, source_target_pairs={{0,1},{1,0},{2,3},{3,2},{4,5},{5,4},{6,7},{7,6},{8,9},{9,8},{10,11... | collective-permute-start | bytes 5898248 | tf_op jit(solution)/shard_map/ppermute | solution.py:268
  89.5 22.8 %collective-permute-start.10 = (bf16[160,2560]{1,0:T(8,128)(2,1)}, bf16[160,2560]{1,0:T(8,128)(2,1)}, u32[]{:S(2)}, u32[]{:S(2)}) collective-permute-start(bf16[160,2560]{1,0:T(8,128)(2,1)} %collective-permute-done.4.refs_2_), channel_id=1, source_target_pairs={{0,4},{1,5},{2,6},{3,7},{4,8},{5,9},{6,10},{7,11},{8,12},{9,13},{1... | collective-permute-start | bytes 2457608 | tf_op jit(solution)/shard_map/ppermute | solution.py:268
  91.1 21.2 %collective-permute-start.11 = (bf16[160,2560]{1,0:T(8,128)(2,1)}, bf16[160,2560]{1,0:T(8,128)(2,1)}, u32[]{:S(2)}, u32[]{:S(2)}) collective-permute-start(bf16[160,2560]{1,0:T(8,128)(2,1)} %collective-permute-done.7.refs_9_), channel_id=1, source_target_pairs={{0,2},{1,3},{2,0},{3,1},{4,6},{5,7},{6,4},{7,5},{8,10},{9,11},{10,... | collective-permute-start | bytes 2457608 | tf_op jit(solution)/shard_map/ppermute | solution.py:268
  91.4 20.9 %collective-permute-start.12 = (bf16[160,2560]{1,0:T(8,128)(2,1)}, bf16[160,2560]{1,0:T(8,128)(2,1)S(1)}, u32[]{:S(2)}, u32[]{:S(2)}) collective-permute-start(bf16[160,2560]{1,0:T(8,128)(2,1)} %collective-permute-done.8.refs_7_), channel_id=1, source_target_pairs={{0,16},{1,17},{2,18},{3,19},{4,20},{5,21},{6,22},{7,23},{8,24},{9,... | collective-permute-start | bytes 2457608 | tf_op jit(solution)/shard_map/ppermute | solution.py:268
  112.2 0.9 copy-start.7
  113.2 19.9 %collective-permute-start.15 = (bf16[160,2560]{1,0:T(8,128)(2,1)S(1)}, bf16[160,2560]{1,0:T(8,128)(2,1)S(1)}, u32[]{:S(2)}, u32[]{:S(2)}) collective-permute-start(bf16[160,2560]{1,0:T(8,128)(2,1)S(1)} %constant_dynamic-slice_fusion), channel_id=1, source_target_pairs={{0,2},{1,3},{2,0},{3,1},{4,6},{5,7},{6,4},{7,5},{8,10},{9,11},{10,... | collective-permute-start | bytes 2457608 | tf_op jit(solution)/shard_map/ppermute | solution.py:268
  114.4 21.2 %collective-permute-start.14 = (bf16[160,2560]{1,0:T(8,128)(2,1)}, bf16[160,2560]{1,0:T(8,128)(2,1)S(1)}, u32[]{:S(2)}, u32[]{:S(2)}) collective-permute-start(bf16[160,2560]{1,0:T(8,128)(2,1)} %collective-permute-done.10.refs_4_), channel_id=1, source_target_pairs={{0,4},{1,5},{2,6},{3,7},{4,8},{5,9},{6,10},{7,11},{8,12},{9,13},{1... | collective-permute-start | bytes 2457608 | tf_op jit(solution)/shard_map/ppermute | solution.py:268
  114.7 20.9 %collective-permute-start.16 = (bf16[160,2560]{1,0:T(8,128)(2,1)}, bf16[160,2560]{1,0:T(8,128)(2,1)}, u32[]{:S(2)}, u32[]{:S(2)}) collective-permute-start(bf16[160,2560]{1,0:T(8,128)(2,1)} %collective-permute-done.11.refs_11_), channel_id=1, source_target_pairs={{0,16},{1,17},{2,18},{3,19},{4,20},{5,21},{6,22},{7,23},{8,24},{9,... | collective-permute-start | bytes 2457608 | tf_op jit(solution)/shard_map/ppermute | solution.py:268
  133.1 2.5 %copy-start.8 = (bf16[160,2560]{1,0:T(8,128)(2,1)}, bf16[160,2560]{1,0:T(8,128)(2,1)S(1)}, u32[]{:S(2)}) copy-start(bf16[160,2560]{1,0:T(8,128)(2,1)S(1)} %collective-permute-done.15.refs_1_) | copy-start | bytes 2457604
  135.6 0.9 copy-start.9
  136.5 7.0 %collective-permute-start.17 = (bf16[384,2176]{1,0:T(8,128)(2,1)}, bf16[384,2176]{1,0:T(8,128)(2,1)S(1)}, u32[]{:S(2)}, u32[]{:S(2)}) collective-permute-start(bf16[384,2176]{1,0:T(8,128)(2,1)} %get-tuple-element.114), channel_id=1, source_target_pairs={{0,1},{1,0},{2,3},{3,2},{4,5},{5,4},{6,7},{7,6},{8,9},{9,8},{10,11... | collective-permute-start | bytes 5013512 | tf_op jit(solution)/shard_map/ppermute | solution.py:268
  142.9 7.3 %collective-permute-start.18 = (bf16[384,512]{1,0:T(8,128)(2,1)}, bf16[384,512]{1,0:T(8,128)(2,1)S(1)}, u32[]{:S(2)}, u32[]{:S(2)}) collective-permute-start(bf16[384,512]{1,0:T(8,128)(2,1)} %get-tuple-element.121), channel_id=1, source_target_pairs={{0,1},{1,0},{2,3},{3,2},{4,5},{5,4},{6,7},{7,6},{8,9},{9,8},{10,11... | collective-permute-start | bytes 1179656 | tf_op jit(solution)/shard_map/ppermute | solution.py:268
  143.5 1.2 copy-start.1
  150.2 0.7 copy-start.5

commit v2 on v1

--- a/solution.py
+++ b/solution.py
@@ -81,7 +81,7 @@
     lax.fori_loop(0, groups, head_group, 0)
 
 
-def attend(queries, keys, values, before, after, neighbours, counts, gate_row, part=0, parts=1):
+def attend(queries, keys, values, halo, neighbours, counts, gate_row, part=0, parts=1):
     slots, rows, channels = queries.shape
     head_dim = channels // HEADS
     heads = 4 if HEADS % 4 == 0 else 1
@@ -112,7 +112,7 @@
             flops=4 * pairs * head_dim, bytes_accessed=12 * slots * rows * groups * width, transcendentals=pairs
         ),
         name="attention",
-    )(neighbours, counts, queries, keys, values, before, after, gate_row)
+    )(neighbours, counts, queries, keys, values, *halo, gate_row)
 
 
 def project_kernel(pieces_of, group_ref, own_hbm, sibling_hbm, *refs):
@@ -138,7 +138,7 @@
         pltpu.make_async_copy(src, att_ref.at[pl.ds(i * rows, rows)], att_sem.at[i])
         for i, src in enumerate((own_hbm, sibling_hbm))
     ]
-    for c in loads[0] + att_loads:
+    for c in att_loads[:1] + loads[0] + att_loads[1:]:
         c.start()
     asked, arrived, done = 1, 0, 0
     while done < at:
@@ -151,10 +151,9 @@
                 for c in loads[asked]:
                     c.start()
                 asked += 1
-        if done == 0:
-            for c in att_loads:
-                c.wait()
         for i, ref in enumerate((own_ref, sibling_ref)):
+            if done == 0:
+                att_loads[i].wait()
             ref[:, done : done + step] = lax.dot_general(
                 att_ref[i * rows : (i + 1) * rows],
                 wbuf[done : done + step],
@@ -169,7 +168,8 @@
     pieces = [p for b in blocks for p in b]
     width = sum(p.shape[0] for p in pieces)
     padded = -(-width // 128) * 128
-    hbm = pl.BlockSpec(memory_space=pltpu.HBM)
+    hbm = pl.BlockSpec(memory_space=pl.ANY)
+    limit = (32 if len(pieces) > 4 else 20) * 1024 * 1024
     result = jax.ShapeDtypeStruct((rows, padded), jnp.bfloat16)
     return pl.pallas_call(
         functools.partial(project_kernel, tuple(len(b) for b in blocks)),
@@ -186,7 +186,7 @@
                 pltpu.SemaphoreType.DMA((len(blocks), 2)),
             ],
         ),
-        compiler_params=pltpu.CompilerParams(vmem_limit_bytes=VMEM_LIMIT),
+        compiler_params=pltpu.CompilerParams(vmem_limit_bytes=limit),
         cost_estimate=pl.CostEstimate(
             flops=4 * rows * channels * width,
             bytes_accessed=2 * (channels * width + 2 * rows * (channels + width)),
@@ -196,21 +196,21 @@
     )(group.reshape(1), own, sibling, *pieces)
 
 
-def assemble_kernel(places, shard, has_old, scalars, *refs):
-    arrays, (out_ref, buf, sem) = refs[: len(refs) - 3 - has_old], refs[-3:]
+def assemble_kernel(places, shard, scalars, *refs):
+    arrays, (out_ref, buf, sem) = refs[:-3], refs[-3:]
     half = shard // 2
+    high = buf.shape[1]
+    rows = pl.ds(pl.multiple_of(pl.program_id(0) * high, high), high)
     stores = []
     for b, parts in enumerate(places):
-        if b >= 2:
-            stores[b - 2].wait()
 
         def place(first_core, group):
             for c in range(CORES):
                 for i, (array, lane) in enumerate(parts):
                     src = arrays[2 * array + (0 if c == first_core else 1)]
-                    high = shard if len(parts) == 1 else half
+                    wide = shard if len(parts) == 1 else half
                     to = c * shard + (0 if len(parts) == 1 else (group if i == 0 else 1 - group) * half)
-                    buf[b % 2, :, to : to + high] = src[:, lane : lane + high]
+                    buf[b, :, to : to + wide] = src[:, lane : lane + wide]
 
         if len(parts) == 1:
             for c in range(CORES):
@@ -220,34 +220,33 @@
                 for g in range(2):
                     pl.when((scalars[0] == c) & (scalars[1] == g))(functools.partial(place, c, g))
         where = pl.ds(pl.multiple_of(scalars[2 + b] * CORES * shard, CORES * shard), CORES * shard)
-        store = pltpu.make_async_copy(buf.at[b % 2], out_ref.at[:, where], sem.at[b % 2])
+        store = pltpu.make_async_copy(buf.at[b], out_ref.at[rows, where], sem.at[b])
         store.start()
         stores.append(store)
-    for store in stores[-2:]:
+    for store in stores:
         store.wait()
 
 
-def assemble(arrays, places, scalars, shard, columns, old=None):
+def assemble(arrays, places, scalars, shard, columns):
     rows = arrays[0].shape[0]
-    has_old = int(old is not None)
-    hbm = pl.BlockSpec(memory_space=pltpu.HBM)
+    chunk = 128 if rows % 128 == 0 else rows
     return pl.pallas_call(
-        functools.partial(assemble_kernel, places, shard, has_old),
+        functools.partial(assemble_kernel, places, shard),
         out_shape=jax.ShapeDtypeStruct((rows, columns), jnp.bfloat16),
         grid_spec=pltpu.PrefetchScalarGridSpec(
             num_scalar_prefetch=1,
-            grid=(1,),
-            in_specs=[pl.BlockSpec(a.shape, lambda i, *_: (0, 0)) for a in arrays] + [hbm] * has_old,
-            out_specs=hbm,
-            scratch_shapes=[pltpu.VMEM((2, rows, CORES * shard), jnp.bfloat16), pltpu.SemaphoreType.DMA((2,))],
-        ),
-        input_output_aliases={1 + len(arrays): 0} if has_old else {},
-        compiler_params=pltpu.CompilerParams(vmem_limit_bytes=VMEM_LIMIT),
-        cost_estimate=pl.CostEstimate(
-            flops=0, bytes_accessed=4 * rows * (CORES * shard * len(places)), transcendentals=0
-        ),
+            grid=(rows // chunk,),
+            in_specs=[pl.BlockSpec((chunk, a.shape[1]), lambda i, *_: (i, 0)) for a in arrays],
+            out_specs=pl.BlockSpec(memory_space=pltpu.HBM),
+            scratch_shapes=[
+                pltpu.VMEM((len(places), chunk, CORES * shard), jnp.bfloat16),
+                pltpu.SemaphoreType.DMA((len(places),)),
+            ],
+        ),
+        compiler_params=pltpu.CompilerParams(vmem_limit_bytes=20 * 1024 * 1024),
+        cost_estimate=pl.CostEstimate(flops=0, bytes_accessed=4 * rows * columns, transcendentals=0),
         name="assemble",
-    )(scalars, *arrays, *([old] if has_old else []))
+    )(scalars, *arrays)
 
 
 def on_device(groups, devices, queries, keys, values, counts, neighbours, gate_table, step, out_weight):
@@ -276,14 +275,13 @@
         return lax.ppermute(array, "dp", pairs)
 
     tail_start = jnp.maximum(counts[0] - HALO, 0)
-    tail = jnp.stack([lax.dynamic_slice_in_dim(a, tail_start, HALO, 0) for a in (keys, values)])
-    lead = jnp.stack([keys[:HALO], values[:HALO]])
+    edges = [(lax.dynamic_slice_in_dim(a, tail_start, HALO, 0), a[:HALO]) for a in (keys, values)]
     gate_row = lax.dynamic_slice_in_dim(gate_table, step[0], 1, 0)
     weight = out_weight.T
 
     if not (groups == 2 and devices % (CORES * COLUMNS) == 0 and length >= 3 and shard % 32 == 0 and (CORES * shard) % 128 == 0):
-        before, after = within_member(tail, 1), within_member(lead, -1)
-        att = attend(queries, keys, values, before, after, neighbours.reshape(-1), counts, gate_row)
+        halo = [within_member(jnp.stack(e), by) for e, by in zip(zip(*edges), (1, -1))]
+        att = attend(queries, keys, values, halo, neighbours.reshape(-1), counts, gate_row)
         full = lax.all_gather(weight, "dp", axis=0, tiled=True)
         mixed = lax.dot_general(
             att.reshape(slots * rows, channels), full, (((1,), (1,)), ((), ())), preferred_element_type=jnp.float32
@@ -325,33 +323,32 @@
     by_then = {"weight", ("z", "p", 0)} | {s[1] for link in sends.values() for s in link[: rounds - 1] if s}
     whole = [b for b in every if all(n in by_then for n in names_of(b))]
     halves = [b for b in every if b not in whole]
-    scalars = [jnp.stack([core, group] + [chip_of(b) for b in bs]).astype(jnp.int32) for bs in (whole, halves)]
-    small = [neighbours.reshape(-1), gate_row, scalars, group.reshape(1)]
+    scalars = jnp.stack([core, group] + [chip_of(b) for b in whole + halves]).astype(jnp.int32)
+    small = [neighbours.reshape(-1), gate_row, scalars, group.reshape(1), weight]
 
     arrived, att, att_sibling, early = [], None, None, None
     for r in range(rounds):
         names = list(arrived)
         items = [(link, *sends[link][r]) for link in ("z", "x", "y") if r < len(sends[link]) and sends[link][r]]
-        halo = [tail, lead] if r == HALO_ROUND else []
-        if r == rounds - 1:
-            have[("z", "q", 0)] = weight
+        edge = [jnp.stack(e) for e in zip(*edges)] if r == HALO_ROUND else []
         bar = lax.optimization_barrier(
-            ([have[n] for n in names], [have[src] for _, src, _ in items], att, att_sibling, halo, small if r else [])
+            ([have[n] for n in names], [have[src] for _, src, _ in items], att, att_sibling, edge, small if r else [])
         )
         for n, a in zip(names, bar[0]):
             have[n] = a
-        _, sources, att, att_sibling, halo, small = (*bar[:5], bar[5] if r else small)
+        _, sources, att, att_sibling, edge, small = (*bar[:5], bar[5] if r else small)
         arrived = []
         for (link, src, dst), a in zip(items, sources):
-            if src == ("z", "q", 0):
-                a = lax.dynamic_slice_in_dim(a, (1 - group) * half, half, 0)
             have[dst] = permute(a, over[link])
             arrived.append(dst)
-        if halo:
-            have["before"], have["after"] = within_member(halo[0], 1), within_member(halo[1], -1)
-            arrived += ["before", "after"]
+        for by, a in zip((1, -1), edge):
+            have["halo", by] = within_member(a, by)
+        if r == 1:
+            have[("z", "q", 0)] = lax.dynamic_slice_in_dim(small[4], (1 - group) * half, half, 0)
+            arrived.append(("z", "q", 0))
         if r == HALO_ROUND + 1:
-            att = attend(queries, keys, values, have["before"], have["after"], small[0], counts, small[1])
+            halo = [have["halo", by] for by in (1, -1)]
+            att = attend(queries, keys, values, halo, small[0], counts, small[1])
             att = att.reshape(slots * rows, channels)
         elif r == HALO_ROUND + 2:
             att_sibling = permute(att, over["s"])
@@ -365,10 +362,10 @@
     early = [early[0], permute(early[1], over["s"])]
     late = project(att, att_sibling, [[have[(b[0], "q", b[1])]] for b in halves], small[3])
     late = [late[0], permute(late[1], over["s"])]
-    out = assemble(early, tuple(((0, i * shard),) for i in range(len(whole))), small[2][0], shard, columns)
     at = len(whole) * shard
-    places = tuple(((0, at + i * half), (1, i * half)) for i in range(len(halves)))
-    out = assemble(early + late, places, small[2][1], shard, columns, out)
+    places = tuple(((0, i * shard),) for i in range(len(whole)))
+    places += tuple(((0, at + i * half), (1, i * half)) for i in range(len(halves)))
+    out = assemble(early + late, places, small[2], shard, columns)
     return out.reshape(slots, rows, columns)
 
 

time: 156 us -> 138 us (0.88)
  waiting for transfers between devices: 73.9 us -> 45 us
  starting transfers between devices: 24.7 us -> 42.6 us
  Pallas kernels: 44.1 us -> 37.1 us
  other arithmetic: 0.24 us -> 2.35 us
  local copies, waits for them, and re-layouts: 11.4 us -> 9.47 us
    ppermute x17, waiting for transfers between devices: 73.9 us -> 41.8 us  [permute(): return lax.ppermute(array, ('groups', 'dp'), pairs)]
    ppermute x17, starting transfers between devices: 16.4 us -> 34.3 us  [permute(): return lax.ppermute(array, ('groups', 'dp'), pairs)]
    pallas_call x2 -> x1, Pallas kernels: 10.3 us -> 5.55 us  [assemble(): pl.pallas_call(functools.partial(assemble_kernel, places, shard), out_sha...]
    pallas_call x2, Pallas kernels: 23.2 us -> 18.8 us  [project(): pl.pallas_call(functools.partial(project_kernel, tuple((len(b) for b in b...]
    ppermute x2, waiting for transfers between devices: 0.01 us -> 3.17 us  [within_member(): return lax.ppermute(array, 'dp', pairs)]
    unnamed x20 -> x12, local copies, waits for them, and re-layouts: 4.83 us -> 2.13 us
    another operation x2, other arithmetic: 0.24 us -> 2.35 us  [on_device(): edge = [jnp.stack(e) for e in zip(*edges)] if r == HALO_ROUND else []]
    pallas_call x1, Pallas kernels: 10.6 us -> 12.7 us  [attend(): pl.pallas_call(functools.partial(attention_kernel, first), out_shape=jax....]
  transfers between devices with their start and end apart: 19 -> 19, of which waited for: 8 -> 9; matrix products, arithmetic and copies ran while one was open for 3% -> 5% of each run, Pallas kernels for 25% -> 23%
where the time goes in v2:
time: 138 us
  waiting for transfers between devices  45 us (33%)
  starting transfers between devices  42.6 us (31%)
  Pallas kernels  37.1 us (27%)
  local copies, waits for them, and re-layouts  9.47 us (7%)
  other arithmetic  2.35 us (2%)
  between operations  1.59 us (1%)
    ppermute x17, waiting for transfers between devices, permute(): return lax.ppermute(array, ('groups', 'dp'), pairs)  41.8 us
    ppermute x17, starting transfers between devices, permute(): return lax.ppermute(array, ('groups', 'dp'), pairs)  34.3 us
    pallas_call x2, Pallas kernels, project(): pl.pallas_call(functools.partial(project_kernel, tuple((len(b) for b in b...  18.8 us
    pallas_call x1, Pallas kernels, attend(): pl.pallas_call(functools.partial(attention_kernel, first), out_shape=jax....  12.7 us
    ppermute x2, starting transfers between devices, within_member(): return lax.ppermute(array, 'dp', pairs)  8.25 us
    pallas_call x1, Pallas kernels, assemble(): pl.pallas_call(functools.partial(assemble_kernel, places, shard), out_sha...  5.55 us
    ppermute x2, waiting for transfers between devices, within_member(): return lax.ppermute(array, 'dp', pairs)  3.17 us
    another operation x1, local copies, waits for them, and re-layouts, on_device(): edge = [jnp.stack(e) for e in zip(*edges)] if r == HALO_ROUND else []  2.92 us
  transfers between devices with their start and end apart: 19, of which 9 were waited for; matrix products, arithmetic and copies ran while one was open for 5% of the time, Pallas kernels for 23%

profile of v2, /device:TPU:0, one launch (start us, length us, event | category | flops | bytes accessed | tf_op | source)
XLA Modules:
  0.0 138.1 jit_solution(9630420250725037809)
XLA Ops:
  0.0 2.1 %dynamic-slice_bitcast_fusion = bf16[160,2560]{1,0:T(8,128)(2,1)} fusion(bf16[2560,320]{0,1:T(8,128)(2,1)} %param.15, s32[]{:T(128)S(6)} %select_n.63), kind=kLoop, calls=%fused_computation.2 | loop fusion | bytes 1638404 | tf_op jit(solution)/shard_map/dynamic_slice | solution.py:304
  2.1 3.0 %collective-permute-start = (bf16[160,2560]{1,0:T(8,128)(2,1)}, bf16[160,2560]{1,0:T(8,128)(2,1)S(1)}, u32[]{:S(2)}, u32[]{:S(2)}) collective-permute-start(bf16[160,2560]{1,0:T(8,128)(2,1)} %dynamic-slice_bitcast_fusion), channel_id=1, source_target_pairs={{0,4},{1,5},{2,6},{3,7},{4,8},{5,9},{6,10},{7,11},{8,12},{9,13},{1... | collective-permute-start | bytes 2457608 | tf_op jit(solution)/shard_map/ppermute | solution.py:267
  5.2 1.5 %collective-permute-start.1 = (bf16[160,2560]{1,0:T(8,128)(2,1)}, bf16[160,2560]{1,0:T(8,128)(2,1)}, u32[]{:S(2)}, u32[]{:S(2)}) collective-permute-start(bf16[160,2560]{1,0:T(8,128)(2,1)} %dynamic-slice_bitcast_fusion), channel_id=1, source_target_pairs={{0,2},{1,3},{2,0},{3,1},{4,6},{5,7},{6,4},{7,5},{8,10},{9,11},{10,... | collective-permute-start | bytes 2457608 | tf_op jit(solution)/shard_map/ppermute | solution.py:267
  8.0 2.9 %slice_bitcast_fusion = (bf16[1,1,128,2560]{3,2,1,0:T(8,128)(2,1)S(1)}, bf16[1,1,128,2560]{3,2,1,0:T(8,128)(2,1)}, bf16[1,1,128,2560]{3,2,1,0:T(8,128)(2,1)}, bf16[1,1,128,2560]{3,2,1,0:T(8,128)(2,1)S(1)}) fusion(bf16[3,128,2560]{2,1,0:T(8,128)(2,1)} %v_hbm.1, s32[]{:T(128)} %bitcast.1, bf16[3,128,2560]{2,1,0:T(8,128)(2,1)} %k_hbm.1), kind=kLoop, calls=%fused_computation.3 | loop fusion | bytes 5242884 | tf_op jit(solution)/shard_map/stack | solution.py:333
  11.5 0.6 reshape.14.index_ref
  12.2 1.2 pad_maximum_fusion.1
  14.0 1.2 pad_maximum_fusion
  15.1 10.5 %collective-permute-done.refs_1_ = bf16[160,2560]{1,0:T(8,128)(2,1)S(1)} collective-permute-done((bf16[160,2560]{1,0:T(8,128)(2,1)}, bf16[160,2560]{1,0:T(8,128)(2,1)S(1)}, u32[]{:S(2)}, u32[]{:S(2)}) %collective-permute-start) | collective-permute-done | bytes 819232 | tf_op jit(solution)/shard_map/ppermute | solution.py:267
  25.7 1.1 collective-permute-start.2
  26.8 1.5 %collective-permute-start.3 = (bf16[160,2560]{1,0:T(8,128)(2,1)S(1)}, bf16[160,2560]{1,0:T(8,128)(2,1)}, u32[]{:S(2)}, u32[]{:S(2)}) collective-permute-start(bf16[160,2560]{1,0:T(8,128)(2,1)S(1)} %collective-permute-done.refs_1_), channel_id=1, source_target_pairs={{0,2},{1,3},{2,0},{3,1},{4,6},{5,7},{6,4},{7,5},{8,10},{9,11},{10,... | collective-permute-start | bytes 2457608 | tf_op jit(solution)/shard_map/ppermute | solution.py:267
  28.3 1.5 %collective-permute-start.4 = (bf16[160,2560]{1,0:T(8,128)(2,1)S(1)}, bf16[160,2560]{1,0:T(8,128)(2,1)}, u32[]{:S(2)}, u32[]{:S(2)}) collective-permute-start(bf16[160,2560]{1,0:T(8,128)(2,1)S(1)} %collective-permute-done.refs_1_), channel_id=1, source_target_pairs={{0,16},{1,17},{2,18},{3,19},{4,20},{5,21},{6,22},{7,23},{8,24},{9,... | collective-permute-start | bytes 2457608 | tf_op jit(solution)/shard_map/ppermute | solution.py:267
  29.8 1.9 %collective-permute-start.8 = (bf16[2,1,128,2560]{3,2,1,0:T(8,128)(2,1)}, bf16[2,1,128,2560]{3,2,1,0:T(8,128)(2,1)}, u32[]{:S(2)}, u32[]{:S(2)}) collective-permute-start(bf16[2,1,128,2560]{3,2,1,0:T(8,128)(2,1)} %pad_maximum_fusion), channel_id=1, source_target_pairs={{0,1},{2,3},{3,4},{4,5},{6,7},{7,8},{8,9},{10,11},{11,12},{12,13},... | collective-permute-start | bytes 3932168 | tf_op jit(solution)/shard_map/ppermute | solution.py:275
  31.7 6.3 %collective-permute-start.9 = (bf16[2,1,128,2560]{3,2,1,0:T(8,128)(2,1)}, bf16[2,1,128,2560]{3,2,1,0:T(8,128)(2,1)}, u32[]{:S(2)}, u32[]{:S(2)}) collective-permute-start(bf16[2,1,128,2560]{3,2,1,0:T(8,128)(2,1)} %pad_maximum_fusion.1), channel_id=1, source_target_pairs={{0,15},{1,0},{3,2},{4,3},{5,4},{7,6},{8,7},{9,8},{11,10},{12,11},{... | collective-permute-start | bytes 3932168 | tf_op jit(solution)/shard_map/ppermute | solution.py:275
  38.1 1.0 constant_dynamic-slice_fusion
  39.0 8.1 %collective-permute-done.2.refs_3_ = bf16[160,2560]{1,0:T(8,128)(2,1)} collective-permute-done((bf16[160,2560]{1,0:T(8,128)(2,1)S(1)}, bf16[160,2560]{1,0:T(8,128)(2,1)}, u32[]{:S(2)}, u32[]{:S(2)}) %collective-permute-start.2) | collective-permute-done | bytes 819232 | tf_op jit(solution)/shard_map/ppermute | solution.py:267
  47.1 14.2 %collective-permute-start.5 = (bf16[160,2560]{1,0:T(8,128)(2,1)}, bf16[160,2560]{1,0:T(8,128)(2,1)}, u32[]{:S(2)}, u32[]{:S(2)}) collective-permute-start(bf16[160,2560]{1,0:T(8,128)(2,1)} %collective-permute-done.2.refs_3_), channel_id=1, source_target_pairs={{0,4},{1,5},{2,6},{3,7},{4,8},{5,9},{6,10},{7,11},{8,12},{9,13},{1... | collective-permute-start | bytes 2457608 | tf_op jit(solution)/shard_map/ppermute | solution.py:267
  61.4 1.5 %collective-permute-start.7 = (bf16[160,2560]{1,0:T(8,128)(2,1)}, bf16[160,2560]{1,0:T(8,128)(2,1)}, u32[]{:S(2)}, u32[]{:S(2)}) collective-permute-start(bf16[160,2560]{1,0:T(8,128)(2,1)} %collective-permute-done.3.refs_5_), channel_id=1, source_target_pairs={{0,16},{1,17},{2,18},{3,19},{4,20},{5,21},{6,22},{7,23},{8,24},{9,... | collective-permute-start | bytes 2457608 | tf_op jit(solution)/shard_map/ppermute | solution.py:267
  62.9 3.2 %collective-permute-done.9.after_hbm = bf16[2,1,128,2560]{3,2,1,0:T(8,128)(2,1)} collective-permute-done((bf16[2,1,128,2560]{3,2,1,0:T(8,128)(2,1)}, bf16[2,1,128,2560]{3,2,1,0:T(8,128)(2,1)}, u32[]{:S(2)}, u32[]{:S(2)}) %collective-permute-start.9) | collective-permute-done | bytes 1310752 | tf_op jit(solution)/shard_map/ppermute | solution.py:275
  66.1 12.7 %attention.1 = bf16[3,128,2560]{2,1,0:T(8,128)(2,1)} custom-call(s32[9]{0:T(128)} %reshape.14.index_ref, s32[1]{0:T(128)S(6)} %copy.9.count_ref, bf16[3,128,2560]{2,1,0:T(8,128)(2,1)} %q_hbm.1, bf16[3,128,2560]{2,1,0:T(8,128)(2,1)} %k_hbm.1, bf16[3,128,2560]{2,1,0:T(8,128)(2,1)} %v_hbm.1, bf16[2,1,128,2560]{3,2,1,0:T(8,128)(2,1)} %collective-permute-done.8.before_hbm, ...), custom_call_target="tpu_custom_call" | custom-call | flops 1509949440 | bytes 11796480 | tf_op jit(solution)/shard_map/attention/pallas_call | solution.py:95
  78.8 3.6 %collective-permute-start.10 = (bf16[160,2560]{1,0:T(8,128)(2,1)}, bf16[160,2560]{1,0:T(8,128)(2,1)S(1)}, u32[]{:S(2)}, u32[]{:S(2)}) collective-permute-start(bf16[160,2560]{1,0:T(8,128)(2,1)} %collective-permute-done.4.refs_2_), channel_id=1, source_target_pairs={{0,4},{1,5},{2,6},{3,7},{4,8},{5,9},{6,10},{7,11},{8,12},{9,13},{1... | collective-permute-start | bytes 2457608 | tf_op jit(solution)/shard_map/ppermute | solution.py:267
  82.4 1.8 %collective-permute-start.11 = (bf16[160,2560]{1,0:T(8,128)(2,1)}, bf16[160,2560]{1,0:T(8,128)(2,1)S(1)}, u32[]{:S(2)}, u32[]{:S(2)}) collective-permute-start(bf16[160,2560]{1,0:T(8,128)(2,1)} %collective-permute-done.5.refs_9_), channel_id=1, source_target_pairs={{0,2},{1,3},{2,0},{3,1},{4,6},{5,7},{6,4},{7,5},{8,10},{9,11},{10,... | collective-permute-start | bytes 2457608 | tf_op jit(solution)/shard_map/ppermute | solution.py:267
  84.2 1.6 %collective-permute-start.12 = (bf16[160,2560]{1,0:T(8,128)(2,1)}, bf16[160,2560]{1,0:T(8,128)(2,1)S(1)}, u32[]{:S(2)}, u32[]{:S(2)}) collective-permute-start(bf16[160,2560]{1,0:T(8,128)(2,1)} %collective-permute-done.6.refs_7_), channel_id=1, source_target_pairs={{0,16},{1,17},{2,18},{3,19},{4,20},{5,21},{6,22},{7,23},{8,24},{9,... | collective-permute-start | bytes 2457608 | tf_op jit(solution)/shard_map/ppermute | solution.py:267
  85.8 15.7 %collective-permute-done.10.refs_4_ = bf16[160,2560]{1,0:T(8,128)(2,1)S(1)} collective-permute-done((bf16[160,2560]{1,0:T(8,128)(2,1)}, bf16[160,2560]{1,0:T(8,128)(2,1)S(1)}, u32[]{:S(2)}, u32[]{:S(2)}) %collective-permute-start.10) | collective-permute-done | bytes 819232 | tf_op jit(solution)/shard_map/ppermute | solution.py:267
  101.5 1.5 %collective-permute-done.11.refs_11_ = bf16[160,2560]{1,0:T(8,128)(2,1)S(1)} collective-permute-done((bf16[160,2560]{1,0:T(8,128)(2,1)}, bf16[160,2560]{1,0:T(8,128)(2,1)S(1)}, u32[]{:S(2)}, u32[]{:S(2)}) %collective-permute-start.11) | collective-permute-done | bytes 819232 | tf_op jit(solution)/shard_map/ppermute | solution.py:267
  103.0 1.5 %collective-permute-done.12.refs_8_ = bf16[160,2560]{1,0:T(8,128)(2,1)S(1)} collective-permute-done((bf16[160,2560]{1,0:T(8,128)(2,1)}, bf16[160,2560]{1,0:T(8,128)(2,1)S(1)}, u32[]{:S(2)}, u32[]{:S(2)}) %collective-permute-start.12) | collective-permute-done | bytes 819232 | tf_op jit(solution)/shard_map/ppermute | solution.py:267
  104.5 2.3 %collective-permute-start.15 = (bf16[160,2560]{1,0:T(8,128)(2,1)}, bf16[160,2560]{1,0:T(8,128)(2,1)S(1)}, u32[]{:S(2)}, u32[]{:S(2)}) collective-permute-start(bf16[160,2560]{1,0:T(8,128)(2,1)} %constant_dynamic-slice_fusion), channel_id=1, source_target_pairs={{0,2},{1,3},{2,0},{3,1},{4,6},{5,7},{6,4},{7,5},{8,10},{9,11},{10,... | collective-permute-start | bytes 2457608 | tf_op jit(solution)/shard_map/ppermute | solution.py:267
  106.8 1.5 %copy-done.1 = bf16[3,128,2560]{2,1,0:T(8,128)(2,1)S(1)} copy-done((bf16[3,128,2560]{2,1,0:T(8,128)(2,1)S(1)}, bf16[3,128,2560]{2,1,0:T(8,128)(2,1)}, u32[]{:S(2)}) %copy-start.1) | copy-done | bytes 1966104
  108.3 14.3 %project.2 = (bf16[384,2176]{1,0:T(8,128)(2,1)S(1)}, bf16[384,2176]{1,0:T(8,128)(2,1)S(1)}) custom-call(s32[1]{0:T(128)} %bitcast.8.group_ref, bf16[384,2560]{1,0:T(8,128)(2,1)S(1)} %bitcast.29, bf16[384,2560]{1,0:T(8,128)(2,1)S(1)} %collective-permute-done.13.sibling_hbm, bf16[320,2560]{1,0:T(8,128)(2,1)S(1)} %bitcast.32, ...), custom_call_target="tpu_custom_call" | custom-call | flops 8178892800 | bytes 17776640 | tf_op jit(solution)/shard_map/project/pallas_call | solution.py:174
  122.7 2.7 %collective-permute-done.14.refs_0_ = bf16[160,2560]{1,0:T(8,128)(2,1)S(1)} collective-permute-done((bf16[160,2560]{1,0:T(8,128)(2,1)S(1)}, bf16[160,2560]{1,0:T(8,128)(2,1)S(1)}, u32[]{:S(2)}, u32[]{:S(2)}) %collective-permute-start.14) | collective-permute-done | bytes 819232 | tf_op jit(solution)/shard_map/ppermute | solution.py:267
  125.9 4.5 %project.3 = (bf16[384,512]{1,0:T(8,128)(2,1)S(1)}, bf16[384,512]{1,0:T(8,128)(2,1)S(1)}) custom-call(s32[1]{0:T(128)} %bitcast.8.group_ref, bf16[384,2560]{1,0:T(8,128)(2,1)S(1)} %bitcast.30, bf16[384,2560]{1,0:T(8,128)(2,1)S(1)} %collective-permute-done.13.sibling_hbm, bf16[160,2560]{1,0:T(8,128)(2,1)S(1)} %collective-permute-done.14.refs_0_, ...), custom_call_target="tpu_custom_call" | custom-call | flops 1887436800 | bytes 7127040 | tf_op jit(solution)/shard_map/project/pallas_call | solution.py:174
  131.0 1.3 collective-permute-done.18.refs_3_
  132.4 5.5 %assemble.1 = bf16[384,5120]{1,0:T(8,128)(2,1)} custom-call(s32[10]{0:T(128)S(1)} %stack.67.scalars, bf16[384,2176]{1,0:T(8,128)(2,1)S(1)} %get-tuple-element.106.refs_0_, bf16[384,2176]{1,0:T(8,128)(2,1)S(1)} %collective-permute-done.17.refs_1_, bf16[384,512]{1,0:T(8,128)(2,1)S(1)} %get-tuple-element.113.refs_2_, ...), custom_call_target="tpu_custom_call" | custom-call | bytes 7864320 | tf_op jit(solution)/shard_map/assemble/pallas_call | solution.py:233
  (30 shorter events, 2.4 us)
Async XLA Ops:
  0.0 10.9 %copy-start = (f32[50,2560]{1,0:T(8,128)S(1)}, f32[50,2560]{1,0:T(8,128)}, u32[]{:S(2)}) copy-start(f32[50,2560]{1,0:T(8,128)} %param.13) | copy-start | bytes 1536004
  2.1 23.5 %collective-permute-start = (bf16[160,2560]{1,0:T(8,128)(2,1)}, bf16[160,2560]{1,0:T(8,128)(2,1)S(1)}, u32[]{:S(2)}, u32[]{:S(2)}) collective-permute-start(bf16[160,2560]{1,0:T(8,128)(2,1)} %dynamic-slice_bitcast_fusion), channel_id=1, source_target_pairs={{0,4},{1,5},{2,6},{3,7},{4,8},{5,9},{6,10},{7,11},{8,12},{9,13},{1... | collective-permute-start | bytes 2457608 | tf_op jit(solution)/shard_map/ppermute | solution.py:267
  5.2 20.5 %collective-permute-start.1 = (bf16[160,2560]{1,0:T(8,128)(2,1)}, bf16[160,2560]{1,0:T(8,128)(2,1)}, u32[]{:S(2)}, u32[]{:S(2)}) collective-permute-start(bf16[160,2560]{1,0:T(8,128)(2,1)} %dynamic-slice_bitcast_fusion), channel_id=1, source_target_pairs={{0,2},{1,3},{2,0},{3,1},{4,6},{5,7},{6,4},{7,5},{8,10},{9,11},{10,... | collective-permute-start | bytes 2457608 | tf_op jit(solution)/shard_map/ppermute | solution.py:267
  8.0 3.5 %copy-start.5 = (s32[3,3]{1,0:T(4,128)S(1)}, s32[3,3]{1,0:T(4,128)}, u32[]{:S(2)}) copy-start(s32[3,3]{1,0:T(4,128)} %param.12) | copy-start | bytes 112
  12.2 1.2 copy-start.3
  12.2 1.8 %copy-start.4 = (bf16[1,1,128,2560]{3,2,1,0:T(8,128)(2,1)S(1)}, bf16[1,1,128,2560]{3,2,1,0:T(8,128)(2,1)}, u32[]{:S(2)}) copy-start(bf16[1,1,128,2560]{3,2,1,0:T(8,128)(2,1)} %get-tuple-element.119) | copy-start | bytes 1966084
  13.4 24.6 %copy-start.2 = (bf16[2560,320]{0,1:T(8,128)(2,1)S(1)}, bf16[2560,320]{0,1:T(8,128)(2,1)}, u32[]{:S(2)}) copy-start(bf16[2560,320]{0,1:T(8,128)(2,1)} %param.15) | copy-start | bytes 4915204
  25.7 21.5 %collective-permute-start.2 = (bf16[160,2560]{1,0:T(8,128)(2,1)S(1)}, bf16[160,2560]{1,0:T(8,128)(2,1)}, u32[]{:S(2)}, u32[]{:S(2)}) collective-permute-start(bf16[160,2560]{1,0:T(8,128)(2,1)S(1)} %collective-permute-done.refs_1_), channel_id=1, source_target_pairs={{0,4},{1,5},{2,6},{3,7},{4,8},{5,9},{6,10},{7,11},{8,12},{9,13},{1... | collective-permute-start | bytes 2457608 | tf_op jit(solution)/shard_map/ppermute | solution.py:267
  26.8 20.4 %collective-permute-start.3 = (bf16[160,2560]{1,0:T(8,128)(2,1)S(1)}, bf16[160,2560]{1,0:T(8,128)(2,1)}, u32[]{:S(2)}, u32[]{:S(2)}) collective-permute-start(bf16[160,2560]{1,0:T(8,128)(2,1)S(1)} %collective-permute-done.refs_1_), channel_id=1, source_target_pairs={{0,2},{1,3},{2,0},{3,1},{4,6},{5,7},{6,4},{7,5},{8,10},{9,11},{10,... | collective-permute-start | bytes 2457608 | tf_op jit(solution)/shard_map/ppermute | solution.py:267
  28.3 18.9 %collective-permute-start.4 = (bf16[160,2560]{1,0:T(8,128)(2,1)S(1)}, bf16[160,2560]{1,0:T(8,128)(2,1)}, u32[]{:S(2)}, u32[]{:S(2)}) collective-permute-start(bf16[160,2560]{1,0:T(8,128)(2,1)S(1)} %collective-permute-done.refs_1_), channel_id=1, source_target_pairs={{0,16},{1,17},{2,18},{3,19},{4,20},{5,21},{6,22},{7,23},{8,24},{9,... | collective-permute-start | bytes 2457608 | tf_op jit(solution)/shard_map/ppermute | solution.py:267
  29.8 33.1 %collective-permute-start.8 = (bf16[2,1,128,2560]{3,2,1,0:T(8,128)(2,1)}, bf16[2,1,128,2560]{3,2,1,0:T(8,128)(2,1)}, u32[]{:S(2)}, u32[]{:S(2)}) collective-permute-start(bf16[2,1,128,2560]{3,2,1,0:T(8,128)(2,1)} %pad_maximum_fusion), channel_id=1, source_target_pairs={{0,1},{2,3},{3,4},{4,5},{6,7},{7,8},{8,9},{10,11},{11,12},{12,13},... | collective-permute-start | bytes 3932168 | tf_op jit(solution)/shard_map/ppermute | solution.py:275
  31.7 34.4 %collective-permute-start.9 = (bf16[2,1,128,2560]{3,2,1,0:T(8,128)(2,1)}, bf16[2,1,128,2560]{3,2,1,0:T(8,128)(2,1)}, u32[]{:S(2)}, u32[]{:S(2)}) collective-permute-start(bf16[2,1,128,2560]{3,2,1,0:T(8,128)(2,1)} %pad_maximum_fusion.1), channel_id=1, source_target_pairs={{0,15},{1,0},{3,2},{4,3},{5,4},{7,6},{8,7},{9,8},{11,10},{12,11},{... | collective-permute-start | bytes 3932168 | tf_op jit(solution)/shard_map/ppermute | solution.py:275
  47.1 31.6 %collective-permute-start.5 = (bf16[160,2560]{1,0:T(8,128)(2,1)}, bf16[160,2560]{1,0:T(8,128)(2,1)}, u32[]{:S(2)}, u32[]{:S(2)}) collective-permute-start(bf16[160,2560]{1,0:T(8,128)(2,1)} %collective-permute-done.2.refs_3_), channel_id=1, source_target_pairs={{0,4},{1,5},{2,6},{3,7},{4,8},{5,9},{6,10},{7,11},{8,12},{9,13},{1... | collective-permute-start | bytes 2457608 | tf_op jit(solution)/shard_map/ppermute | solution.py:267
  61.4 17.4 %collective-permute-start.6 = (bf16[160,2560]{1,0:T(8,128)(2,1)}, bf16[160,2560]{1,0:T(8,128)(2,1)}, u32[]{:S(2)}, u32[]{:S(2)}) collective-permute-start(bf16[160,2560]{1,0:T(8,128)(2,1)} %collective-permute-done.2.refs_3_), channel_id=1, source_target_pairs={{0,2},{1,3},{2,0},{3,1},{4,6},{5,7},{6,4},{7,5},{8,10},{9,11},{10,... | collective-permute-start | bytes 2457608 | tf_op jit(solution)/shard_map/ppermute | solution.py:267
  61.4 17.4 %collective-permute-start.7 = (bf16[160,2560]{1,0:T(8,128)(2,1)}, bf16[160,2560]{1,0:T(8,128)(2,1)}, u32[]{:S(2)}, u32[]{:S(2)}) collective-permute-start(bf16[160,2560]{1,0:T(8,128)(2,1)} %collective-permute-done.3.refs_5_), channel_id=1, source_target_pairs={{0,16},{1,17},{2,18},{3,19},{4,20},{5,21},{6,22},{7,23},{8,24},{9,... | collective-permute-start | bytes 2457608 | tf_op jit(solution)/shard_map/ppermute | solution.py:267
  78.8 25.7 %collective-permute-start.13 = (bf16[384,2560]{1,0:T(8,128)(2,1)}, bf16[384,2560]{1,0:T(8,128)(2,1)S(1)}, u32[]{:S(2)}, u32[]{:S(2)}) collective-permute-start(bf16[384,2560]{1,0:T(8,128)(2,1)} %bitcast.28), channel_id=1, source_target_pairs={{0,1},{1,0},{2,3},{3,2},{4,5},{5,4},{6,7},{7,6},{8,9},{9,8},{10,11... | collective-permute-start | bytes 5898248 | tf_op jit(solution)/shard_map/ppermute | solution.py:267
  78.8 22.7 %collective-permute-start.10 = (bf16[160,2560]{1,0:T(8,128)(2,1)}, bf16[160,2560]{1,0:T(8,128)(2,1)S(1)}, u32[]{:S(2)}, u32[]{:S(2)}) collective-permute-start(bf16[160,2560]{1,0:T(8,128)(2,1)} %collective-permute-done.4.refs_2_), channel_id=1, source_target_pairs={{0,4},{1,5},{2,6},{3,7},{4,8},{5,9},{6,10},{7,11},{8,12},{9,13},{1... | collective-permute-start | bytes 2457608 | tf_op jit(solution)/shard_map/ppermute | solution.py:267
  82.4 20.6 %collective-permute-start.11 = (bf16[160,2560]{1,0:T(8,128)(2,1)}, bf16[160,2560]{1,0:T(8,128)(2,1)S(1)}, u32[]{:S(2)}, u32[]{:S(2)}) collective-permute-start(bf16[160,2560]{1,0:T(8,128)(2,1)} %collective-permute-done.5.refs_9_), channel_id=1, source_target_pairs={{0,2},{1,3},{2,0},{3,1},{4,6},{5,7},{6,4},{7,5},{8,10},{9,11},{10,... | collective-permute-start | bytes 2457608 | tf_op jit(solution)/shard_map/ppermute | solution.py:267
  84.2 20.2 %collective-permute-start.12 = (bf16[160,2560]{1,0:T(8,128)(2,1)}, bf16[160,2560]{1,0:T(8,128)(2,1)S(1)}, u32[]{:S(2)}, u32[]{:S(2)}) collective-permute-start(bf16[160,2560]{1,0:T(8,128)(2,1)} %collective-permute-done.6.refs_7_), channel_id=1, source_target_pairs={{0,16},{1,17},{2,18},{3,19},{4,20},{5,21},{6,22},{7,23},{8,24},{9,... | collective-permute-start | bytes 2457608 | tf_op jit(solution)/shard_map/ppermute | solution.py:267
  104.5 20.9 %collective-permute-start.14 = (bf16[160,2560]{1,0:T(8,128)(2,1)S(1)}, bf16[160,2560]{1,0:T(8,128)(2,1)S(1)}, u32[]{:S(2)}, u32[]{:S(2)}) collective-permute-start(bf16[160,2560]{1,0:T(8,128)(2,1)S(1)} %collective-permute-done.10.refs_4_), channel_id=1, source_target_pairs={{0,4},{1,5},{2,6},{3,7},{4,8},{5,9},{6,10},{7,11},{8,12},{9,13},{1... | collective-permute-start | bytes 2457608 | tf_op jit(solution)/shard_map/ppermute | solution.py:267
  104.5 20.9 %collective-permute-start.15 = (bf16[160,2560]{1,0:T(8,128)(2,1)}, bf16[160,2560]{1,0:T(8,128)(2,1)S(1)}, u32[]{:S(2)}, u32[]{:S(2)}) collective-permute-start(bf16[160,2560]{1,0:T(8,128)(2,1)} %constant_dynamic-slice_fusion), channel_id=1, source_target_pairs={{0,2},{1,3},{2,0},{3,1},{4,6},{5,7},{6,4},{7,5},{8,10},{9,11},{10,... | collective-permute-start | bytes 2457608 | tf_op jit(solution)/shard_map/ppermute | solution.py:267
  106.8 19.1 %collective-permute-start.16 = (bf16[160,2560]{1,0:T(8,128)(2,1)S(1)}, bf16[160,2560]{1,0:T(8,128)(2,1)S(1)}, u32[]{:S(2)}, u32[]{:S(2)}) collective-permute-start(bf16[160,2560]{1,0:T(8,128)(2,1)S(1)} %collective-permute-done.11.refs_11_), channel_id=1, source_target_pairs={{0,16},{1,17},{2,18},{3,19},{4,20},{5,21},{6,22},{7,23},{8,24},{9,... | collective-permute-start | bytes 2457608 | tf_op jit(solution)/shard_map/ppermute | solution.py:267
  106.8 1.5 %copy-start.1 = (bf16[3,128,2560]{2,1,0:T(8,128)(2,1)S(1)}, bf16[3,128,2560]{2,1,0:T(8,128)(2,1)}, u32[]{:S(2)}) copy-start(bf16[3,128,2560]{2,1,0:T(8,128)(2,1)} %attention.1) | copy-start | bytes 5898244
  125.9 6.5 %collective-permute-start.17 = (bf16[384,2176]{1,0:T(8,128)(2,1)S(1)}, bf16[384,2176]{1,0:T(8,128)(2,1)S(1)}, u32[]{:S(2)}, u32[]{:S(2)}) collective-permute-start(bf16[384,2176]{1,0:T(8,128)(2,1)S(1)} %get-tuple-element.107), channel_id=1, source_target_pairs={{0,1},{1,0},{2,3},{3,2},{4,5},{5,4},{6,7},{7,6},{8,9},{9,8},{10,11... | collective-permute-start | bytes 5013512 | tf_op jit(solution)/shard_map/ppermute | solution.py:267
  130.4 1.9 %collective-permute-start.18 = (bf16[384,512]{1,0:T(8,128)(2,1)S(1)}, bf16[384,512]{1,0:T(8,128)(2,1)S(1)}, u32[]{:S(2)}, u32[]{:S(2)}) collective-permute-start(bf16[384,512]{1,0:T(8,128)(2,1)S(1)} %get-tuple-element.114), channel_id=1, source_target_pairs={{0,1},{1,0},{2,3},{3,2},{4,5},{5,4},{6,7},{7,6},{8,9},{9,8},{10,11... | collective-permute-start | bytes 1179656 | tf_op jit(solution)/shard_map/ppermute | solution.py:267

commit v3 on v2

--- a/solution.py
+++ b/solution.py
@@ -347,10 +347,12 @@
             have[("z", "q", 0)] = lax.dynamic_slice_in_dim(small[4], (1 - group) * half, half, 0)
             arrived.append(("z", "q", 0))
         if r == HALO_ROUND + 1:
+            arrived += [("halo", by) for by in (1, -1)]
+        if r == HALO_ROUND + 2:
             halo = [have["halo", by] for by in (1, -1)]
             att = attend(queries, keys, values, halo, small[0], counts, small[1])
             att = att.reshape(slots * rows, channels)
-        elif r == HALO_ROUND + 2:
+        elif r == HALO_ROUND + 3:
             att_sibling = permute(att, over["s"])
         if r == rounds - 1:
             pieces = [[have[n] for n in names_of(b)] for b in whole] + [[have[(b[0], "p", b[1])]] for b in halves]

time: 138 us -> 134 us (0.971)
  waiting for transfers between devices: 45 us -> 42.3 us
  local copies, waits for them, and re-layouts: 9.47 us -> 11.8 us
  Pallas kernels: 37.1 us -> 34.8 us
  starting transfers between devices: 42.6 us -> 40.6 us
    ppermute x17, waiting for transfers between devices: 41.8 us -> 39.1 us  [permute(): return lax.ppermute(array, ('groups', 'dp'), pairs)]
    pallas_call x1, Pallas kernels: 12.7 us -> 10.6 us  [attend(): pl.pallas_call(functools.partial(attention_kernel, first), out_shape=jax....]
    ppermute x17, starting transfers between devices: 34.3 us -> 32.3 us  [permute(): return lax.ppermute(array, ('groups', 'dp'), pairs)]
    unnamed x12 -> x16, local copies, waits for them, and re-layouts: 2.13 us -> 4.12 us
  transfers between devices with their start and end apart: 19 -> 19, of which waited for: 9 -> 8; matrix products, arithmetic and copies ran while one was open for 5% -> 6% of each run, Pallas kernels for 23% -> 22%
where the time goes in v3:
time: 134 us; the launch traced here: 133 us
  waiting for transfers between devices  42.3 us (32%)
  starting transfers between devices  40.6 us (30%)
  Pallas kernels  34.8 us (26%)
  local copies, waits for them, and re-layouts  11.8 us (9%)
  other arithmetic  2.38 us (2%)
  between operations  1.57 us (1%)
    ppermute x17, waiting for transfers between devices, permute(): return lax.ppermute(array, ('groups', 'dp'), pairs)  39.1 us
    ppermute x17, starting transfers between devices, permute(): return lax.ppermute(array, ('groups', 'dp'), pairs)  32.3 us
    pallas_call x2, Pallas kernels, project(): pl.pallas_call(functools.partial(project_kernel, tuple((len(b) for b in b...  18.7 us
    pallas_call x1, Pallas kernels, attend(): pl.pallas_call(functools.partial(attention_kernel, first), out_shape=jax....  10.6 us
    ppermute x2, starting transfers between devices, within_member(): return lax.ppermute(array, 'dp', pairs)  8.25 us
    pallas_call x1, Pallas kernels, assemble(): pl.pallas_call(functools.partial(assemble_kernel, places, shard), out_sha...  5.55 us
    unnamed x16, local copies, waits for them, and re-layouts  4.12 us
    ppermute x2, waiting for transfers between devices, within_member(): return lax.ppermute(array, 'dp', pairs)  3.17 us
  transfers between devices with their start and end apart: 19, of which 8 were waited for; matrix products, arithmetic and copies ran while one was open for 6% of the time, Pallas kernels for 22%

profile of v3, /device:TPU:0, one launch (start us, length us, event | category | flops | bytes accessed | tf_op | source)
XLA Modules:
  0.0 133.4 jit_solution(14902042423151282821)
XLA Ops:
  0.0 2.2 %dynamic-slice_bitcast_fusion = bf16[160,2560]{1,0:T(8,128)(2,1)} fusion(bf16[2560,320]{0,1:T(8,128)(2,1)} %param.15, s32[]{:T(128)S(6)} %select_n.63), kind=kLoop, calls=%fused_computation.2 | loop fusion | bytes 1638404 | tf_op jit(solution)/shard_map/dynamic_slice | solution.py:304
  2.2 3.0 %collective-permute-start = (bf16[160,2560]{1,0:T(8,128)(2,1)}, bf16[160,2560]{1,0:T(8,128)(2,1)S(1)}, u32[]{:S(2)}, u32[]{:S(2)}) collective-permute-start(bf16[160,2560]{1,0:T(8,128)(2,1)} %dynamic-slice_bitcast_fusion), channel_id=1, source_target_pairs={{0,4},{1,5},{2,6},{3,7},{4,8},{5,9},{6,10},{7,11},{8,12},{9,13},{1... | collective-permute-start | bytes 2457608 | tf_op jit(solution)/shard_map/ppermute | solution.py:267
  5.2 1.5 %collective-permute-start.1 = (bf16[160,2560]{1,0:T(8,128)(2,1)}, bf16[160,2560]{1,0:T(8,128)(2,1)}, u32[]{:S(2)}, u32[]{:S(2)}) collective-permute-start(bf16[160,2560]{1,0:T(8,128)(2,1)} %dynamic-slice_bitcast_fusion), channel_id=1, source_target_pairs={{0,2},{1,3},{2,0},{3,1},{4,6},{5,7},{6,4},{7,5},{8,10},{9,11},{10,... | collective-permute-start | bytes 2457608 | tf_op jit(solution)/shard_map/ppermute | solution.py:267
  8.0 3.2 %slice_bitcast_fusion = (bf16[1,1,128,2560]{3,2,1,0:T(8,128)(2,1)S(1)}, bf16[1,1,128,2560]{3,2,1,0:T(8,128)(2,1)}, bf16[1,1,128,2560]{3,2,1,0:T(8,128)(2,1)}, bf16[1,1,128,2560]{3,2,1,0:T(8,128)(2,1)S(1)}) fusion(bf16[3,128,2560]{2,1,0:T(8,128)(2,1)} %v_hbm.1, s32[]{:T(128)} %bitcast.1, bf16[3,128,2560]{2,1,0:T(8,128)(2,1)} %k_hbm.1), kind=kLoop, calls=%fused_computation.3 | loop fusion | bytes 5242884 | tf_op jit(solution)/shard_map/stack | solution.py:333
  12.5 1.2 pad_maximum_fusion.1
  14.3 1.2 pad_maximum_fusion
  15.5 10.2 %collective-permute-done.refs_1_ = bf16[160,2560]{1,0:T(8,128)(2,1)S(1)} collective-permute-done((bf16[160,2560]{1,0:T(8,128)(2,1)}, bf16[160,2560]{1,0:T(8,128)(2,1)S(1)}, u32[]{:S(2)}, u32[]{:S(2)}) %collective-permute-start) | collective-permute-done | bytes 819232 | tf_op jit(solution)/shard_map/ppermute | solution.py:267
  25.7 1.1 collective-permute-start.2
  26.8 1.5 %collective-permute-start.3 = (bf16[160,2560]{1,0:T(8,128)(2,1)S(1)}, bf16[160,2560]{1,0:T(8,128)(2,1)}, u32[]{:S(2)}, u32[]{:S(2)}) collective-permute-start(bf16[160,2560]{1,0:T(8,128)(2,1)S(1)} %collective-permute-done.refs_1_), channel_id=1, source_target_pairs={{0,2},{1,3},{2,0},{3,1},{4,6},{5,7},{6,4},{7,5},{8,10},{9,11},{10,... | collective-permute-start | bytes 2457608 | tf_op jit(solution)/shard_map/ppermute | solution.py:267
  28.3 1.5 %collective-permute-start.4 = (bf16[160,2560]{1,0:T(8,128)(2,1)S(1)}, bf16[160,2560]{1,0:T(8,128)(2,1)}, u32[]{:S(2)}, u32[]{:S(2)}) collective-permute-start(bf16[160,2560]{1,0:T(8,128)(2,1)S(1)} %collective-permute-done.refs_1_), channel_id=1, source_target_pairs={{0,16},{1,17},{2,18},{3,19},{4,20},{5,21},{6,22},{7,23},{8,24},{9,... | collective-permute-start | bytes 2457608 | tf_op jit(solution)/shard_map/ppermute | solution.py:267
  29.8 1.9 %collective-permute-start.8 = (bf16[2,1,128,2560]{3,2,1,0:T(8,128)(2,1)}, bf16[2,1,128,2560]{3,2,1,0:T(8,128)(2,1)}, u32[]{:S(2)}, u32[]{:S(2)}) collective-permute-start(bf16[2,1,128,2560]{3,2,1,0:T(8,128)(2,1)} %pad_maximum_fusion), channel_id=1, source_target_pairs={{0,1},{2,3},{3,4},{4,5},{6,7},{7,8},{8,9},{10,11},{11,12},{12,13},... | collective-permute-start | bytes 3932168 | tf_op jit(solution)/shard_map/ppermute | solution.py:275
  31.7 6.3 %collective-permute-start.9 = (bf16[2,1,128,2560]{3,2,1,0:T(8,128)(2,1)}, bf16[2,1,128,2560]{3,2,1,0:T(8,128)(2,1)}, u32[]{:S(2)}, u32[]{:S(2)}) collective-permute-start(bf16[2,1,128,2560]{3,2,1,0:T(8,128)(2,1)} %pad_maximum_fusion.1), channel_id=1, source_target_pairs={{0,15},{1,0},{3,2},{4,3},{5,4},{7,6},{8,7},{9,8},{11,10},{12,11},{... | collective-permute-start | bytes 3932168 | tf_op jit(solution)/shard_map/ppermute | solution.py:275
  38.1 1.0 constant_dynamic-slice_fusion
  39.1 8.1 %collective-permute-done.2.refs_3_ = bf16[160,2560]{1,0:T(8,128)(2,1)} collective-permute-done((bf16[160,2560]{1,0:T(8,128)(2,1)S(1)}, bf16[160,2560]{1,0:T(8,128)(2,1)}, u32[]{:S(2)}, u32[]{:S(2)}) %collective-permute-start.2) | collective-permute-done | bytes 819232 | tf_op jit(solution)/shard_map/ppermute | solution.py:267
  47.2 14.2 %collective-permute-start.5 = (bf16[160,2560]{1,0:T(8,128)(2,1)}, bf16[160,2560]{1,0:T(8,128)(2,1)}, u32[]{:S(2)}, u32[]{:S(2)}) collective-permute-start(bf16[160,2560]{1,0:T(8,128)(2,1)} %collective-permute-done.2.refs_3_), channel_id=1, source_target_pairs={{0,4},{1,5},{2,6},{3,7},{4,8},{5,9},{6,10},{7,11},{8,12},{9,13},{1... | collective-permute-start | bytes 2457608 | tf_op jit(solution)/shard_map/ppermute | solution.py:267
  61.4 1.5 %collective-permute-start.7 = (bf16[160,2560]{1,0:T(8,128)(2,1)}, bf16[160,2560]{1,0:T(8,128)(2,1)S(1)}, u32[]{:S(2)}, u32[]{:S(2)}) collective-permute-start(bf16[160,2560]{1,0:T(8,128)(2,1)} %collective-permute-done.3.refs_5_), channel_id=1, source_target_pairs={{0,16},{1,17},{2,18},{3,19},{4,20},{5,21},{6,22},{7,23},{8,24},{9,... | collective-permute-start | bytes 2457608 | tf_op jit(solution)/shard_map/ppermute | solution.py:267
  62.9 3.2 %collective-permute-done.9.after_hbm = bf16[2,1,128,2560]{3,2,1,0:T(8,128)(2,1)} collective-permute-done((bf16[2,1,128,2560]{3,2,1,0:T(8,128)(2,1)}, bf16[2,1,128,2560]{3,2,1,0:T(8,128)(2,1)}, u32[]{:S(2)}, u32[]{:S(2)}) %collective-permute-start.9) | collective-permute-done | bytes 1310752 | tf_op jit(solution)/shard_map/ppermute | solution.py:275
  66.1 12.6 %collective-permute-done.5.refs_9_ = bf16[160,2560]{1,0:T(8,128)(2,1)} collective-permute-done((bf16[160,2560]{1,0:T(8,128)(2,1)}, bf16[160,2560]{1,0:T(8,128)(2,1)}, u32[]{:S(2)}, u32[]{:S(2)}) %collective-permute-start.5) | collective-permute-done | bytes 819232 | tf_op jit(solution)/shard_map/ppermute | solution.py:267
  79.6 1.9 %collective-permute-start.11 = (bf16[160,2560]{1,0:T(8,128)(2,1)}, bf16[160,2560]{1,0:T(8,128)(2,1)}, u32[]{:S(2)}, u32[]{:S(2)}) collective-permute-start(bf16[160,2560]{1,0:T(8,128)(2,1)} %collective-permute-done.5.refs_9_), channel_id=1, source_target_pairs={{0,2},{1,3},{2,0},{3,1},{4,6},{5,7},{6,4},{7,5},{8,10},{9,11},{10,... | collective-permute-start | bytes 2457608 | tf_op jit(solution)/shard_map/ppermute | solution.py:267
  81.5 1.3 collective-permute-start.12
  82.8 10.6 %attention.1 = bf16[3,128,2560]{2,1,0:T(8,128)(2,1)} custom-call(s32[9]{0:T(128)} %reshape.14.index_ref, s32[1]{0:T(128)S(6)} %copy.9.count_ref, bf16[3,128,2560]{2,1,0:T(8,128)(2,1)} %q_hbm.1, bf16[3,128,2560]{2,1,0:T(8,128)(2,1)} %k_hbm.1, bf16[3,128,2560]{2,1,0:T(8,128)(2,1)} %v_hbm.1, bf16[2,1,128,2560]{3,2,1,0:T(8,128)(2,1)} %collective-permute-done.8.before_hbm, ...), custom_call_target="tpu_custom_call" | custom-call | flops 1509949440 | bytes 11796480 | tf_op jit(solution)/shard_map/attention/pallas_call | solution.py:95
  93.4 4.3 %collective-permute-done.10.refs_4_ = bf16[160,2560]{1,0:T(8,128)(2,1)} collective-permute-done((bf16[160,2560]{1,0:T(8,128)(2,1)}, bf16[160,2560]{1,0:T(8,128)(2,1)}, u32[]{:S(2)}, u32[]{:S(2)}) %collective-permute-start.10) | collective-permute-done | bytes 819232 | tf_op jit(solution)/shard_map/ppermute | solution.py:267
  98.5 1.0 collective-permute-start.13
  99.5 1.1 collective-permute-start.14
  100.7 2.0 %collective-permute-start.15 = (bf16[160,2560]{1,0:T(8,128)(2,1)}, bf16[160,2560]{1,0:T(8,128)(2,1)S(1)}, u32[]{:S(2)}, u32[]{:S(2)}) collective-permute-start(bf16[160,2560]{1,0:T(8,128)(2,1)} %collective-permute-done.11.refs_11_), channel_id=1, source_target_pairs={{0,16},{1,17},{2,18},{3,19},{4,20},{5,21},{6,22},{7,23},{8,24},{9,... | collective-permute-start | bytes 2457608 | tf_op jit(solution)/shard_map/ppermute | solution.py:267
  102.7 1.5 %copy-done.1 = bf16[3,128,2560]{2,1,0:T(8,128)(2,1)S(1)} copy-done((bf16[3,128,2560]{2,1,0:T(8,128)(2,1)S(1)}, bf16[3,128,2560]{2,1,0:T(8,128)(2,1)}, u32[]{:S(2)}) %copy-start.1) | copy-done | bytes 1966104
  104.3 1.1 copy-done.4
  105.4 14.1 %project.2 = (bf16[384,2176]{1,0:T(8,128)(2,1)S(1)}, bf16[384,2176]{1,0:T(8,128)(2,1)S(1)}) custom-call(s32[1]{0:T(128)} %bitcast.8.group_ref, bf16[384,2560]{1,0:T(8,128)(2,1)S(1)} %bitcast.29, bf16[384,2560]{1,0:T(8,128)(2,1)S(1)} %collective-permute-done.16.sibling_hbm, bf16[320,2560]{1,0:T(8,128)(2,1)S(1)} %bitcast.32, ...), custom_call_target="tpu_custom_call" | custom-call | flops 8178892800 | bytes 17776640 | tf_op jit(solution)/shard_map/project/pallas_call | solution.py:174
  119.6 1.6 %collective-permute-done.13.refs_0_ = bf16[160,2560]{1,0:T(8,128)(2,1)S(1)} collective-permute-done((bf16[160,2560]{1,0:T(8,128)(2,1)}, bf16[160,2560]{1,0:T(8,128)(2,1)S(1)}, u32[]{:S(2)}, u32[]{:S(2)}) %collective-permute-start.13) | collective-permute-done | bytes 819232 | tf_op jit(solution)/shard_map/ppermute | solution.py:267
  121.2 4.5 %project.3 = (bf16[384,512]{1,0:T(8,128)(2,1)S(1)}, bf16[384,512]{1,0:T(8,128)(2,1)S(1)}) custom-call(s32[1]{0:T(128)} %bitcast.8.group_ref, bf16[384,2560]{1,0:T(8,128)(2,1)S(1)} %bitcast.30, bf16[384,2560]{1,0:T(8,128)(2,1)S(1)} %collective-permute-done.16.sibling_hbm, bf16[160,2560]{1,0:T(8,128)(2,1)S(1)} %collective-permute-done.13.refs_0_, ...), custom_call_target="tpu_custom_call" | custom-call | flops 1887436800 | bytes 7127040 | tf_op jit(solution)/shard_map/project/pallas_call | solution.py:174
  126.3 1.3 %collective-permute-done.18.refs_3_ = bf16[384,512]{1,0:T(8,128)(2,1)S(1)} collective-permute-done((bf16[384,512]{1,0:T(8,128)(2,1)S(1)}, bf16[384,512]{1,0:T(8,128)(2,1)S(1)}, u32[]{:S(2)}, u32[]{:S(2)}) %collective-permute-start.18) | collective-permute-done | bytes 393248 | tf_op jit(solution)/shard_map/ppermute | solution.py:267
  127.7 5.5 %assemble.1 = bf16[384,5120]{1,0:T(8,128)(2,1)} custom-call(s32[10]{0:T(128)S(1)} %stack.67.scalars, bf16[384,2176]{1,0:T(8,128)(2,1)S(1)} %get-tuple-element.110.refs_0_, bf16[384,2176]{1,0:T(8,128)(2,1)S(1)} %collective-permute-done.17.refs_1_, bf16[384,512]{1,0:T(8,128)(2,1)S(1)} %get-tuple-element.117.refs_2_, ...), custom_call_target="tpu_custom_call" | custom-call | bytes 7864320 | tf_op jit(solution)/shard_map/assemble/pallas_call | solution.py:233
  (34 shorter events, 4.3 us)
Async XLA Ops:
  0.0 11.2 %copy-start = (f32[50,2560]{1,0:T(8,128)S(1)}, f32[50,2560]{1,0:T(8,128)}, u32[]{:S(2)}) copy-start(f32[50,2560]{1,0:T(8,128)} %param.13) | copy-start | bytes 1536004
  2.2 23.5 %collective-permute-start = (bf16[160,2560]{1,0:T(8,128)(2,1)}, bf16[160,2560]{1,0:T(8,128)(2,1)S(1)}, u32[]{:S(2)}, u32[]{:S(2)}) collective-permute-start(bf16[160,2560]{1,0:T(8,128)(2,1)} %dynamic-slice_bitcast_fusion), channel_id=1, source_target_pairs={{0,4},{1,5},{2,6},{3,7},{4,8},{5,9},{6,10},{7,11},{8,12},{9,13},{1... | collective-permute-start | bytes 2457608 | tf_op jit(solution)/shard_map/ppermute | solution.py:267
  5.2 20.5 %collective-permute-start.1 = (bf16[160,2560]{1,0:T(8,128)(2,1)}, bf16[160,2560]{1,0:T(8,128)(2,1)}, u32[]{:S(2)}, u32[]{:S(2)}) collective-permute-start(bf16[160,2560]{1,0:T(8,128)(2,1)} %dynamic-slice_bitcast_fusion), channel_id=1, source_target_pairs={{0,2},{1,3},{2,0},{3,1},{4,6},{5,7},{6,4},{7,5},{8,10},{9,11},{10,... | collective-permute-start | bytes 2457608 | tf_op jit(solution)/shard_map/ppermute | solution.py:267
  8.0 3.8 %copy-start.7 = (s32[3,3]{1,0:T(4,128)S(1)}, s32[3,3]{1,0:T(4,128)}, u32[]{:S(2)}) copy-start(s32[3,3]{1,0:T(4,128)} %param.12) | copy-start | bytes 112
  12.5 1.2 copy-start.5
  12.5 1.8 %copy-start.6 = (bf16[1,1,128,2560]{3,2,1,0:T(8,128)(2,1)S(1)}, bf16[1,1,128,2560]{3,2,1,0:T(8,128)(2,1)}, u32[]{:S(2)}) copy-start(bf16[1,1,128,2560]{3,2,1,0:T(8,128)(2,1)} %get-tuple-element.123) | copy-start | bytes 1966084
  13.8 24.3 %copy-start.2 = (bf16[2560,320]{0,1:T(8,128)(2,1)S(1)}, bf16[2560,320]{0,1:T(8,128)(2,1)}, u32[]{:S(2)}) copy-start(bf16[2560,320]{0,1:T(8,128)(2,1)} %param.15) | copy-start | bytes 4915204
  25.7 21.5 %collective-permute-start.2 = (bf16[160,2560]{1,0:T(8,128)(2,1)S(1)}, bf16[160,2560]{1,0:T(8,128)(2,1)}, u32[]{:S(2)}, u32[]{:S(2)}) collective-permute-start(bf16[160,2560]{1,0:T(8,128)(2,1)S(1)} %collective-permute-done.refs_1_), channel_id=1, source_target_pairs={{0,4},{1,5},{2,6},{3,7},{4,8},{5,9},{6,10},{7,11},{8,12},{9,13},{1... | collective-permute-start | bytes 2457608 | tf_op jit(solution)/shard_map/ppermute | solution.py:267
  26.8 20.4 %collective-permute-start.3 = (bf16[160,2560]{1,0:T(8,128)(2,1)S(1)}, bf16[160,2560]{1,0:T(8,128)(2,1)}, u32[]{:S(2)}, u32[]{:S(2)}) collective-permute-start(bf16[160,2560]{1,0:T(8,128)(2,1)S(1)} %collective-permute-done.refs_1_), channel_id=1, source_target_pairs={{0,2},{1,3},{2,0},{3,1},{4,6},{5,7},{6,4},{7,5},{8,10},{9,11},{10,... | collective-permute-start | bytes 2457608 | tf_op jit(solution)/shard_map/ppermute | solution.py:267
  28.3 18.9 %collective-permute-start.4 = (bf16[160,2560]{1,0:T(8,128)(2,1)S(1)}, bf16[160,2560]{1,0:T(8,128)(2,1)}, u32[]{:S(2)}, u32[]{:S(2)}) collective-permute-start(bf16[160,2560]{1,0:T(8,128)(2,1)S(1)} %collective-permute-done.refs_1_), channel_id=1, source_target_pairs={{0,16},{1,17},{2,18},{3,19},{4,20},{5,21},{6,22},{7,23},{8,24},{9,... | collective-permute-start | bytes 2457608 | tf_op jit(solution)/shard_map/ppermute | solution.py:267
  29.8 33.1 %collective-permute-start.8 = (bf16[2,1,128,2560]{3,2,1,0:T(8,128)(2,1)}, bf16[2,1,128,2560]{3,2,1,0:T(8,128)(2,1)}, u32[]{:S(2)}, u32[]{:S(2)}) collective-permute-start(bf16[2,1,128,2560]{3,2,1,0:T(8,128)(2,1)} %pad_maximum_fusion), channel_id=1, source_target_pairs={{0,1},{2,3},{3,4},{4,5},{6,7},{7,8},{8,9},{10,11},{11,12},{12,13},... | collective-permute-start | bytes 3932168 | tf_op jit(solution)/shard_map/ppermute | solution.py:275
  31.7 34.4 %collective-permute-start.9 = (bf16[2,1,128,2560]{3,2,1,0:T(8,128)(2,1)}, bf16[2,1,128,2560]{3,2,1,0:T(8,128)(2,1)}, u32[]{:S(2)}, u32[]{:S(2)}) collective-permute-start(bf16[2,1,128,2560]{3,2,1,0:T(8,128)(2,1)} %pad_maximum_fusion.1), channel_id=1, source_target_pairs={{0,15},{1,0},{3,2},{4,3},{5,4},{7,6},{8,7},{9,8},{11,10},{12,11},{... | collective-permute-start | bytes 3932168 | tf_op jit(solution)/shard_map/ppermute | solution.py:275
  47.2 31.5 %collective-permute-start.5 = (bf16[160,2560]{1,0:T(8,128)(2,1)}, bf16[160,2560]{1,0:T(8,128)(2,1)}, u32[]{:S(2)}, u32[]{:S(2)}) collective-permute-start(bf16[160,2560]{1,0:T(8,128)(2,1)} %collective-permute-done.2.refs_3_), channel_id=1, source_target_pairs={{0,4},{1,5},{2,6},{3,7},{4,8},{5,9},{6,10},{7,11},{8,12},{9,13},{1... | collective-permute-start | bytes 2457608 | tf_op jit(solution)/shard_map/ppermute | solution.py:267
  61.4 17.3 %collective-permute-start.6 = (bf16[160,2560]{1,0:T(8,128)(2,1)}, bf16[160,2560]{1,0:T(8,128)(2,1)}, u32[]{:S(2)}, u32[]{:S(2)}) collective-permute-start(bf16[160,2560]{1,0:T(8,128)(2,1)} %collective-permute-done.2.refs_3_), channel_id=1, source_target_pairs={{0,2},{1,3},{2,0},{3,1},{4,6},{5,7},{6,4},{7,5},{8,10},{9,11},{10,... | collective-permute-start | bytes 2457608 | tf_op jit(solution)/shard_map/ppermute | solution.py:267
  61.4 17.3 %collective-permute-start.7 = (bf16[160,2560]{1,0:T(8,128)(2,1)}, bf16[160,2560]{1,0:T(8,128)(2,1)S(1)}, u32[]{:S(2)}, u32[]{:S(2)}) collective-permute-start(bf16[160,2560]{1,0:T(8,128)(2,1)} %collective-permute-done.3.refs_5_), channel_id=1, source_target_pairs={{0,16},{1,17},{2,18},{3,19},{4,20},{5,21},{6,22},{7,23},{8,24},{9,... | collective-permute-start | bytes 2457608 | tf_op jit(solution)/shard_map/ppermute | solution.py:267
  78.7 0.9 copy-start.3
  79.6 18.1 %collective-permute-start.10 = (bf16[160,2560]{1,0:T(8,128)(2,1)}, bf16[160,2560]{1,0:T(8,128)(2,1)}, u32[]{:S(2)}, u32[]{:S(2)}) collective-permute-start(bf16[160,2560]{1,0:T(8,128)(2,1)} %collective-permute-done.4.refs_2_), channel_id=1, source_target_pairs={{0,4},{1,5},{2,6},{3,7},{4,8},{5,9},{6,10},{7,11},{8,12},{9,13},{1... | collective-permute-start | bytes 2457608 | tf_op jit(solution)/shard_map/ppermute | solution.py:267
  79.6 18.1 %collective-permute-start.11 = (bf16[160,2560]{1,0:T(8,128)(2,1)}, bf16[160,2560]{1,0:T(8,128)(2,1)}, u32[]{:S(2)}, u32[]{:S(2)}) collective-permute-start(bf16[160,2560]{1,0:T(8,128)(2,1)} %collective-permute-done.5.refs_9_), channel_id=1, source_target_pairs={{0,2},{1,3},{2,0},{3,1},{4,6},{5,7},{6,4},{7,5},{8,10},{9,11},{10,... | collective-permute-start | bytes 2457608 | tf_op jit(solution)/shard_map/ppermute | solution.py:267
  81.5 17.0 %collective-permute-start.12 = (bf16[160,2560]{1,0:T(8,128)(2,1)}, bf16[160,2560]{1,0:T(8,128)(2,1)}, u32[]{:S(2)}, u32[]{:S(2)}) collective-permute-start(bf16[160,2560]{1,0:T(8,128)(2,1)} %collective-permute-done.6.refs_7_), channel_id=1, source_target_pairs={{0,16},{1,17},{2,18},{3,19},{4,20},{5,21},{6,22},{7,23},{8,24},{9,... | collective-permute-start | bytes 2457608 | tf_op jit(solution)/shard_map/ppermute | solution.py:267
  98.5 4.2 %collective-permute-start.16 = (bf16[384,2560]{1,0:T(8,128)(2,1)}, bf16[384,2560]{1,0:T(8,128)(2,1)S(1)}, u32[]{:S(2)}, u32[]{:S(2)}) collective-permute-start(bf16[384,2560]{1,0:T(8,128)(2,1)} %bitcast.28), channel_id=1, source_target_pairs={{0,1},{1,0},{2,3},{3,2},{4,5},{5,4},{6,7},{7,6},{8,9},{9,8},{10,11... | collective-permute-start | bytes 5898248 | tf_op jit(solution)/shard_map/ppermute | solution.py:267
  98.5 22.7 %collective-permute-start.13 = (bf16[160,2560]{1,0:T(8,128)(2,1)}, bf16[160,2560]{1,0:T(8,128)(2,1)S(1)}, u32[]{:S(2)}, u32[]{:S(2)}) collective-permute-start(bf16[160,2560]{1,0:T(8,128)(2,1)} %collective-permute-done.10.refs_4_), channel_id=1, source_target_pairs={{0,4},{1,5},{2,6},{3,7},{4,8},{5,9},{6,10},{7,11},{8,12},{9,13},{1... | collective-permute-start | bytes 2457608 | tf_op jit(solution)/shard_map/ppermute | solution.py:267
  99.5 21.7 %collective-permute-start.14 = (bf16[160,2560]{1,0:T(8,128)(2,1)}, bf16[160,2560]{1,0:T(8,128)(2,1)S(1)}, u32[]{:S(2)}, u32[]{:S(2)}) collective-permute-start(bf16[160,2560]{1,0:T(8,128)(2,1)} %constant_dynamic-slice_fusion), channel_id=1, source_target_pairs={{0,2},{1,3},{2,0},{3,1},{4,6},{5,7},{6,4},{7,5},{8,10},{9,11},{10,... | collective-permute-start | bytes 2457608 | tf_op jit(solution)/shard_map/ppermute | solution.py:267
  100.7 20.5 %collective-permute-start.15 = (bf16[160,2560]{1,0:T(8,128)(2,1)}, bf16[160,2560]{1,0:T(8,128)(2,1)S(1)}, u32[]{:S(2)}, u32[]{:S(2)}) collective-permute-start(bf16[160,2560]{1,0:T(8,128)(2,1)} %collective-permute-done.11.refs_11_), channel_id=1, source_target_pairs={{0,16},{1,17},{2,18},{3,19},{4,20},{5,21},{6,22},{7,23},{8,24},{9,... | collective-permute-start | bytes 2457608 | tf_op jit(solution)/shard_map/ppermute | solution.py:267
  102.7 1.5 %copy-start.1 = (bf16[3,128,2560]{2,1,0:T(8,128)(2,1)S(1)}, bf16[3,128,2560]{2,1,0:T(8,128)(2,1)}, u32[]{:S(2)}) copy-start(bf16[3,128,2560]{2,1,0:T(8,128)(2,1)} %attention.1) | copy-start | bytes 5898244
  104.3 1.1 copy-start.4
  121.2 6.5 %collective-permute-start.17 = (bf16[384,2176]{1,0:T(8,128)(2,1)S(1)}, bf16[384,2176]{1,0:T(8,128)(2,1)S(1)}, u32[]{:S(2)}, u32[]{:S(2)}) collective-permute-start(bf16[384,2176]{1,0:T(8,128)(2,1)S(1)} %get-tuple-element.111), channel_id=1, source_target_pairs={{0,1},{1,0},{2,3},{3,2},{4,5},{5,4},{6,7},{7,6},{8,9},{9,8},{10,11... | collective-permute-start | bytes 5013512 | tf_op jit(solution)/shard_map/ppermute | solution.py:267
  125.8 1.9 %collective-permute-start.18 = (bf16[384,512]{1,0:T(8,128)(2,1)S(1)}, bf16[384,512]{1,0:T(8,128)(2,1)S(1)}, u32[]{:S(2)}, u32[]{:S(2)}) collective-permute-start(bf16[384,512]{1,0:T(8,128)(2,1)S(1)} %get-tuple-element.118), channel_id=1, source_target_pairs={{0,1},{1,0},{2,3},{3,2},{4,5},{5,4},{6,7},{7,6},{8,9},{9,8},{10,11... | collective-permute-start | bytes 1179656 | tf_op jit(solution)/shard_map/ppermute | solution.py:267

commit v4 on v3

--- a/solution.py
+++ b/solution.py
@@ -199,8 +199,6 @@
 def assemble_kernel(places, shard, scalars, *refs):
     arrays, (out_ref, buf, sem) = refs[:-3], refs[-3:]
     half = shard // 2
-    high = buf.shape[1]
-    rows = pl.ds(pl.multiple_of(pl.program_id(0) * high, high), high)
     stores = []
     for b, parts in enumerate(places):
 
@@ -220,7 +218,7 @@
                 for g in range(2):
                     pl.when((scalars[0] == c) & (scalars[1] == g))(functools.partial(place, c, g))
         where = pl.ds(pl.multiple_of(scalars[2 + b] * CORES * shard, CORES * shard), CORES * shard)
-        store = pltpu.make_async_copy(buf.at[b], out_ref.at[rows, where], sem.at[b])
+        store = pltpu.make_async_copy(buf.at[b], out_ref.at[:, where], sem.at[b])
         store.start()
         stores.append(store)
     for store in stores:
@@ -229,17 +227,16 @@
 
 def assemble(arrays, places, scalars, shard, columns):
     rows = arrays[0].shape[0]
-    chunk = 128 if rows % 128 == 0 else rows
     return pl.pallas_call(
         functools.partial(assemble_kernel, places, shard),
         out_shape=jax.ShapeDtypeStruct((rows, columns), jnp.bfloat16),
         grid_spec=pltpu.PrefetchScalarGridSpec(
             num_scalar_prefetch=1,
-            grid=(rows // chunk,),
-            in_specs=[pl.BlockSpec((chunk, a.shape[1]), lambda i, *_: (i, 0)) for a in arrays],
+            grid=(1,),
+            in_specs=[pl.BlockSpec(a.shape, lambda i, *_: (0, 0)) for a in arrays],
             out_specs=pl.BlockSpec(memory_space=pltpu.HBM),
             scratch_shapes=[
-                pltpu.VMEM((len(places), chunk, CORES * shard), jnp.bfloat16),
+                pltpu.VMEM((len(places), rows, CORES * shard), jnp.bfloat16),
                 pltpu.SemaphoreType.DMA((len(places),)),
             ],
         ),

time: 134 us -> 132 us (0.985)
  waiting for transfers between devices: 42.3 us -> 40.6 us
    pallas_call x1, Pallas kernels: 5.55 us -> 3.19 us  [assemble(): pl.pallas_call(functools.partial(assemble_kernel, places, shard), out_sha...]
    pallas_call x1, Pallas kernels: 10.6 us -> 12.7 us  [attend(): pl.pallas_call(functools.partial(attention_kernel, first), out_shape=jax....]
    ppermute x17, waiting for transfers between devices: 39.1 us -> 37.4 us  [permute(): return lax.ppermute(array, ('groups', 'dp'), pairs)]
  transfers between devices with their start and end apart: 19 -> 19, of which waited for: 8 -> 9; matrix products, arithmetic and copies ran while one was open for 6% -> 6% of each run, Pallas kernels for 22% -> 24%
where the time goes in v4:
time: 132 us; the launch traced here: 131 us
  waiting for transfers between devices  40.6 us (31%)
  starting transfers between devices  40.4 us (31%)
  Pallas kernels  34.5 us (26%)
  local copies, waits for them, and re-layouts  11.6 us (9%)
  other arithmetic  2.38 us (2%)
  between operations  1.57 us (1%)
    ppermute x17, waiting for transfers between devices, permute(): return lax.ppermute(array, ('groups', 'dp'), pairs)  37.4 us
    ppermute x17, starting transfers between devices, permute(): return lax.ppermute(array, ('groups', 'dp'), pairs)  32.2 us
    pallas_call x2, Pallas kernels, project(): pl.pallas_call(functools.partial(project_kernel, tuple((len(b) for b in b...  18.7 us
    pallas_call x1, Pallas kernels, attend(): pl.pallas_call(functools.partial(attention_kernel, first), out_shape=jax....  12.7 us
    ppermute x2, starting transfers between devices, within_member(): return lax.ppermute(array, 'dp', pairs)  8.25 us
    unnamed x16, local copies, waits for them, and re-layouts  4.12 us
    pallas_call x1, Pallas kernels, assemble(): pl.pallas_call(functools.partial(assemble_kernel, places, shard), out_sha...  3.19 us
    ppermute x2, waiting for transfers between devices, within_member(): return lax.ppermute(array, 'dp', pairs)  3.17 us
  transfers between devices with their start and end apart: 19, of which 9 were waited for; matrix products, arithmetic and copies ran while one was open for 6% of the time, Pallas kernels for 24%

profile of v4, /device:TPU:0, one launch (start us, length us, event | category | flops | bytes accessed | tf_op | source)
XLA Modules:
  0.0 131.0 jit_solution(4726350571694376825)
XLA Ops:
  0.0 2.2 %dynamic-slice_bitcast_fusion = bf16[160,2560]{1,0:T(8,128)(2,1)} fusion(bf16[2560,320]{0,1:T(8,128)(2,1)} %param.15, s32[]{:T(128)S(6)} %select_n.63), kind=kLoop, calls=%fused_computation.2 | loop fusion | bytes 1638404 | tf_op jit(solution)/shard_map/dynamic_slice | solution.py:301
  2.2 3.0 %collective-permute-start = (bf16[160,2560]{1,0:T(8,128)(2,1)}, bf16[160,2560]{1,0:T(8,128)(2,1)S(1)}, u32[]{:S(2)}, u32[]{:S(2)}) collective-permute-start(bf16[160,2560]{1,0:T(8,128)(2,1)} %dynamic-slice_bitcast_fusion), channel_id=1, source_target_pairs={{0,4},{1,5},{2,6},{3,7},{4,8},{5,9},{6,10},{7,11},{8,12},{9,13},{1... | collective-permute-start | bytes 2457608 | tf_op jit(solution)/shard_map/ppermute | solution.py:264
  5.2 1.5 %collective-permute-start.1 = (bf16[160,2560]{1,0:T(8,128)(2,1)}, bf16[160,2560]{1,0:T(8,128)(2,1)}, u32[]{:S(2)}, u32[]{:S(2)}) collective-permute-start(bf16[160,2560]{1,0:T(8,128)(2,1)} %dynamic-slice_bitcast_fusion), channel_id=1, source_target_pairs={{0,2},{1,3},{2,0},{3,1},{4,6},{5,7},{6,4},{7,5},{8,10},{9,11},{10,... | collective-permute-start | bytes 2457608 | tf_op jit(solution)/shard_map/ppermute | solution.py:264
  8.0 2.9 %slice_bitcast_fusion = (bf16[1,1,128,2560]{3,2,1,0:T(8,128)(2,1)S(1)}, bf16[1,1,128,2560]{3,2,1,0:T(8,128)(2,1)}, bf16[1,1,128,2560]{3,2,1,0:T(8,128)(2,1)}, bf16[1,1,128,2560]{3,2,1,0:T(8,128)(2,1)S(1)}) fusion(bf16[3,128,2560]{2,1,0:T(8,128)(2,1)} %v_hbm.1, s32[]{:T(128)} %bitcast.1, bf16[3,128,2560]{2,1,0:T(8,128)(2,1)} %k_hbm.1), kind=kLoop, calls=%fused_computation.3 | loop fusion | bytes 5242884 | tf_op jit(solution)/shard_map/stack | solution.py:330
  12.3 1.2 pad_maximum_fusion.1
  14.1 1.2 pad_maximum_fusion
  15.2 10.5 %collective-permute-done.refs_1_ = bf16[160,2560]{1,0:T(8,128)(2,1)S(1)} collective-permute-done((bf16[160,2560]{1,0:T(8,128)(2,1)}, bf16[160,2560]{1,0:T(8,128)(2,1)S(1)}, u32[]{:S(2)}, u32[]{:S(2)}) %collective-permute-start) | collective-permute-done | bytes 819232 | tf_op jit(solution)/shard_map/ppermute | solution.py:264
  25.7 1.1 collective-permute-start.2
  26.8 1.5 %collective-permute-start.3 = (bf16[160,2560]{1,0:T(8,128)(2,1)S(1)}, bf16[160,2560]{1,0:T(8,128)(2,1)}, u32[]{:S(2)}, u32[]{:S(2)}) collective-permute-start(bf16[160,2560]{1,0:T(8,128)(2,1)S(1)} %collective-permute-done.refs_1_), channel_id=1, source_target_pairs={{0,2},{1,3},{2,0},{3,1},{4,6},{5,7},{6,4},{7,5},{8,10},{9,11},{10,... | collective-permute-start | bytes 2457608 | tf_op jit(solution)/shard_map/ppermute | solution.py:264
  28.3 1.5 %collective-permute-start.4 = (bf16[160,2560]{1,0:T(8,128)(2,1)S(1)}, bf16[160,2560]{1,0:T(8,128)(2,1)}, u32[]{:S(2)}, u32[]{:S(2)}) collective-permute-start(bf16[160,2560]{1,0:T(8,128)(2,1)S(1)} %collective-permute-done.refs_1_), channel_id=1, source_target_pairs={{0,16},{1,17},{2,18},{3,19},{4,20},{5,21},{6,22},{7,23},{8,24},{9,... | collective-permute-start | bytes 2457608 | tf_op jit(solution)/shard_map/ppermute | solution.py:264
  29.8 1.9 %collective-permute-start.8 = (bf16[2,1,128,2560]{3,2,1,0:T(8,128)(2,1)}, bf16[2,1,128,2560]{3,2,1,0:T(8,128)(2,1)}, u32[]{:S(2)}, u32[]{:S(2)}) collective-permute-start(bf16[2,1,128,2560]{3,2,1,0:T(8,128)(2,1)} %pad_maximum_fusion), channel_id=1, source_target_pairs={{0,1},{2,3},{3,4},{4,5},{6,7},{7,8},{8,9},{10,11},{11,12},{12,13},... | collective-permute-start | bytes 3932168 | tf_op jit(solution)/shard_map/ppermute | solution.py:272
  31.7 6.3 %collective-permute-start.9 = (bf16[2,1,128,2560]{3,2,1,0:T(8,128)(2,1)}, bf16[2,1,128,2560]{3,2,1,0:T(8,128)(2,1)}, u32[]{:S(2)}, u32[]{:S(2)}) collective-permute-start(bf16[2,1,128,2560]{3,2,1,0:T(8,128)(2,1)} %pad_maximum_fusion.1), channel_id=1, source_target_pairs={{0,15},{1,0},{3,2},{4,3},{5,4},{7,6},{8,7},{9,8},{11,10},{12,11},{... | collective-permute-start | bytes 3932168 | tf_op jit(solution)/shard_map/ppermute | solution.py:272
  38.1 1.0 constant_dynamic-slice_fusion
  39.1 8.1 %collective-permute-done.2.refs_3_ = bf16[160,2560]{1,0:T(8,128)(2,1)} collective-permute-done((bf16[160,2560]{1,0:T(8,128)(2,1)S(1)}, bf16[160,2560]{1,0:T(8,128)(2,1)}, u32[]{:S(2)}, u32[]{:S(2)}) %collective-permute-start.2) | collective-permute-done | bytes 819232 | tf_op jit(solution)/shard_map/ppermute | solution.py:264
  47.2 14.2 %collective-permute-start.5 = (bf16[160,2560]{1,0:T(8,128)(2,1)}, bf16[160,2560]{1,0:T(8,128)(2,1)}, u32[]{:S(2)}, u32[]{:S(2)}) collective-permute-start(bf16[160,2560]{1,0:T(8,128)(2,1)} %collective-permute-done.2.refs_3_), channel_id=1, source_target_pairs={{0,4},{1,5},{2,6},{3,7},{4,8},{5,9},{6,10},{7,11},{8,12},{9,13},{1... | collective-permute-start | bytes 2457608 | tf_op jit(solution)/shard_map/ppermute | solution.py:264
  61.4 1.5 %collective-permute-start.7 = (bf16[160,2560]{1,0:T(8,128)(2,1)}, bf16[160,2560]{1,0:T(8,128)(2,1)S(1)}, u32[]{:S(2)}, u32[]{:S(2)}) collective-permute-start(bf16[160,2560]{1,0:T(8,128)(2,1)} %collective-permute-done.3.refs_5_), channel_id=1, source_target_pairs={{0,16},{1,17},{2,18},{3,19},{4,20},{5,21},{6,22},{7,23},{8,24},{9,... | collective-permute-start | bytes 2457608 | tf_op jit(solution)/shard_map/ppermute | solution.py:264
  62.9 3.2 %collective-permute-done.9.after_hbm = bf16[2,1,128,2560]{3,2,1,0:T(8,128)(2,1)} collective-permute-done((bf16[2,1,128,2560]{3,2,1,0:T(8,128)(2,1)}, bf16[2,1,128,2560]{3,2,1,0:T(8,128)(2,1)}, u32[]{:S(2)}, u32[]{:S(2)}) %collective-permute-start.9) | collective-permute-done | bytes 1310752 | tf_op jit(solution)/shard_map/ppermute | solution.py:272
  66.1 12.6 %collective-permute-done.5.refs_9_ = bf16[160,2560]{1,0:T(8,128)(2,1)} collective-permute-done((bf16[160,2560]{1,0:T(8,128)(2,1)}, bf16[160,2560]{1,0:T(8,128)(2,1)}, u32[]{:S(2)}, u32[]{:S(2)}) %collective-permute-start.5) | collective-permute-done | bytes 819232 | tf_op jit(solution)/shard_map/ppermute | solution.py:264
  79.6 1.9 %collective-permute-start.11 = (bf16[160,2560]{1,0:T(8,128)(2,1)}, bf16[160,2560]{1,0:T(8,128)(2,1)}, u32[]{:S(2)}, u32[]{:S(2)}) collective-permute-start(bf16[160,2560]{1,0:T(8,128)(2,1)} %collective-permute-done.5.refs_9_), channel_id=1, source_target_pairs={{0,2},{1,3},{2,0},{3,1},{4,6},{5,7},{6,4},{7,5},{8,10},{9,11},{10,... | collective-permute-start | bytes 2457608 | tf_op jit(solution)/shard_map/ppermute | solution.py:264
  81.5 1.3 collective-permute-start.12
  82.8 12.7 %attention.1 = bf16[3,128,2560]{2,1,0:T(8,128)(2,1)} custom-call(s32[9]{0:T(128)} %reshape.14.index_ref, s32[1]{0:T(128)S(6)} %copy.9.count_ref, bf16[3,128,2560]{2,1,0:T(8,128)(2,1)} %q_hbm.1, bf16[3,128,2560]{2,1,0:T(8,128)(2,1)} %k_hbm.1, bf16[3,128,2560]{2,1,0:T(8,128)(2,1)} %v_hbm.1, bf16[2,1,128,2560]{3,2,1,0:T(8,128)(2,1)} %collective-permute-done.8.before_hbm, ...), custom_call_target="tpu_custom_call" | custom-call | flops 1509949440 | bytes 11796480 | tf_op jit(solution)/shard_map/attention/pallas_call | solution.py:95
  95.5 2.2 %collective-permute-done.10.refs_4_ = bf16[160,2560]{1,0:T(8,128)(2,1)} collective-permute-done((bf16[160,2560]{1,0:T(8,128)(2,1)}, bf16[160,2560]{1,0:T(8,128)(2,1)}, u32[]{:S(2)}, u32[]{:S(2)}) %collective-permute-start.10) | collective-permute-done | bytes 819232 | tf_op jit(solution)/shard_map/ppermute | solution.py:264
  98.5 1.0 collective-permute-start.13
  99.5 1.0 collective-permute-start.14
  100.5 2.0 %collective-permute-start.15 = (bf16[160,2560]{1,0:T(8,128)(2,1)}, bf16[160,2560]{1,0:T(8,128)(2,1)S(1)}, u32[]{:S(2)}, u32[]{:S(2)}) collective-permute-start(bf16[160,2560]{1,0:T(8,128)(2,1)} %collective-permute-done.11.refs_11_), channel_id=1, source_target_pairs={{0,16},{1,17},{2,18},{3,19},{4,20},{5,21},{6,22},{7,23},{8,24},{9,... | collective-permute-start | bytes 2457608 | tf_op jit(solution)/shard_map/ppermute | solution.py:264
  102.7 1.5 %copy-done.1 = bf16[3,128,2560]{2,1,0:T(8,128)(2,1)S(1)} copy-done((bf16[3,128,2560]{2,1,0:T(8,128)(2,1)S(1)}, bf16[3,128,2560]{2,1,0:T(8,128)(2,1)}, u32[]{:S(2)}) %copy-start.1) | copy-done | bytes 1966104
  104.3 1.1 copy-done.4
  105.4 14.1 %project.2 = (bf16[384,2176]{1,0:T(8,128)(2,1)S(1)}, bf16[384,2176]{1,0:T(8,128)(2,1)S(1)}) custom-call(s32[1]{0:T(128)} %bitcast.8.group_ref, bf16[384,2560]{1,0:T(8,128)(2,1)S(1)} %bitcast.29, bf16[384,2560]{1,0:T(8,128)(2,1)S(1)} %collective-permute-done.16.sibling_hbm, bf16[320,2560]{1,0:T(8,128)(2,1)S(1)} %bitcast.32, ...), custom_call_target="tpu_custom_call" | custom-call | flops 8178892800 | bytes 17776640 | tf_op jit(solution)/shard_map/project/pallas_call | solution.py:174
  119.6 1.6 %collective-permute-done.13.refs_0_ = bf16[160,2560]{1,0:T(8,128)(2,1)S(1)} collective-permute-done((bf16[160,2560]{1,0:T(8,128)(2,1)}, bf16[160,2560]{1,0:T(8,128)(2,1)S(1)}, u32[]{:S(2)}, u32[]{:S(2)}) %collective-permute-start.13) | collective-permute-done | bytes 819232 | tf_op jit(solution)/shard_map/ppermute | solution.py:264
  121.2 4.5 %project.3 = (bf16[384,512]{1,0:T(8,128)(2,1)S(1)}, bf16[384,512]{1,0:T(8,128)(2,1)S(1)}) custom-call(s32[1]{0:T(128)} %bitcast.8.group_ref, bf16[384,2560]{1,0:T(8,128)(2,1)S(1)} %bitcast.30, bf16[384,2560]{1,0:T(8,128)(2,1)S(1)} %collective-permute-done.16.sibling_hbm, bf16[160,2560]{1,0:T(8,128)(2,1)S(1)} %collective-permute-done.13.refs_0_, ...), custom_call_target="tpu_custom_call" | custom-call | flops 1887436800 | bytes 7127040 | tf_op jit(solution)/shard_map/project/pallas_call | solution.py:174
  126.3 1.3 %collective-permute-done.18.refs_3_ = bf16[384,512]{1,0:T(8,128)(2,1)S(1)} collective-permute-done((bf16[384,512]{1,0:T(8,128)(2,1)S(1)}, bf16[384,512]{1,0:T(8,128)(2,1)S(1)}, u32[]{:S(2)}, u32[]{:S(2)}) %collective-permute-start.18) | collective-permute-done | bytes 393248 | tf_op jit(solution)/shard_map/ppermute | solution.py:264
  127.7 3.2 %assemble.1 = bf16[384,5120]{1,0:T(8,128)(2,1)} custom-call(s32[10]{0:T(128)S(1)} %stack.67.scalars, bf16[384,2176]{1,0:T(8,128)(2,1)S(1)} %get-tuple-element.110.refs_0_, bf16[384,2176]{1,0:T(8,128)(2,1)S(1)} %collective-permute-done.17.refs_1_, bf16[384,512]{1,0:T(8,128)(2,1)S(1)} %get-tuple-element.117.refs_2_, ...), custom_call_target="tpu_custom_call" | custom-call | bytes 7864320 | tf_op jit(solution)/shard_map/assemble/pallas_call | solution.py:230
  (34 shorter events, 4.4 us)
Async XLA Ops:
  0.0 11.0 %copy-start = (f32[50,2560]{1,0:T(8,128)S(1)}, f32[50,2560]{1,0:T(8,128)}, u32[]{:S(2)}) copy-start(f32[50,2560]{1,0:T(8,128)} %param.13) | copy-start | bytes 1536004
  2.2 23.5 %collective-permute-start = (bf16[160,2560]{1,0:T(8,128)(2,1)}, bf16[160,2560]{1,0:T(8,128)(2,1)S(1)}, u32[]{:S(2)}, u32[]{:S(2)}) collective-permute-start(bf16[160,2560]{1,0:T(8,128)(2,1)} %dynamic-slice_bitcast_fusion), channel_id=1, source_target_pairs={{0,4},{1,5},{2,6},{3,7},{4,8},{5,9},{6,10},{7,11},{8,12},{9,13},{1... | collective-permute-start | bytes 2457608 | tf_op jit(solution)/shard_map/ppermute | solution.py:264
  5.2 20.5 %collective-permute-start.1 = (bf16[160,2560]{1,0:T(8,128)(2,1)}, bf16[160,2560]{1,0:T(8,128)(2,1)}, u32[]{:S(2)}, u32[]{:S(2)}) collective-permute-start(bf16[160,2560]{1,0:T(8,128)(2,1)} %dynamic-slice_bitcast_fusion), channel_id=1, source_target_pairs={{0,2},{1,3},{2,0},{3,1},{4,6},{5,7},{6,4},{7,5},{8,10},{9,11},{10,... | collective-permute-start | bytes 2457608 | tf_op jit(solution)/shard_map/ppermute | solution.py:264
  8.0 3.6 %copy-start.7 = (s32[3,3]{1,0:T(4,128)S(1)}, s32[3,3]{1,0:T(4,128)}, u32[]{:S(2)}) copy-start(s32[3,3]{1,0:T(4,128)} %param.12) | copy-start | bytes 112
  12.3 1.2 copy-start.5
  12.3 1.8 %copy-start.6 = (bf16[1,1,128,2560]{3,2,1,0:T(8,128)(2,1)S(1)}, bf16[1,1,128,2560]{3,2,1,0:T(8,128)(2,1)}, u32[]{:S(2)}) copy-start(bf16[1,1,128,2560]{3,2,1,0:T(8,128)(2,1)} %get-tuple-element.123) | copy-start | bytes 1966084
  13.5 24.6 %copy-start.2 = (bf16[2560,320]{0,1:T(8,128)(2,1)S(1)}, bf16[2560,320]{0,1:T(8,128)(2,1)}, u32[]{:S(2)}) copy-start(bf16[2560,320]{0,1:T(8,128)(2,1)} %param.15) | copy-start | bytes 4915204
  25.7 21.5 %collective-permute-start.2 = (bf16[160,2560]{1,0:T(8,128)(2,1)S(1)}, bf16[160,2560]{1,0:T(8,128)(2,1)}, u32[]{:S(2)}, u32[]{:S(2)}) collective-permute-start(bf16[160,2560]{1,0:T(8,128)(2,1)S(1)} %collective-permute-done.refs_1_), channel_id=1, source_target_pairs={{0,4},{1,5},{2,6},{3,7},{4,8},{5,9},{6,10},{7,11},{8,12},{9,13},{1... | collective-permute-start | bytes 2457608 | tf_op jit(solution)/shard_map/ppermute | solution.py:264
  26.8 20.4 %collective-permute-start.3 = (bf16[160,2560]{1,0:T(8,128)(2,1)S(1)}, bf16[160,2560]{1,0:T(8,128)(2,1)}, u32[]{:S(2)}, u32[]{:S(2)}) collective-permute-start(bf16[160,2560]{1,0:T(8,128)(2,1)S(1)} %collective-permute-done.refs_1_), channel_id=1, source_target_pairs={{0,2},{1,3},{2,0},{3,1},{4,6},{5,7},{6,4},{7,5},{8,10},{9,11},{10,... | collective-permute-start | bytes 2457608 | tf_op jit(solution)/shard_map/ppermute | solution.py:264
  28.3 18.9 %collective-permute-start.4 = (bf16[160,2560]{1,0:T(8,128)(2,1)S(1)}, bf16[160,2560]{1,0:T(8,128)(2,1)}, u32[]{:S(2)}, u32[]{:S(2)}) collective-permute-start(bf16[160,2560]{1,0:T(8,128)(2,1)S(1)} %collective-permute-done.refs_1_), channel_id=1, source_target_pairs={{0,16},{1,17},{2,18},{3,19},{4,20},{5,21},{6,22},{7,23},{8,24},{9,... | collective-permute-start | bytes 2457608 | tf_op jit(solution)/shard_map/ppermute | solution.py:264
  29.8 33.1 %collective-permute-start.8 = (bf16[2,1,128,2560]{3,2,1,0:T(8,128)(2,1)}, bf16[2,1,128,2560]{3,2,1,0:T(8,128)(2,1)}, u32[]{:S(2)}, u32[]{:S(2)}) collective-permute-start(bf16[2,1,128,2560]{3,2,1,0:T(8,128)(2,1)} %pad_maximum_fusion), channel_id=1, source_target_pairs={{0,1},{2,3},{3,4},{4,5},{6,7},{7,8},{8,9},{10,11},{11,12},{12,13},... | collective-permute-start | bytes 3932168 | tf_op jit(solution)/shard_map/ppermute | solution.py:272
  31.7 34.4 %collective-permute-start.9 = (bf16[2,1,128,2560]{3,2,1,0:T(8,128)(2,1)}, bf16[2,1,128,2560]{3,2,1,0:T(8,128)(2,1)}, u32[]{:S(2)}, u32[]{:S(2)}) collective-permute-start(bf16[2,1,128,2560]{3,2,1,0:T(8,128)(2,1)} %pad_maximum_fusion.1), channel_id=1, source_target_pairs={{0,15},{1,0},{3,2},{4,3},{5,4},{7,6},{8,7},{9,8},{11,10},{12,11},{... | collective-permute-start | bytes 3932168 | tf_op jit(solution)/shard_map/ppermute | solution.py:272
  47.2 31.5 %collective-permute-start.5 = (bf16[160,2560]{1,0:T(8,128)(2,1)}, bf16[160,2560]{1,0:T(8,128)(2,1)}, u32[]{:S(2)}, u32[]{:S(2)}) collective-permute-start(bf16[160,2560]{1,0:T(8,128)(2,1)} %collective-permute-done.2.refs_3_), channel_id=1, source_target_pairs={{0,4},{1,5},{2,6},{3,7},{4,8},{5,9},{6,10},{7,11},{8,12},{9,13},{1... | collective-permute-start | bytes 2457608 | tf_op jit(solution)/shard_map/ppermute | solution.py:264
  61.4 17.3 %collective-permute-start.6 = (bf16[160,2560]{1,0:T(8,128)(2,1)}, bf16[160,2560]{1,0:T(8,128)(2,1)}, u32[]{:S(2)}, u32[]{:S(2)}) collective-permute-start(bf16[160,2560]{1,0:T(8,128)(2,1)} %collective-permute-done.2.refs_3_), channel_id=1, source_target_pairs={{0,2},{1,3},{2,0},{3,1},{4,6},{5,7},{6,4},{7,5},{8,10},{9,11},{10,... | collective-permute-start | bytes 2457608 | tf_op jit(solution)/shard_map/ppermute | solution.py:264
  61.4 17.3 %collective-permute-start.7 = (bf16[160,2560]{1,0:T(8,128)(2,1)}, bf16[160,2560]{1,0:T(8,128)(2,1)S(1)}, u32[]{:S(2)}, u32[]{:S(2)}) collective-permute-start(bf16[160,2560]{1,0:T(8,128)(2,1)} %collective-permute-done.3.refs_5_), channel_id=1, source_target_pairs={{0,16},{1,17},{2,18},{3,19},{4,20},{5,21},{6,22},{7,23},{8,24},{9,... | collective-permute-start | bytes 2457608 | tf_op jit(solution)/shard_map/ppermute | solution.py:264
  78.7 0.9 copy-start.3
  79.6 18.1 %collective-permute-start.10 = (bf16[160,2560]{1,0:T(8,128)(2,1)}, bf16[160,2560]{1,0:T(8,128)(2,1)}, u32[]{:S(2)}, u32[]{:S(2)}) collective-permute-start(bf16[160,2560]{1,0:T(8,128)(2,1)} %collective-permute-done.4.refs_2_), channel_id=1, source_target_pairs={{0,4},{1,5},{2,6},{3,7},{4,8},{5,9},{6,10},{7,11},{8,12},{9,13},{1... | collective-permute-start | bytes 2457608 | tf_op jit(solution)/shard_map/ppermute | solution.py:264
  79.6 18.1 %collective-permute-start.11 = (bf16[160,2560]{1,0:T(8,128)(2,1)}, bf16[160,2560]{1,0:T(8,128)(2,1)}, u32[]{:S(2)}, u32[]{:S(2)}) collective-permute-start(bf16[160,2560]{1,0:T(8,128)(2,1)} %collective-permute-done.5.refs_9_), channel_id=1, source_target_pairs={{0,2},{1,3},{2,0},{3,1},{4,6},{5,7},{6,4},{7,5},{8,10},{9,11},{10,... | collective-permute-start | bytes 2457608 | tf_op jit(solution)/shard_map/ppermute | solution.py:264
  81.5 17.0 %collective-permute-start.12 = (bf16[160,2560]{1,0:T(8,128)(2,1)}, bf16[160,2560]{1,0:T(8,128)(2,1)}, u32[]{:S(2)}, u32[]{:S(2)}) collective-permute-start(bf16[160,2560]{1,0:T(8,128)(2,1)} %collective-permute-done.6.refs_7_), channel_id=1, source_target_pairs={{0,16},{1,17},{2,18},{3,19},{4,20},{5,21},{6,22},{7,23},{8,24},{9,... | collective-permute-start | bytes 2457608 | tf_op jit(solution)/shard_map/ppermute | solution.py:264
  98.5 4.2 %collective-permute-start.16 = (bf16[384,2560]{1,0:T(8,128)(2,1)}, bf16[384,2560]{1,0:T(8,128)(2,1)S(1)}, u32[]{:S(2)}, u32[]{:S(2)}) collective-permute-start(bf16[384,2560]{1,0:T(8,128)(2,1)} %bitcast.28), channel_id=1, source_target_pairs={{0,1},{1,0},{2,3},{3,2},{4,5},{5,4},{6,7},{7,6},{8,9},{9,8},{10,11... | collective-permute-start | bytes 5898248 | tf_op jit(solution)/shard_map/ppermute | solution.py:264
  98.5 22.7 %collective-permute-start.13 = (bf16[160,2560]{1,0:T(8,128)(2,1)}, bf16[160,2560]{1,0:T(8,128)(2,1)S(1)}, u32[]{:S(2)}, u32[]{:S(2)}) collective-permute-start(bf16[160,2560]{1,0:T(8,128)(2,1)} %collective-permute-done.10.refs_4_), channel_id=1, source_target_pairs={{0,4},{1,5},{2,6},{3,7},{4,8},{5,9},{6,10},{7,11},{8,12},{9,13},{1... | collective-permute-start | bytes 2457608 | tf_op jit(solution)/shard_map/ppermute | solution.py:264
  99.5 21.7 %collective-permute-start.14 = (bf16[160,2560]{1,0:T(8,128)(2,1)}, bf16[160,2560]{1,0:T(8,128)(2,1)S(1)}, u32[]{:S(2)}, u32[]{:S(2)}) collective-permute-start(bf16[160,2560]{1,0:T(8,128)(2,1)} %constant_dynamic-slice_fusion), channel_id=1, source_target_pairs={{0,2},{1,3},{2,0},{3,1},{4,6},{5,7},{6,4},{7,5},{8,10},{9,11},{10,... | collective-permute-start | bytes 2457608 | tf_op jit(solution)/shard_map/ppermute | solution.py:264
  100.5 20.7 %collective-permute-start.15 = (bf16[160,2560]{1,0:T(8,128)(2,1)}, bf16[160,2560]{1,0:T(8,128)(2,1)S(1)}, u32[]{:S(2)}, u32[]{:S(2)}) collective-permute-start(bf16[160,2560]{1,0:T(8,128)(2,1)} %collective-permute-done.11.refs_11_), channel_id=1, source_target_pairs={{0,16},{1,17},{2,18},{3,19},{4,20},{5,21},{6,22},{7,23},{8,24},{9,... | collective-permute-start | bytes 2457608 | tf_op jit(solution)/shard_map/ppermute | solution.py:264
  102.7 1.5 %copy-start.1 = (bf16[3,128,2560]{2,1,0:T(8,128)(2,1)S(1)}, bf16[3,128,2560]{2,1,0:T(8,128)(2,1)}, u32[]{:S(2)}) copy-start(bf16[3,128,2560]{2,1,0:T(8,128)(2,1)} %attention.1) | copy-start | bytes 5898244
  104.3 1.1 copy-start.4
  121.2 6.5 %collective-permute-start.17 = (bf16[384,2176]{1,0:T(8,128)(2,1)S(1)}, bf16[384,2176]{1,0:T(8,128)(2,1)S(1)}, u32[]{:S(2)}, u32[]{:S(2)}) collective-permute-start(bf16[384,2176]{1,0:T(8,128)(2,1)S(1)} %get-tuple-element.111), channel_id=1, source_target_pairs={{0,1},{1,0},{2,3},{3,2},{4,5},{5,4},{6,7},{7,6},{8,9},{9,8},{10,11... | collective-permute-start | bytes 5013512 | tf_op jit(solution)/shard_map/ppermute | solution.py:264
  125.8 1.9 %collective-permute-start.18 = (bf16[384,512]{1,0:T(8,128)(2,1)S(1)}, bf16[384,512]{1,0:T(8,128)(2,1)S(1)}, u32[]{:S(2)}, u32[]{:S(2)}) collective-permute-start(bf16[384,512]{1,0:T(8,128)(2,1)S(1)} %get-tuple-element.118), channel_id=1, source_target_pairs={{0,1},{1,0},{2,3},{3,2},{4,5},{5,4},{6,7},{7,6},{8,9},{9,8},{10,11... | collective-permute-start | bytes 1179656 | tf_op jit(solution)/shard_map/ppermute | solution.py:264
